TPU v7x, 32 devices: a whole 2x2x4 slice. The times are simulated.
32 devices in a mesh: frow: 2 (over x), fcol: 2 (over core), chan: 8 (over z, y).
Axes of the slice: x: 2, y: 2, z: 4, core: 2. Of those that a mesh axis runs over, the one named last changes fastest.
Arguments:
- dirty_image: float32 [32, 64, 512], P('chan', 'frow', 'fcol'), may hold values from -12 to 12
- density: float32 [32, 64, 512], P('chan', 'frow', 'fcol'), may hold values from 0.25 to 4
Outputs:
- image_estimate: float32 [32, 64, 512], P('chan', 'frow', 'fcol')
All inputs are finite; a program needn't handle non-finite values.
Results may differ from a plain program's by a relative error of at most 0.0003.
Values sent between devices are 32-bit elements; how exact they have to be, the bound alone decides.
No kernel may reach another device: no remote copies, remote signals or barrier semaphores. Data moves between devices by JAX's collectives and lax.ppermute only.
A program may use at most 64 MiB of HBM per device.

v0:
```python
import math

import jax
import jax.numpy as jnp
import numpy as np
from jax import lax
from jax.sharding import PartitionSpec as P

NDB = 4
LEVELS = 1


DAUBECHIES = (
    (0.7071067811865476, 0.7071067811865476),
    (0.48296291314469025, 0.836516303737469, 0.22414386804185735, -0.12940952255092145),
    (
        0.3326705529509569,
        0.8068915093133388,
        0.4598775021193313,
        -0.13501102001039084,
        -0.08544127388224149,
        0.035226291882100656,
    ),
    (
        0.23037781330885523,
        0.7148465705525415,
        0.6308807679295904,
        -0.02798376941698385,
        -0.18703481171888114,
        0.030841381835986965,
        0.032883011666982945,
        -0.010597401784997278,
    ),
)
rim_analysis = 3
rim_synthesis = 2
jacobi_sweeps = 6
STEP_PRIMAL = 0.2
STEP_NUCLEAR = 1.0
STEP_SPARSE = 0.5
NUCLEAR_SCALE = 1.0
SPARSE_SCALE = 0.5
BEST_ACCURACY = lax.Precision.HIGHEST


def extended_2(cells, sides, width):
    for axis, dim in sides:
        count = lax.axis_size(axis)
        ends = count - 1
        head = lax.slice_in_dim(cells, 0, width, axis=dim)
        tail = lax.slice_in_dim(cells, cells.shape[dim] - width, cells.shape[dim], axis=dim)
        cells = jnp.concatenate(
            [
                lax.ppermute(tail, axis, [(i, (i + 1) % count) for i in range(ends)]),
                cells,
                lax.ppermute(head, axis, [((i + 1) % count, i) for i in range(ends)]),
            ],
            axis=dim,
        )
    return cells


def analyse_axis(extended, filter_taps, axis_index, margin, out_total):
    tap_count = len(filter_taps)
    offset = tap_count // 2 - 1
    half_total = out_total // 2
    low_band = None
    high_band = None
    for tap_index in range(tap_count):
        start_at = margin + tap_index - offset
        sliced = lax.slice_in_dim(extended, start_at, start_at + 2 * half_total - 1, 2, axis_index)
        low_part = filter_taps[tap_index] * sliced
        high_part = (-1.0) ** tap_index * filter_taps[tap_count - 1 - tap_index] * sliced
        if low_band is None:
            low_band, high_band = (low_part, high_part)
        else:
            low_band, high_band = (low_band + low_part, high_band + high_part)
    return (low_band, high_band)


def decompose_across_width(extended, filter_taps, margin, col_count):
    return jnp.stack(analyse_axis(extended, filter_taps, extended.ndim - 1, margin, col_count), 0)


def analyse_rows(halves, filter_taps, margin, row_count):
    band_ll, band_lh = analyse_axis(halves[0], filter_taps, halves.ndim - 3, margin, row_count)
    band_hl, band_hh = analyse_axis(halves[1], filter_taps, halves.ndim - 3, margin, row_count)
    return jnp.stack([band_ll, band_lh, band_hl, band_hh], 0)


def upsample(values, axis_index):
    spaced = jnp.stack([values, jnp.zeros_like(values)], axis_index + 1)
    new_shape = list(values.shape)
    new_shape[axis_index] = 2 * new_shape[axis_index]
    return spaced.reshape(new_shape)


def synthesise_axis(low_band, high_band, filter_taps, axis_index, margin, out_total):
    tap_count = len(filter_taps)
    offset = tap_count // 2 - 1
    low_up = upsample(low_band, axis_index)
    high_up = upsample(high_band, axis_index)
    result = None
    for tap_index in range(tap_count):
        start_at = offset - tap_index + 2 * margin
        low_slice = lax.slice_in_dim(low_up, start_at, start_at + 2 * out_total, 1, axis_index)
        high_slice = lax.slice_in_dim(high_up, start_at, start_at + 2 * out_total, 1, axis_index)
        contribution = (
            filter_taps[tap_index] * low_slice
            + (-1.0) ** tap_index * filter_taps[tap_count - 1 - tap_index] * high_slice
        )
        result = contribution if result is None else result + contribution
    return result


def synthesise_plane(band_stack, filter_taps, margin, row_count, col_count):
    col_low = synthesise_axis(
        band_stack[0], band_stack[1], filter_taps, band_stack.ndim - 3, margin, row_count
    )
    col_high = synthesise_axis(
        band_stack[2], band_stack[3], filter_taps, band_stack.ndim - 3, margin, row_count
    )
    return synthesise_axis(col_low, col_high, filter_taps, band_stack.ndim - 2, margin, col_count)


def pairing_rounds(matrix_order):
    players = list(range(matrix_order))
    rounds_list = []
    for round_index in range(matrix_order - 1):
        left_side = []
        right_side = []
        for slot_index in range(matrix_order // 2):
            first_id = players[slot_index]
            second_id = players[matrix_order - 1 - slot_index]
            left_side.append(min(first_id, second_id))
            right_side.append(max(first_id, second_id))
        order = np.concatenate([np.array(left_side), np.array(right_side)])
        rounds_list.append((np.array(left_side), np.array(right_side), np.argsort(order)))
        players = [players[0]] + [players[-1]] + players[1:-1]
    return rounds_list


def jacobi_mix(gram_matrix, threshold):
    matrix_order = gram_matrix.shape[-1]
    plan = pairing_rounds(matrix_order)
    identity = jnp.broadcast_to(jnp.eye(matrix_order, dtype=gram_matrix.dtype), gram_matrix.shape)

    def rotate_cols(values, upper_ids, lower_ids, restore, rotation_cosine, sine_part):
        cos_row = rotation_cosine[..., None, :]
        sin_row = sine_part[..., None, :]
        upper_cols = values[..., :, upper_ids]
        beneath_vertical_lines = values[..., :, lower_ids]
        joined = jnp.concatenate(
            [
                upper_cols * cos_row - beneath_vertical_lines * sin_row,
                upper_cols * sin_row + beneath_vertical_lines * cos_row,
            ],
            -1,
        )
        return joined[..., :, restore]

    def jacobi_sweep(step_index, state_pair):
        tableau_array, vectors = state_pair
        for upper_ids, lower_ids, restore in plan:
            diag_upper = tableau_array[..., upper_ids, upper_ids]
            diag_lower = tableau_array[..., lower_ids, lower_ids]
            coupling = tableau_array[..., upper_ids, lower_ids]
            spread = diag_lower - diag_upper
            denominator = jnp.abs(spread) + jnp.sqrt(spread * spread + 4.0 * coupling * coupling)
            positive = denominator > 0
            tangent = jnp.where(
                positive,
                jnp.where(spread >= 0, 2.0, -2.0)
                * coupling
                / jnp.where(positive, denominator, 1.0),
                0.0,
            )
            rotation_cosine = 1.0 / jnp.sqrt(1.0 + tangent * tangent)
            sine_part = tangent * rotation_cosine
            cos_col = rotation_cosine[..., :, None]
            sine_column = sine_part[..., :, None]
            upper_rows = tableau_array[..., upper_ids, :]
            lower_rows = tableau_array[..., lower_ids, :]
            tableau_array = jnp.concatenate(
                [
                    cos_col * upper_rows - sine_column * lower_rows,
                    sine_column * upper_rows + cos_col * lower_rows,
                ],
                -2,
            )[..., restore, :]
            tableau_array = rotate_cols(
                tableau_array, upper_ids, lower_ids, restore, rotation_cosine, sine_part
            )
            vectors = rotate_cols(
                vectors, upper_ids, lower_ids, restore, rotation_cosine, sine_part
            )
        return (tableau_array, vectors)

    tableau_array, vectors = lax.fori_loop(0, jacobi_sweeps, jacobi_sweep, (gram_matrix, identity))
    values = jnp.diagonal(tableau_array, axis1=-2, axis2=-1)
    magnitude = jnp.sqrt(jnp.maximum(values, 0.0))
    weights = threshold / jnp.maximum(magnitude, threshold)
    return jnp.matmul(
        vectors * weights[..., None, :], jnp.swapaxes(vectors, -1, -2), precision=BEST_ACCURACY
    )


def analyse_level(stacked, row_count, col_count):
    families = []
    extended = extended_2(stacked, (("frow", 2), ("fcol", 3)), rim_analysis)
    for family in range(NDB):
        source = extended[0]
        halves = decompose_across_width(source, DAUBECHIES[family], rim_analysis, col_count)
        families.append(analyse_rows(halves, DAUBECHIES[family], rim_analysis, row_count))
    return jnp.stack(families, 0)


def analyse_local(image):
    current = image[None]
    row_count = image.shape[1] // 2**0
    col_count = image.shape[2] // 2**0
    stacked = analyse_level(current, row_count, col_count)
    details = [stacked[:, 1:]]
    current = stacked[:, 0]
    return (details, current)


def synthesise_local(details, approx):
    recon = approx
    for level_index in reversed(range(LEVELS)):
        band_stack = jnp.concatenate([recon[:, None], details[level_index]], 1)
        family_count, band_count, chan_here, row_count, col_count = band_stack.shape
        merged = band_stack.reshape(family_count, band_count * chan_here, row_count, col_count)
        extended = extended_2(merged, (("frow", 2), ("fcol", 3)), rim_synthesis)
        extended = extended.reshape(
            family_count,
            band_count,
            chan_here,
            row_count + 2 * rim_synthesis,
            col_count + 2 * rim_synthesis,
        )
        families = []
        for family in range(NDB):
            families.append(
                synthesise_plane(
                    extended[family], DAUBECHIES[family], rim_synthesis, row_count, col_count
                )
            )
        recon = jnp.stack(families, 0)
    return jnp.sum(recon, 0)


def split_like(flat_values, templates):
    pieces = []
    start_at = 0
    for template in templates:
        pieces.append(flat_values[start_at : start_at + template.size].reshape(template.shape))
        start_at = start_at + template.size
    return pieces


def on_device(dirty_image, density):
    chan_here, row_count, col_count = dirty_image.shape
    total_channels = chan_here * lax.axis_size("chan")
    group_count = total_channels // (2 * chan_here)
    nuclear_limit = NUCLEAR_SCALE * math.sqrt(row_count * col_count)
    sparse_limit = SPARSE_SCALE * math.sqrt(total_channels)
    estimate = jnp.maximum(dirty_image, 0.0)
    dual_details = None
    dual_approx = None
    coeff_details, coeff_approx = analyse_local(estimate)
    upd_dirac = STEP_SPARSE * estimate
    upd_details = [STEP_SPARSE * coeff_details[0]]
    upd_approx = STEP_SPARSE * coeff_approx
    local_norms = [jnp.sum(upd_dirac * upd_dirac, 0), jnp.sum(upd_approx * upd_approx, 1)] + [
        jnp.sum(item * item, 2) for item in upd_details
    ]
    norm_terms = jnp.concatenate([item.reshape(-1) for item in local_norms], 0)
    shifted = (STEP_NUCLEAR * estimate).reshape(chan_here, row_count * col_count)
    by_pixel = lax.all_to_all(shifted, "chan", split_axis=1, concat_axis=0, tiled=True)
    bundled_vertical_lines = by_pixel.reshape(group_count, 2 * chan_here, by_pixel.shape[1])
    partial_gram_blocks = jnp.einsum(
        "cko,cqo->ckq", bundled_vertical_lines, bundled_vertical_lines, precision=BEST_ACCURACY
    )
    norm_totals, gram_totals = lax.psum((norm_terms, partial_gram_blocks), "chan")
    rotation_matrix = jacobi_mix(gram_totals, nuclear_limit)
    rotated_matrix = jnp.einsum(
        "oae,oer->oar", rotation_matrix, bundled_vertical_lines, precision=BEST_ACCURACY
    ).reshape(total_channels, by_pixel.shape[1])
    nuclear_flat = lax.all_to_all(rotated_matrix, "chan", split_axis=0, concat_axis=1, tiled=True)
    nuclear_dual = nuclear_flat.reshape(chan_here, row_count, col_count)
    global_norms = split_like(norm_totals, local_norms)
    dual_dirac = (
        upd_dirac * (sparse_limit / jnp.maximum(jnp.sqrt(global_norms[0]), sparse_limit))[None]
    )
    dual_approx = (
        upd_approx * (sparse_limit / jnp.maximum(jnp.sqrt(global_norms[1]), sparse_limit))[:, None]
    )
    dual_details = [
        upd_details[0]
        * (sparse_limit / jnp.maximum(jnp.sqrt(global_norms[2]), sparse_limit))[:, :, None]
    ]
    synthesis = dual_dirac + synthesise_local(dual_details, dual_approx)
    renewed = jnp.maximum(
        estimate - STEP_PRIMAL * (density * estimate - dirty_image + nuclear_dual + synthesis), 0.0
    )
    return renewed


def solution(mesh):
    return jax.shard_map(
        on_device,
        mesh=mesh,
        in_specs=(P("chan", "frow", "fcol"), P("chan", "frow", "fcol")),
        out_specs=P("chan", "frow", "fcol"),
        check_vma=False,
    )
```

profile of v0, /device:TPU:0, one launch (start us, length us, event | category | flops | bytes accessed | tf_op | source)
XLA Modules:
  0.0 623.8 jit_solution(13662604305937762628)
XLA Ops:
  7.5 4.8 collective-permute-start
  13.8 4.2 collective-permute-done.1
  21.5 5.8 all-to-all-start
  27.6 2.6 slice.694
  30.2 2.6 slice.693
  32.8 2.6 slice.680
  35.5 2.6 slice.679
  38.1 3.1 slice.670
  41.2 2.6 slice.669
  43.8 2.6 slice.664
  46.5 2.6 slice.663
  51.2 70.3 %all-reduce.26.cloned.1.call-done = f32[40960]{0:T(1024)} async-done(((f32[40960]{0:T(1024)}), f32[40960]{0:T(1024)}) %all-reduce.26.cloned.1.call-update) | async-done | bytes 163856 | tf_op jit(solution)/shard_map/psum | solution.py:285
  123.9 2.9 copy.1018
  128.2 4.5 collective-permute-start.4
  133.1 36.1 %psum.14 = f32[4,8,8]{2,1,0:T(8,128)S(1)} all-reduce(f32[4,8,8]{2,1,0:T(8,128)S(1)} %fusion.191), channel_id=1, replica_groups=mesh['frow'=2,'fcol'=2,'chan'=8] {'chan'}, use_global_device_ids=true, to_apply=%region_0.0 | all-reduce | flops 256 | bytes 2048 | tf_op jit(solution)/shard_map/psum | solution.py:285
  169.8 332.2 %while.15 = (s32[]{:T(128)}, f32[4,8,8]{1,0,2:T(4,128)S(1)}, f32[4,8,8]{1,0,2:T(4,128)S(1)}, s32[]{:T(128)}, s32[4]{0:T(128)S(1)}, /*index=5*/s32[4]{0:T(128)S(1...) while((s32[]{:T(128)}, f32[4,8,8]{1,0,2:T(4,128)S(1)}, ...), condition=%wide.region_2.0_spmd.clone.clone.clone, body=%wide.region_1.0_spmd.sunk.clone.clone.clone.sunk | while | flops 45262 | bytes 316501 | solution.py:199
  503.0 3.0 copy.1017
  506.0 3.0 copy.1019
  509.0 6.9 %pad_maximum_fusion.21 = f32[4,16,20,128]{2,1,3,0:T(8,128)S(1)} fusion(f32[4,16,2,128]{2,1,3,0:T(8,128)} %copy.1019, f32[4,16,16,128]{2,1,3,0:T(8,128)} %copy.1018, f32[4,16,2,128]{2,1,3,0:T(8,128)} %copy.1017), kind=kLoop, calls=%fused_computation.325 | loop fusion | flops 327680 | bytes 1310720 | tf_op jit(solution)/shard_map/concatenate | solution.py:52
  521.5 4.0 all-to-all-start.1
  525.5 3.5 copy.1021
  547.8 2.3 fusion.181
  575.6 2.1 copy.1107
  612.9 3.6 fusion.164
  (1598 shorter events, 426.6 us)
Async XLA Ops:
  7.5 6.3 %collective-permute-start = (f32[1,4,3,256]{3,2,1,0:T(4,128)S(1)}, f32[1,4,3,256]{3,2,1,0:T(4,128)S(1)}, u32[]{:S(2)}, u32[]{:S(2)}) collective-permute-start(f32[1,4,3,256]{3,2,1,0:T(4,128)S(1)} %get-tuple-element.1170), channel_id=1, source_target_pairs={{0,16},{1,17},{2,18},{3,19},{4,20},{5,21},{6,22},{7,23},{8,24},{9,... | collective-permute-start | bytes 36872 | tf_op jit(solution)/shard_map/ppermute | solution.py:54
  12.3 5.6 collective-permute-start.1
  18.1 9.3 %collective-permute-start.2 = (f32[1,4,38,3]{3,2,1,0:T(8,128)S(1)}, f32[1,4,38,3]{3,2,1,0:T(8,128)S(1)}, u32[]{:S(2)}, u32[]{:S(2)}) collective-permute-start(f32[1,4,38,3]{3,2,1,0:T(8,128)S(1)} %get-tuple-element.1161), channel_id=1, source_target_pairs={{0,8},{1,9},{2,10},{3,11},{4,12},{5,13},{6,14},{7,15},{16,24},{17,... | collective-permute-start | bytes 5480 | tf_op jit(solution)/shard_map/ppermute | solution.py:54
  19.4 8.0 %collective-permute-start.3 = (f32[1,4,38,3]{3,2,1,0:T(8,128)S(1)}, f32[1,4,38,3]{3,2,1,0:T(8,128)S(1)}, u32[]{:S(2)}, u32[]{:S(2)}) collective-permute-start(f32[1,4,38,3]{3,2,1,0:T(8,128)S(1)} %get-tuple-element.1162), channel_id=1, source_target_pairs={{8,0},{9,1},{10,2},{11,3},{12,4},{13,5},{14,6},{15,7},{24,16},{25,... | collective-permute-start | bytes 5480 | tf_op jit(solution)/shard_map/ppermute | solution.py:56
  21.5 111.3 %all-to-all-start = ((f32[4,8,1024]{2,0,1:T(4,128)}), f32[4,8,1024]{2,0,1:T(4,128)S(1)}, u32[]{:S(2)}, u32[]{:S(2)}) async-start(f32[4,8,1024]{2,0,1:T(4,128)} %copy.1009), calls=%async_computation | async-start | bytes 262144 | tf_op jit(solution)/shard_map/all_to_all | solution.py:280
  27.3 94.2 %all-reduce.26.cloned.1.call-start = ((), (), s32[]{:S(2)}) async-start(), calls=%async_computation.2 | async-start | bytes 327680 | tf_op jit(solution)/shard_map/psum | solution.py:285
  122.4 47.0 %copy-start.5 = (s32[4]{0:T(128)S(1)}, s32[4]{0:T(128)}, u32[]{:S(2)}) copy-start(s32[4]{0:T(128)} %constant.1842) | copy-start | bytes 52
  122.4 46.9 %copy-start.6 = (s32[4]{0:T(128)S(1)}, s32[4]{0:T(128)}, u32[]{:S(2)}) copy-start(s32[4]{0:T(128)} %constant.1841) | copy-start | bytes 52
  122.4 46.9 %copy-start.7 = (s32[4]{0:T(128)S(1)}, s32[4]{0:T(128)}, u32[]{:S(2)}) copy-start(s32[4]{0:T(128)} %constant.1840) | copy-start | bytes 52
  122.5 46.9 %copy-start.8 = (s32[4]{0:T(128)S(1)}, s32[4]{0:T(128)}, u32[]{:S(2)}) copy-start(s32[4]{0:T(128)} %constant.1836) | copy-start | bytes 52
  122.5 46.9 %copy-start.9 = (s32[4]{0:T(128)S(1)}, s32[4]{0:T(128)}, u32[]{:S(2)}) copy-start(s32[4]{0:T(128)} %constant.1835) | copy-start | bytes 52
  122.5 46.9 %copy-start.10 = (s32[4]{0:T(128)S(1)}, s32[4]{0:T(128)}, u32[]{:S(2)}) copy-start(s32[4]{0:T(128)} %constant.1834) | copy-start | bytes 52
  122.5 46.9 %copy-start.11 = (s32[4]{0:T(128)S(1)}, s32[4]{0:T(128)}, u32[]{:S(2)}) copy-start(s32[4]{0:T(128)} %constant.1830) | copy-start | bytes 52
  122.5 46.9 %copy-start.12 = (s32[4]{0:T(128)S(1)}, s32[4]{0:T(128)}, u32[]{:S(2)}) copy-start(s32[4]{0:T(128)} %constant.1829) | copy-start | bytes 52
  122.5 46.9 %copy-start.13 = (s32[4]{0:T(128)S(1)}, s32[4]{0:T(128)}, u32[]{:S(2)}) copy-start(s32[4]{0:T(128)} %constant.1828) | copy-start | bytes 52
  122.5 46.9 %copy-start.14 = (s32[4]{0:T(128)S(1)}, s32[4]{0:T(128)}, u32[]{:S(2)}) copy-start(s32[4]{0:T(128)} %constant.1824) | copy-start | bytes 52
  122.5 46.9 %copy-start.15 = (s32[4]{0:T(128)S(1)}, s32[4]{0:T(128)}, u32[]{:S(2)}) copy-start(s32[4]{0:T(128)} %constant.1823) | copy-start | bytes 52
  122.6 46.9 %copy-start.16 = (s32[4]{0:T(128)S(1)}, s32[4]{0:T(128)}, u32[]{:S(2)}) copy-start(s32[4]{0:T(128)} %constant.1822) | copy-start | bytes 52
  122.6 46.9 %copy-start.17 = (s32[4]{0:T(128)S(1)}, s32[4]{0:T(128)}, u32[]{:S(2)}) copy-start(s32[4]{0:T(128)} %constant.1818) | copy-start | bytes 52
  126.9 379.1 %collective-permute-start.5 = (f32[4,16,2,128]{3,1,2,0:T(8,128)S(1)}, f32[4,16,2,128]{3,1,2,0:T(8,128)S(1)}, u32[]{:S(2)}, u32[]{:S(2)}) collective-permute-start(f32[4,16,2,128]{3,1,2,0:T(8,128)S(1)} %copy.1088), channel_id=1, source_target_pairs={{16,0},{17,1},{18,2},{19,3},{20,4},{21,5},{22,6},{23,7},{24,8},{25... | collective-permute-start | bytes 196616 | tf_op jit(solution)/shard_map/ppermute | solution.py:56
  128.2 374.8 %collective-permute-start.4 = (f32[4,16,2,128]{3,1,2,0:T(8,128)S(1)}, f32[4,16,2,128]{3,1,2,0:T(8,128)S(1)}, u32[]{:S(2)}, u32[]{:S(2)}) collective-permute-start(f32[4,16,2,128]{3,1,2,0:T(8,128)S(1)} %copy.1087), channel_id=1, source_target_pairs={{0,16},{1,17},{2,18},{3,19},{4,20},{5,21},{6,22},{7,23},{8,24},{9,... | collective-permute-start | bytes 196616 | tf_op jit(solution)/shard_map/ppermute | solution.py:54
  517.9 11.6 %collective-permute-start.6 = (f32[4,16,20,2]{2,1,3,0:T(8,128)S(1)}, f32[4,16,20,2]{2,1,3,0:T(8,128)S(1)}, u32[]{:S(2)}, u32[]{:S(2)}) collective-permute-start(f32[4,16,20,2]{2,1,3,0:T(8,128)S(1)} %get-tuple-element.1083), channel_id=1, source_target_pairs={{0,8},{1,9},{2,10},{3,11},{4,12},{5,13},{6,14},{7,15},{16,24},{17,... | collective-permute-start | bytes 30728 | tf_op jit(solution)/shard_map/ppermute | solution.py:54
  519.2 9.8 %collective-permute-start.7 = (f32[4,16,20,2]{2,1,3,0:T(8,128)S(1)}, f32[4,16,20,2]{2,1,3,0:T(8,128)S(1)}, u32[]{:S(2)}, u32[]{:S(2)}) collective-permute-start(f32[4,16,20,2]{2,1,3,0:T(8,128)S(1)} %get-tuple-element.1084), channel_id=1, source_target_pairs={{8,0},{9,1},{10,2},{11,3},{12,4},{13,5},{14,6},{15,7},{24,16},{25,... | collective-permute-start | bytes 30728 | tf_op jit(solution)/shard_map/ppermute | solution.py:56
  521.5 90.3 %all-to-all-start.1 = ((f32[8,4,1024]{2,1,0:T(4,128)}), f32[8,4,1024]{2,1,0:T(4,128)}, u32[]{:S(2)}, u32[]{:S(2)}) async-start(f32[8,4,1024]{2,1,0:T(4,128)} %all_to_all.27), calls=%async_computation.1 | async-start | bytes 262144 | tf_op jit(solution)/shard_map/all_to_all | solution.py:290
  (32 other events, 1300.9 us)
Sparse Core Ops, SparseCore 0:
  51.3 70.1 all-reduce.25
where the time goes:
time: 635 us; the launch traced here: 624 us
  local copies, waits for them, and re-layouts  440 us (69%)
  waiting for transfers between devices  74.6 us (12%)
  blocking collectives  36.1 us (6%)
  starting transfers between devices  27 us (4%)
  other arithmetic  26.9 us (4%)
  between operations  15.6 us (2%)
    psum x1, waiting for transfers between devices, on_device(): lax.psum((norm_terms, partial_gram_blocks), 'chan')  70.3 us
    unnamed x158, local copies, waits for them, and re-layouts  62.6 us
    gather x156, local copies, waits for them, and re-layouts, rotate_cols(): return joined[..., :, restore]  56 us
    gather x84, local copies, waits for them, and re-layouts, rotate_cols(): upper_cols = values[..., :, upper_ids]  48 us
    gather x84, local copies, waits for them, and re-layouts, rotate_cols(): beneath_vertical_lines = values[..., :, lower_ids]  47.9 us
    psum x1, blocking collectives, on_device(): lax.psum((norm_terms, partial_gram_blocks), 'chan')  36.1 us
    gather x84, local copies, waits for them, and re-layouts, jacobi_sweep(): jnp.concatenate([cos_col * upper_rows - sine_column * lower_rows, sine_co...  27.7 us
    gather x84, local copies, waits for them, and re-layouts, jacobi_sweep(): coupling = tableau_array[..., upper_ids, lower_ids]  27.7 us
  transfers between devices with their start and end apart: 11, of which 3 were waited for; matrix products, arithmetic and copies ran while one was open for 72% of the time, Pallas kernels for 0%

commit v1 on v0

v1 whole, which is shorter than its diff:
```python
import math

import jax
import jax.numpy as jnp
import numpy as np
from jax import lax
from jax.experimental import pallas as pl
from jax.experimental.pallas import tpu as pltpu
from jax.sharding import PartitionSpec as P

DAUBECHIES = (
    (0.7071067811865476, 0.7071067811865476),
    (0.48296291314469025, 0.836516303737469, 0.22414386804185735, -0.12940952255092145),
    (
        0.3326705529509569,
        0.8068915093133388,
        0.4598775021193313,
        -0.13501102001039084,
        -0.08544127388224149,
        0.035226291882100656,
    ),
    (
        0.23037781330885523,
        0.7148465705525415,
        0.6308807679295904,
        -0.02798376941698385,
        -0.18703481171888114,
        0.030841381835986965,
        0.032883011666982945,
        -0.010597401784997278,
    ),
)
NDB = len(DAUBECHIES)
JACOBI_SWEEPS = 6
STEP_PRIMAL = 0.2
STEP_SPARSE = 0.5
SPARSE_SCALE = 0.5
LANES = 128
HALO = 8
MIB = 1 << 20
F32 = jnp.float32
BF16 = jnp.bfloat16


def band_taps(family):
    low = DAUBECHIES[family]
    high = [(-1.0) ** k * low[len(low) - 1 - k] for k in range(len(low))]
    return low, high


def phase_taps(family):
    low, high = band_taps(family)
    offset = len(low) // 2 - 1
    table = {}
    for k in range(len(low)):
        s, odd = divmod(k - offset, 2)
        entry = table.setdefault(s, [0.0, 0.0, 0.0, 0.0])
        entry[odd] = low[k]
        entry[2 + odd] = high[k]
    return table


def column_weight(family, band, coefs, pixels):
    taps = band_taps(family)[band]
    k = pixels[:, None] - 2 * coefs[None, :] + len(taps) // 2 - 1
    inside = (k >= 0) & (k < len(taps))
    return np.where(inside, np.asarray(taps)[np.clip(k, 0, len(taps) - 1)], 0.0)


def column_tables(cols, facets):
    half = cols // 2
    pixels = np.arange(cols)
    pairs = [(f, b) for b in range(2) for f in range(NDB)]
    main = np.concatenate([column_weight(f, b, np.arange(half), pixels) for f, b in pairs], 1)
    left, right = pixels[:LANES] - LANES, pixels[:LANES] + cols
    variants = []
    for has_left, has_right in ((False, True), (True, False)) if facets == 2 else ((False, True), (True, True), (True, False)):
        coefs = np.array([-2, -1, half, half + 1])
        real = np.array([has_left, has_left, has_right, has_right])
        around = ([left] if has_left else []) + ([right] if has_right else []) if facets == 2 else [left, right]
        around = np.concatenate(around)

        def strip(rows):
            parts = [column_weight(f, b, coefs, rows) * real for f, b in pairs]
            return np.pad(np.concatenate(parts, 1), ((0, 0), (0, LANES - 4 * len(parts))))

        halo_main = np.concatenate([column_weight(f, b, np.arange(half), around) for f, b in pairs], 1)
        variants.append((strip(pixels), np.concatenate([halo_main, strip(around)], 1)))
    return main, np.stack([v[0] for v in variants]), np.stack([v[1] for v in variants])


def split(table):
    table = jnp.asarray(table, F32)
    top = table.astype(BF16)
    return top, (table - top.astype(F32)).astype(BF16)


def halves(values):
    top = values.astype(BF16)
    return top, (values - top.astype(F32)).astype(BF16)


def dot3(left, right_top, right_low):
    top, low = left
    total = jnp.dot(top, right_low, preferred_element_type=F32) + jnp.dot(low, right_top, preferred_element_type=F32)
    return total + jnp.dot(top, right_top, preferred_element_type=F32)


def side_by_side(ref, tiles):
    return jnp.concatenate([ref[t] for t in tiles], 1)


def swap_halves(values):
    return pltpu.roll(values, 4, 0)


def sublane_taps(first, second):
    rows = lax.broadcasted_iota(jnp.int32, (8, LANES), 0)
    return jnp.where(rows < 4, F32(first), F32(second))


def strip_taps(pick_first, pick_second, s):
    family = lax.broadcasted_iota(jnp.int32, (8, LANES), 1) // 4 % 4
    total = jnp.zeros((8, LANES), F32)
    for f in range(NDB):
        entry = phase_taps(f).get(s)
        if entry is not None:
            total = jnp.where(family == f, sublane_taps(entry[pick_first], entry[pick_second]), total)
    return total


def row_taps(tile, tiles, cross, scale):
    if tile == tiles - 1:
        shifts = range(-2, 3)
        return {s: (strip_taps(0, 3, s) * scale, strip_taps(*cross, s) * scale) for s in shifts}
    table = phase_taps(tile % NDB)
    return {s: (sublane_taps(e[0] * scale, e[3] * scale), sublane_taps(e[cross[0]] * scale, e[cross[1]] * scale)) for s, e in table.items()}


def pack4(squares):
    rows = lax.broadcasted_iota(jnp.int32, (8, LANES), 0)

    def merge(a, b, step):
        keep = rows % (2 * step) < step
        if b is None:
            return a + pltpu.roll(a, 8 - step, 0)
        return jnp.where(keep, a, pltpu.roll(b, step, 0)) + jnp.where(keep, pltpu.roll(a, 8 - step, 0), b)

    items = list(squares) + [None] * (4 - len(squares))
    first = merge(items[0], items[1], 1)
    second = None if items[2] is None else merge(items[2], items[3], 1)
    return merge(first, second, 2)


def analysis_kernel(sides, dirty, above, beside, corner, main_t, main_l, strip_t, strip_l, halo_t, halo_l, u_ref, n_ref, ext, coef):
    channels, rows, cols = dirty.shape
    window = rows + HALO + 4
    x, y = lax.axis_index("frow"), lax.axis_index("chan") % 2
    place, facets = lax.axis_index("fcol"), lax.axis_size("fcol")
    var = place if facets == 2 else jnp.where(place == 0, 0, jnp.where(place == facets - 1, 2, 1))
    tiles = 2 * NDB + 1

    edge = jnp.zeros((ext.shape[0], 4 * channels, LANES), F32)
    ext[:, pl.ds(pl.multiple_of(x * (window - 4) * channels, 16), 4 * channels), :] = edge
    for start, count, mid, wing in ((4 + 4 * x, rows, dirty, beside), ((1 - x) * (window - HALO), HALO, above, corner)):
        for c in range(channels):
            at = pl.ds(start * channels + c, count, stride=channels)
            for t in range(cols // LANES):
                ext[t, at, :] = jnp.maximum(mid[c, :, t * LANES : (t + 1) * LANES], 0.0)
            for t in range(sides):
                ext[cols // LANES + t, at, :] = jnp.maximum(wing[c, :, t * LANES : (t + 1) * LANES], 0.0)

    inner = halves(side_by_side(ext, range(cols // LANES)))
    outer = halves(side_by_side(ext, range(cols // LANES, cols // LANES + sides)))
    coef[:, : cols * NDB] = dot3(inner, main_t[...], main_l[...]) + dot3(outer, halo_t[var, :, : cols * NDB], halo_l[var, :, : cols * NDB])
    coef[:, cols * NDB :] = dot3(inner, strip_t[var], strip_l[var]) + dot3(outer, halo_t[var, :, cols * NDB :], halo_l[var, :, cols * NDB :])

    outs = rows // 2 + 2
    squares = {}
    for tile in range(tiles):
        lanes = slice(tile * LANES, (tile + 1) * LANES)
        taps = row_taps(tile, tiles, (2, 1), STEP_SPARSE)
        pairs = [coef[8 * i : 8 * i + 8, lanes] for i in range(window // 2)]
        for j in range(outs):
            direct = crossed = None
            for s, (d, e) in taps.items():
                source = pairs[j + 2 + s]
                direct = d * source if direct is None else direct + d * source
                crossed = e * source if crossed is None else crossed + e * source
            value = direct + swap_halves(crossed)
            u_ref[8 * j : 8 * j + 8, lanes] = value
            squares[tile, j] = value * value
        if tile % NDB == NDB - 1:
            side = (tile // NDB) ^ y
            flat = [squares.pop((t, j)) for t in range(tile - NDB + 1, tile + 1) for j in range(outs)]
            for g in range(len(flat) // 4):
                n_ref[side, 8 * g : 8 * g + 8, :] = pack4(flat[4 * g : 4 * g + 4])
    base = outs * NDB * 2
    for half in range(2):
        at = base
        flat = [squares.pop((tiles - 1, j)) for j in range(half * outs // 2, (half + 1) * outs // 2)]
        for g in range(0, len(flat), 4):
            n_ref[half ^ y, at : at + 8, :] = pack4(flat[g : g + 4])
            at += 8
        for r in range(half * rows // 2, (half + 1) * rows // 2, 8):
            for t in range(cols // LANES):
                total = None
                for c in range(channels):
                    value = STEP_SPARSE * jnp.maximum(dirty[c, r : r + 8, t * LANES : (t + 1) * LANES], 0.0)
                    total = value * value if total is None else total + value * value
                n_ref[half ^ y, at : at + 8, :] = total
                at += 8


def pairing_rounds(order):
    players = list(range(order))
    rounds = []
    for _ in range(order - 1):
        rounds.append([(min(a, b), max(a, b)) for a, b in zip(players[: order // 2], players[: order // 2 - 1 : -1])])
        players = [players[0]] + [players[-1]] + players[1:-1]
    return rounds


def down(values):
    for step in (4, 2, 1):
        values = values + pltpu.roll(values, step, 0)
    return values


def nuclear_kernel(limit, own, other, out, group, mix):
    channels, rows, cols = own.shape
    order = 2 * channels
    y = lax.axis_index("chan") % 2
    for c in range(channels):
        group[y * channels + c] = jnp.maximum(own[c], 0.0)
        group[(1 - y) * channels + c] = jnp.maximum(other[c], 0.0)
    blocks = [(slice(r, r + 8), slice(t, t + LANES)) for r in range(0, rows, 8) for t in range(0, cols, LANES)]
    partial = {}
    for at in blocks:
        held = [group[(c, *at)] for c in range(order)]
        for i in range(order):
            for j in range(i + 1):
                term = held[i] * held[j]
                partial[i, j] = partial[i, j] + term if (i, j) in partial else term
    row_sum = {key: jnp.sum(value, axis=0, keepdims=True) for key, value in partial.items()}
    sub = lax.broadcasted_iota(jnp.int32, (order, LANES), 0)
    turned, vectors, diag = [], [], []
    for j in range(order):
        stacked = jnp.concatenate([row_sum[max(i, j), min(i, j)] for i in range(order)], 0)
        column = jnp.broadcast_to(jnp.sum(stacked, axis=1, keepdims=True), (order, LANES))
        turned.append(column)
        unit = jnp.where(sub == j, F32(1.0), F32(0.0))
        vectors.append(unit)
        diag.append(down(column * unit))

    rounds = pairing_rounds(order)

    def sweep(_, state):
        turned, vectors, diag = (list(part) for part in state)
        for pairs in rounds:
            for p, q in pairs:
                coupling = down(vectors[p] * turned[q])
                spread = diag[q] - diag[p]
                square = spread * spread + 4.0 * coupling * coupling
                positive = square > 0.0
                inverse = jnp.where(positive, lax.rsqrt(jnp.where(positive, square, 1.0)), 0.0)
                cosine2 = jnp.where(positive, 0.5 + 0.5 * jnp.abs(spread) * inverse, 1.0)
                other = lax.rsqrt(cosine2)
                c = cosine2 * other
                s = jnp.where(spread >= 0.0, coupling, -coupling) * inverse * other
                shift = s * other * coupling
                diag[p], diag[q] = diag[p] - shift, diag[q] + shift
                turned[p], turned[q] = c * turned[p] - s * turned[q], s * turned[p] + c * turned[q]
                vectors[p], vectors[q] = c * vectors[p] - s * vectors[q], s * vectors[p] + c * vectors[q]
        return tuple(turned), tuple(vectors), tuple(diag)

    turned, vectors, _ = lax.fori_loop(0, JACOBI_SWEEPS, sweep, (tuple(turned), tuple(vectors), tuple(diag)))
    weighted = []
    for j in range(order):
        value = down(vectors[j] * turned[j])
        weighted.append(vectors[j] * (limit / jnp.maximum(jnp.sqrt(jnp.maximum(value, 0.0)), limit)))
    for k in range(order):
        total = None
        for j in range(order):
            term = weighted[j] * jnp.broadcast_to(vectors[j][k : k + 1, :], (order, LANES))
            total = term if total is None else total + term
        mix[k] = total
    for i in range(channels):
        row = [jnp.broadcast_to(mix[k, pl.ds(y * channels + i, 1), :], (order, LANES)) for k in range(order)]
        for at in blocks:
            total = None
            for k in range(order):
                term = row[k] * group[(k, *at)]
                total = term if total is None else total + term
            out[(i, *at)] = total


def synthesis_kernel(limit, dirty, density, nuclear, u_ref, n_ref, main_t, main_l, strip_t, strip_l, out, scale, spread, image):
    channels, rows, cols = dirty.shape
    x, y = lax.axis_index("frow"), lax.axis_index("chan") % 2
    place, facets = lax.axis_index("fcol"), lax.axis_size("fcol")
    var = place if facets == 2 else jnp.where(place == 0, 0, jnp.where(place == facets - 1, 2, 1))
    tiles = 2 * NDB + 1
    outs = rows // 2 + 2
    for half in range(2):
        scale[half] = limit * lax.rsqrt(jnp.maximum(n_ref[half ^ y], limit * limit))
    sub = lax.broadcasted_iota(jnp.int32, (8, LANES), 0)

    def widen(half, at, item):
        first = jnp.broadcast_to(scale[half, at + item : at + item + 1, :], (8, LANES))
        second = jnp.broadcast_to(scale[half, at + 4 + item : at + 5 + item, :], (8, LANES))
        return jnp.where(sub < 4, first, second)

    base = outs * NDB * 2
    strips = (outs // 2 + 3) // 4
    for tile in range(tiles):
        lanes = slice(tile * LANES, (tile + 1) * LANES)
        taps = row_taps(tile, tiles, (1, 2), 1.0)
        dual = []
        for j in range(outs):
            if tile == tiles - 1:
                half, item = divmod(j, outs // 2)
                factor = widen(half, base + 8 * (item // 4), item % 4)
            else:
                half, item = tile // NDB, (tile % NDB) * outs + j
                factor = widen(half, 8 * (item // 4), item % 4)
            dual.append(u_ref[8 * j : 8 * j + 8, lanes] * factor)
        empty = jnp.zeros((8, LANES), F32)
        below = [jnp.where(x == 0, empty, dual[0]), jnp.where(x == 0, empty, dual[1])]
        middle = [jnp.where(x == 0, dual[i], dual[i + 2]) for i in range(rows // 2)]
        after = [jnp.where(x == 0, dual[outs - 2], empty), jnp.where(x == 0, dual[outs - 1], empty)]
        padded = below + middle + after
        for i in range(rows // 2):
            direct = crossed = None
            for s, (d, e) in taps.items():
                source = padded[i + 2 - s]
                direct = d * source if direct is None else direct + d * source
                crossed = e * source if crossed is None else crossed + e * source
            spread[8 * i : 8 * i + 8, lanes] = direct + swap_halves(crossed)
    result = dot3(halves(spread[:, : cols * NDB]), main_t[...], main_l[...]) + dot3(halves(spread[:, cols * NDB :]), strip_t[var], strip_l[var])
    for t in range(cols // LANES):
        image[t] = result[:, t * LANES : (t + 1) * LANES]
    for c in range(channels):
        for r in range(0, rows, 8):
            for t in range(cols // LANES):
                lanes = slice(t * LANES, (t + 1) * LANES)
                half, inside = divmod(r, rows // 2)
                at = base + 8 * strips + 8 * (inside // 8 * (cols // LANES) + t)
                raw = dirty[c, r : r + 8, lanes]
                estimate = jnp.maximum(raw, 0.0)
                dual = STEP_SPARSE * estimate * scale[half, at : at + 8, :]
                synthesis = dual + image[t, pl.ds(r * channels + c, 8, stride=channels), :]
                step = density[c, r : r + 8, lanes] * estimate - raw + nuclear[c, r : r + 8, lanes] + synthesis
                out[c, r : r + 8, lanes] = jnp.maximum(estimate - STEP_PRIMAL * step, 0.0)


def exchange(values, axis, bit):
    count = lax.axis_size(axis)
    return lax.ppermute(values, axis, [(i, i ^ bit) for i in range(count)])


def vmem(count):
    return [pl.BlockSpec(memory_space=pltpu.VMEM)] * count


def beside_columns(values, facets):
    last, first = values[..., values.shape[-1] - LANES :], values[..., :LANES]
    if facets == 2:
        return exchange(jnp.where(lax.axis_index("fcol") == 0, last, first), "fcol", 1)
    left = lax.ppermute(last, "fcol", [(i, i + 1) for i in range(facets - 1)])
    right = lax.ppermute(first, "fcol", [(i + 1, i) for i in range(facets - 1)])
    return jnp.concatenate([left, right], -1)


def on_device(dirty_image, density):
    channels, rows, cols = dirty_image.shape
    facets, chans = lax.axis_size("fcol"), lax.axis_size("chan")
    nuclear_limit = math.sqrt(rows * cols)
    sparse_limit = SPARSE_SCALE * math.sqrt(channels * chans)
    main, strip, halo = column_tables(cols, facets)
    sides = halo.shape[1] // LANES
    main_t, main_l = split(main)
    strip_t, strip_l = split(strip)
    halo_t, halo_l = split(halo)
    main_back, main_back_l = split(main.T)
    strip_back, strip_back_l = split(strip.transpose(0, 2, 1))

    x = lax.axis_index("frow")
    edge = lax.dynamic_slice_in_dim(dirty_image, (1 - x) * (rows - HALO), HALO, 1)
    above = exchange(edge, "frow", 1)
    other = exchange(dirty_image, "chan", 1)
    beside = beside_columns(dirty_image, facets)
    corner = beside_columns(above, facets)

    window = rows + HALO + 4
    outs = rows // 2 + 2
    tiles = 2 * NDB + 1
    packed = outs * NDB * 2 + 8 * ((outs // 2 + 3) // 4) + rows * cols // LANES // 2
    coefs, norms = pl.pallas_call(
        lambda *refs: analysis_kernel(sides, *refs),
        name="analysis",
        out_shape=(jax.ShapeDtypeStruct((8 * outs, tiles * LANES), F32), jax.ShapeDtypeStruct((2, packed, LANES), F32)),
        in_specs=vmem(10),
        out_specs=tuple(vmem(2)),
        scratch_shapes=[pltpu.VMEM((cols // LANES + sides, window * channels, LANES), F32), pltpu.VMEM((window * channels, tiles * LANES), F32)],
        compiler_params=pltpu.CompilerParams(vmem_limit_bytes=24 * MIB),
    )(dirty_image, above, beside, corner, main_t, main_l, strip_t, strip_l, halo_t, halo_l)

    nuclear = pl.pallas_call(
        lambda *refs: nuclear_kernel(nuclear_limit, *refs),
        name="nuclear",
        out_shape=jax.ShapeDtypeStruct(dirty_image.shape, F32),
        in_specs=vmem(2),
        out_specs=vmem(1)[0],
        scratch_shapes=[pltpu.VMEM((2 * channels, rows, cols), F32), pltpu.VMEM((2 * channels, 2 * channels, LANES), F32)],
        compiler_params=pltpu.CompilerParams(vmem_limit_bytes=16 * MIB),
    )(dirty_image, other)

    total = norms[0] + exchange(norms[1], "chan", 1)
    bit = 2
    while bit < chans:
        total = total + exchange(total, "chan", bit)
        bit *= 2
    totals = jnp.stack([total, exchange(total, "chan", 1)], 0)

    return pl.pallas_call(
        lambda *refs: synthesis_kernel(sparse_limit, *refs),
        name="synthesis",
        out_shape=jax.ShapeDtypeStruct(dirty_image.shape, F32),
        in_specs=vmem(9),
        out_specs=vmem(1)[0],
        scratch_shapes=[
            pltpu.VMEM((2, packed, LANES), F32),
            pltpu.VMEM((4 * rows, tiles * LANES), F32),
            pltpu.VMEM((cols // LANES, 4 * rows, LANES), F32),
        ],
        compiler_params=pltpu.CompilerParams(vmem_limit_bytes=24 * MIB),
    )(dirty_image, density, nuclear, coefs, totals, main_back, main_back_l, strip_back, strip_back_l)


def solution(mesh):
    return jax.shard_map(
        on_device,
        mesh=mesh,
        in_specs=(P("chan", "frow", "fcol"), P("chan", "frow", "fcol")),
        out_specs=P("chan", "frow", "fcol"),
        check_vma=False,
    )
```

time: 635 us -> 35.8 us (0.06); the launches traced: 624 us -> 35.4 us
  local copies, waits for them, and re-layouts: 440 us -> 5.95 us
  waiting for transfers between devices: 74.6 us -> 10.9 us
  blocking collectives: 36.1 us -> 0 us
  other arithmetic: 26.9 us -> 0.96 us
  between operations: 15.6 us -> 0.12 us
  starting transfers between devices: 27 us -> 13.2 us
    gather x733 -> x0, local copies, waits for them, and re-layouts: 310 us -> none  [the longest x156 56 us: rotate_cols(): return joined[..., :, restore]]
    psum x1 -> x0, waiting for transfers between devices: 70.3 us -> none  [on_device(): lax.psum((norm_terms, partial_gram_blocks), 'chan')]
    unnamed x158 -> x24, local copies, waits for them, and re-layouts: 62.6 us -> 5.14 us
    psum x1 -> x0, blocking collectives: 36.1 us -> none  [on_device(): lax.psum((norm_terms, partial_gram_blocks), 'chan')]
    slice x60 -> x0, local copies, waits for them, and re-layouts: 34 us -> none  [the longest x48 22.1 us: analyse_axis(): lax.slice_in_dim(extended, start_at, start_at + 2 * half_total - 1, 2, ax...]
    all_to_all x2 -> x0, starting transfers between devices: 9.83 us -> none  [the longest x1 5.83 us: on_device(): lax.all_to_all(shifted, 'chan', split_axis=1, concat_axis=0, tiled=True)]
    concatenate x138 -> x0, other arithmetic: 9.73 us -> none  [the longest x3 7.48 us: extended_2(): jnp.concatenate([lax.ppermute(tail, axis, [(i, (i + 1) % count) for i in...]
    ppermute x4 -> x0, local copies, waits for them, and re-layouts: 7.03 us -> none  [the longest x2 3.54 us: extended_2(): lax.ppermute(tail, axis, [(i, (i + 1) % count) for i in range(ends)])]
  transfers between devices with their start and end apart: 11 -> 8, of which waited for: 3 -> 6; matrix products, arithmetic and copies ran while one was open for 72% -> 3% of each run, Pallas kernels for 0% -> 5%
where the time goes in v1:
time: 35.8 us; the launch traced here: 35.4 us
  starting transfers between devices  13.2 us (37%)
  waiting for transfers between devices  10.9 us (30%)
  local copies, waits for them, and re-layouts  5.95 us (17%)
  Pallas kernels  4.32 us (12%)
  other arithmetic  0.96 us (3%)
    ppermute x8, starting transfers between devices, exchange(): return lax.ppermute(values, axis, [(i, i ^ bit) for i in range(count)])  13.2 us
    ppermute x8, waiting for transfers between devices, exchange(): return lax.ppermute(values, axis, [(i, i ^ bit) for i in range(count)])  10.9 us
    unnamed x24, local copies, waits for them, and re-layouts  5.14 us
    pallas_call x1, Pallas kernels, on_device(): pl.pallas_call(lambda *refs: nuclear_kernel(nuclear_limit, *refs), name='...  1.83 us
    pallas_call x1, Pallas kernels, on_device(): pl.pallas_call(lambda *refs: synthesis_kernel(sparse_limit, *refs), name=...  1.36 us
    pallas_call x1, Pallas kernels, on_device(): pl.pallas_call(lambda *refs: analysis_kernel(sides, *refs), name='analysi...  1.13 us
    select_n x2, other arithmetic, beside_columns(): jnp.where(lax.axis_index('fcol') == 0, last, first)  0.89 us
    dynamic_slice x1, local copies, waits for them, and re-layouts, on_device(): lax.dynamic_slice_in_dim(dirty_image, (1 - x) * (rows - HALO), HALO, 1)  0.8 us
  transfers between devices with their start and end apart: 8, of which 6 were waited for; matrix products, arithmetic and copies ran while one was open for 3% of the time, Pallas kernels for 5%

profile of v1, /device:TPU:0, one launch (start us, length us, event | category | flops | bytes accessed | tf_op | source)
XLA Modules:
  0.0 35.4 jit_solution(12668507888581580889)
XLA Ops:
  0.0 0.8 %constant_dynamic-slice_fusion = f32[4,8,256]{2,1,0:T(8,128)S(1)} fusion(f32[4,32,256]{2,1,0:T(8,128)} %refs_0_.5, s32[]{:T(128)S(6)} %select_n.19), kind=kLoop, calls=%fused_computation.5 | loop fusion | bytes 65540 | tf_op jit(solution)/shard_map/dynamic_slice | solution.py:389
  0.8 2.9 %collective-permute-start.1 = (f32[4,8,256]{2,1,0:T(8,128)S(1)}, f32[4,8,256]{2,1,0:T(8,128)S(1)}, u32[]{:S(2)}, u32[]{:S(2)}) collective-permute-start(f32[4,8,256]{2,1,0:T(8,128)S(1)} %constant_dynamic-slice_fusion), channel_id=1, source_target_pairs={{0,16},{16,0},{1,17},{17,1},{2,18},{18,2},{3,19},{19,3},{4,20},{20... | collective-permute-start | bytes 98312 | tf_op jit(solution)/shard_map/ppermute | solution.py:359
  3.7 0.9 %slice_select_fusion = f32[4,32,128]{2,1,0:T(8,128)S(1)} fusion(f32[4,32,256]{2,1,0:T(8,128)} %refs_0_.5, pred[]{:T(512)S(6)} %eq.4), kind=kLoop, calls=%fused_computation.3 | loop fusion | flops 16384 | bytes 196609 | tf_op jit(solution)/shard_map/jit(_where)/select_n | solution.py:369
  4.6 0.1 collective-permute-start.2
  4.7 0.9 %collective-permute-done.1.refs_1_ = f32[4,8,256]{2,1,0:T(8,128)S(1)} collective-permute-done((f32[4,8,256]{2,1,0:T(8,128)S(1)}, f32[4,8,256]{2,1,0:T(8,128)S(1)}, u32[]{:S(2)}, u32[]{:S(2)}) %collective-permute-start.1) | collective-permute-done | bytes 32800 | tf_op jit(solution)/shard_map/ppermute | solution.py:359
  5.6 1.2 %collective-permute-done.3.refs_3_ = f32[4,8,128]{2,1,0:T(8,128)S(1)} collective-permute-done((f32[4,8,128]{2,1,0:T(8,128)S(1)}, f32[4,8,128]{2,1,0:T(8,128)S(1)}, u32[]{:S(2)}, u32[]{:S(2)}) %collective-permute-start.3) | collective-permute-done | bytes 16416 | tf_op jit(solution)/shard_map/ppermute | solution.py:359
  6.8 1.1 %copy-done.1 = bf16[2,128,1152]{2,1,0:T(8,128)(2,1)S(1)} copy-done((bf16[2,128,1152]{2,1,0:T(8,128)(2,1)S(1)}, bf16[2,128,1152]{2,1,0:T(8,128)(2,1)}, u32[]{:S(2)}) %copy-start.1) | copy-done | bytes 589848
  7.9 1.1 %copy-done.2 = bf16[2,128,1152]{2,1,0:T(8,128)(2,1)S(1)} copy-done((bf16[2,128,1152]{2,1,0:T(8,128)(2,1)S(1)}, bf16[2,128,1152]{2,1,0:T(8,128)(2,1)}, u32[]{:S(2)}) %copy-start.2) | copy-done | bytes 589848
  9.0 1.0 %copy-done.5 = bf16[256,1024]{1,0:T(8,128)(2,1)S(1)} copy-done((bf16[256,1024]{1,0:T(8,128)(2,1)S(1)}, bf16[256,1024]{1,0:T(8,128)(2,1)}, u32[]{:S(2)}) %copy-start.5) | copy-done | bytes 524312
  10.0 1.0 %copy-done.6 = bf16[256,1024]{1,0:T(8,128)(2,1)S(1)} copy-done((bf16[256,1024]{1,0:T(8,128)(2,1)S(1)}, bf16[256,1024]{1,0:T(8,128)(2,1)}, u32[]{:S(2)}) %copy-start.6) | copy-done | bytes 524312
  11.1 0.9 %copy-done.11 = bf16[2,256,128]{2,1,0:T(8,128)(2,1)S(1)} copy-done((bf16[2,256,128]{2,1,0:T(8,128)(2,1)S(1)}, bf16[2,256,128]{2,1,0:T(8,128)(2,1)}, u32[]{:S(2)}) %copy-start.11) | copy-done | bytes 131096
  12.0 1.1 %analysis.1 = (f32[144,1152]{1,0:T(8,128)S(1)}, f32[2,200,128]{2,1,0:T(8,128)S(1)}) custom-call(f32[4,32,256]{2,1,0:T(8,128)S(1)} %copy-done, f32[4,8,256]{2,1,0:T(8,128)S(1)} %collective-permute-done.1.refs_1_, f32[4,32,128]{2,1,0:T(8,128)S(1)} %collective-permute-done.2.refs_2_, f32[4,8,128]{2,1,0:T(8,128)S(1)} %collective-permute-done.3.refs_3_, ...), custom_call_target="tpu_custom_call" | custom-call | tf_op jit(solution)/shard_map/analysis/pallas_call | solution.py:399
  13.1 2.1 %collective-permute-start.4 = (f32[200,128]{1,0:T(8,128)S(1)}, f32[200,128]{1,0:T(8,128)S(1)}, u32[]{:S(2)}, u32[]{:S(2)}) collective-permute-start(f32[200,128]{1,0:T(8,128)S(1)} %slice_bitcast_fusion), channel_id=1, source_target_pairs={{0,1},{1,0},{2,3},{3,2},{4,5},{5,4},{6,7},{7,6},{8,9},{9,8},{10,11... | collective-permute-start | bytes 307208 | tf_op jit(solution)/shard_map/ppermute | solution.py:359
  15.2 3.2 %collective-permute-done.4 = f32[200,128]{1,0:T(8,128)S(1)} collective-permute-done((f32[200,128]{1,0:T(8,128)S(1)}, f32[200,128]{1,0:T(8,128)S(1)}, u32[]{:S(2)}, u32[]{:S(2)}) %collective-permute-start.4) | collective-permute-done | bytes 102432 | tf_op jit(solution)/shard_map/ppermute | solution.py:359
  18.4 1.9 %collective-permute-start.5 = (f32[200,128]{1,0:T(8,128)S(1)}, f32[200,128]{1,0:T(8,128)S(1)}, u32[]{:S(2)}, u32[]{:S(2)}) collective-permute-start(f32[200,128]{1,0:T(8,128)S(1)} %bitcast_add_fusion), channel_id=1, source_target_pairs={{0,2},{1,3},{2,0},{3,1},{4,6},{5,7},{6,4},{7,5},{8,10},{9,11},{10,... | collective-permute-start | bytes 307208 | tf_op jit(solution)/shard_map/ppermute | solution.py:359
  20.3 2.9 %collective-permute-done.5 = f32[200,128]{1,0:T(8,128)S(1)} collective-permute-done((f32[200,128]{1,0:T(8,128)S(1)}, f32[200,128]{1,0:T(8,128)S(1)}, u32[]{:S(2)}, u32[]{:S(2)}) %collective-permute-start.5) | collective-permute-done | bytes 102432 | tf_op jit(solution)/shard_map/ppermute | solution.py:359
  23.2 0.0 copy-start.3
  23.2 2.9 %collective-permute-start.6 = (f32[200,128]{1,0:T(8,128)S(1)}, f32[200,128]{1,0:T(8,128)S(1)}, u32[]{:S(2)}, u32[]{:S(2)}) collective-permute-start(f32[200,128]{1,0:T(8,128)S(1)} %add.14), channel_id=1, source_target_pairs={{0,4},{1,5},{2,6},{3,7},{4,0},{5,1},{6,2},{7,3},{8,12},{9,13},{10,... | collective-permute-start | bytes 307208 | tf_op jit(solution)/shard_map/ppermute | solution.py:359
  26.1 1.5 %collective-permute-start = (f32[4,32,256]{2,1,0:T(8,128)S(1)}, f32[4,32,256]{2,1,0:T(8,128)S(1)}, u32[]{:S(2)}, u32[]{:S(2)}) collective-permute-start(f32[4,32,256]{2,1,0:T(8,128)S(1)} %copy-done), channel_id=1, source_target_pairs={{0,1},{1,0},{2,3},{3,2},{4,5},{5,4},{6,7},{7,6},{8,9},{9,8},{10,11... | collective-permute-start | bytes 393224 | tf_op jit(solution)/shard_map/ppermute | solution.py:359
  27.6 1.2 %collective-permute-done.6 = f32[200,128]{1,0:T(8,128)S(1)} collective-permute-done((f32[200,128]{1,0:T(8,128)S(1)}, f32[200,128]{1,0:T(8,128)S(1)}, u32[]{:S(2)}, u32[]{:S(2)}) %collective-permute-start.6) | collective-permute-done | bytes 102432 | tf_op jit(solution)/shard_map/ppermute | solution.py:359
  28.9 1.8 %collective-permute-start.7 = (f32[200,128]{1,0:T(8,128)S(1)}, f32[200,128]{1,0:T(8,128)S(1)}, u32[]{:S(2)}, u32[]{:S(2)}) collective-permute-start(f32[200,128]{1,0:T(8,128)S(1)} %add.15), channel_id=1, source_target_pairs={{0,1},{1,0},{2,3},{3,2},{4,5},{5,4},{6,7},{7,6},{8,9},{9,8},{10,11... | collective-permute-start | bytes 307208 | tf_op jit(solution)/shard_map/ppermute | solution.py:359
  30.7 1.5 %collective-permute-done.refs_1_ = f32[4,32,256]{2,1,0:T(8,128)S(1)} collective-permute-done((f32[4,32,256]{2,1,0:T(8,128)S(1)}, f32[4,32,256]{2,1,0:T(8,128)S(1)}, u32[]{:S(2)}, u32[]{:S(2)}) %collective-permute-start) | collective-permute-done | bytes 131104 | tf_op jit(solution)/shard_map/ppermute | solution.py:359
  32.2 1.8 %nuclear.1.refs_2_ = f32[4,32,256]{2,1,0:T(8,128)S(1)} custom-call(f32[4,32,256]{2,1,0:T(8,128)S(1)} %copy-done, f32[4,32,256]{2,1,0:T(8,128)S(1)} %collective-permute-done.refs_1_), custom_call_target="tpu_custom_call" | custom-call | tf_op jit(solution)/shard_map/nuclear/pallas_call | solution.py:409
  34.1 1.4 %synthesis.1 = f32[4,32,256]{2,1,0:T(8,128)} custom-call(f32[4,32,256]{2,1,0:T(8,128)S(1)} %copy-done, f32[4,32,256]{2,1,0:T(8,128)S(1)} %copy-done.7, f32[4,32,256]{2,1,0:T(8,128)S(1)} %nuclear.1.refs_2_, f32[144,1152]{1,0:T(8,128)S(1)} %get-tuple-element.7.refs_3_, f32[2,200,128]{2,1,0:T(8,128)S(1)} %pad_maximum_fusion.refs_4_, ...), custom_call_target="tpu_custom_call" | custom-call | tf_op jit(solution)/shard_map/synthesis/pallas_call | solution.py:426
  (27 shorter events, 0.1 us)
Async XLA Ops:
  0.0 6.8 %copy-start.10 = (bf16[2,256,128]{2,1,0:T(8,128)(2,1)S(1)}, bf16[2,256,128]{2,1,0:T(8,128)(2,1)}, u32[]{:S(2)}) copy-start(bf16[2,256,128]{2,1,0:T(8,128)(2,1)} %constant.39.refs_6_) | copy-start | bytes 393220
  0.8 6.0 %copy-start = (f32[4,32,256]{2,1,0:T(8,128)S(1)}, f32[4,32,256]{2,1,0:T(8,128)}, u32[]{:S(2)}) copy-start(f32[4,32,256]{2,1,0:T(8,128)} %refs_0_.5) | copy-start | bytes 393220
  0.8 4.8 %collective-permute-start.1 = (f32[4,8,256]{2,1,0:T(8,128)S(1)}, f32[4,8,256]{2,1,0:T(8,128)S(1)}, u32[]{:S(2)}, u32[]{:S(2)}) collective-permute-start(f32[4,8,256]{2,1,0:T(8,128)S(1)} %constant_dynamic-slice_fusion), channel_id=1, source_target_pairs={{0,16},{16,0},{1,17},{17,1},{2,18},{18,2},{3,19},{19,3},{4,20},{20... | collective-permute-start | bytes 98312 | tf_op jit(solution)/shard_map/ppermute | solution.py:359
  4.6 2.2 %collective-permute-start.2 = (f32[4,32,128]{2,1,0:T(8,128)S(1)}, f32[4,32,128]{2,1,0:T(8,128)S(1)}, u32[]{:S(2)}, u32[]{:S(2)}) collective-permute-start(f32[4,32,128]{2,1,0:T(8,128)S(1)} %slice_select_fusion), channel_id=1, source_target_pairs={{0,8},{8,0},{1,9},{9,1},{2,10},{10,2},{3,11},{11,3},{4,12},{12,4},... | collective-permute-start | bytes 196616 | tf_op jit(solution)/shard_map/ppermute | solution.py:359
  5.6 1.2 %collective-permute-start.3 = (f32[4,8,128]{2,1,0:T(8,128)S(1)}, f32[4,8,128]{2,1,0:T(8,128)S(1)}, u32[]{:S(2)}, u32[]{:S(2)}) collective-permute-start(f32[4,8,128]{2,1,0:T(8,128)S(1)} %slice_select_fusion.1), channel_id=1, source_target_pairs={{0,8},{8,0},{1,9},{9,1},{2,10},{10,2},{3,11},{11,3},{4,12},{12,4},... | collective-permute-start | bytes 49160 | tf_op jit(solution)/shard_map/ppermute | solution.py:359
  6.8 1.1 %copy-start.1 = (bf16[2,128,1152]{2,1,0:T(8,128)(2,1)S(1)}, bf16[2,128,1152]{2,1,0:T(8,128)(2,1)}, u32[]{:S(2)}) copy-start(bf16[2,128,1152]{2,1,0:T(8,128)(2,1)} %constant.43.refs_8_) | copy-start | bytes 1769476
  7.9 1.1 %copy-start.2 = (bf16[2,128,1152]{2,1,0:T(8,128)(2,1)S(1)}, bf16[2,128,1152]{2,1,0:T(8,128)(2,1)}, u32[]{:S(2)}) copy-start(bf16[2,128,1152]{2,1,0:T(8,128)(2,1)} %constant.46.refs_9_) | copy-start | bytes 1769476
  9.0 1.0 %copy-start.5 = (bf16[256,1024]{1,0:T(8,128)(2,1)S(1)}, bf16[256,1024]{1,0:T(8,128)(2,1)}, u32[]{:S(2)}) copy-start(bf16[256,1024]{1,0:T(8,128)(2,1)} %constant.35.refs_4_) | copy-start | bytes 1572868
  10.0 1.0 %copy-start.6 = (bf16[256,1024]{1,0:T(8,128)(2,1)S(1)}, bf16[256,1024]{1,0:T(8,128)(2,1)}, u32[]{:S(2)}) copy-start(bf16[256,1024]{1,0:T(8,128)(2,1)} %constant.38.refs_5_) | copy-start | bytes 1572868
  11.0 0.9 %copy-start.11 = (bf16[2,256,128]{2,1,0:T(8,128)(2,1)S(1)}, bf16[2,256,128]{2,1,0:T(8,128)(2,1)}, u32[]{:S(2)}) copy-start(bf16[2,256,128]{2,1,0:T(8,128)(2,1)} %constant.42.refs_7_) | copy-start | bytes 393220
  13.1 5.3 %collective-permute-start.4 = (f32[200,128]{1,0:T(8,128)S(1)}, f32[200,128]{1,0:T(8,128)S(1)}, u32[]{:S(2)}, u32[]{:S(2)}) collective-permute-start(f32[200,128]{1,0:T(8,128)S(1)} %slice_bitcast_fusion), channel_id=1, source_target_pairs={{0,1},{1,0},{2,3},{3,2},{4,5},{5,4},{6,7},{7,6},{8,9},{9,8},{10,11... | collective-permute-start | bytes 307208 | tf_op jit(solution)/shard_map/ppermute | solution.py:359
  18.4 15.6 %copy-start.9 = (bf16[2,128,256]{2,1,0:T(8,128)(2,1)S(1)}, bf16[2,128,256]{2,1,0:T(8,128)(2,1)}, u32[]{:S(2)}) copy-start(bf16[2,128,256]{2,1,0:T(8,128)(2,1)} %constant.54.refs_8_) | copy-start | bytes 393220
  18.4 4.7 %collective-permute-start.5 = (f32[200,128]{1,0:T(8,128)S(1)}, f32[200,128]{1,0:T(8,128)S(1)}, u32[]{:S(2)}, u32[]{:S(2)}) collective-permute-start(f32[200,128]{1,0:T(8,128)S(1)} %bitcast_add_fusion), channel_id=1, source_target_pairs={{0,2},{1,3},{2,0},{3,1},{4,6},{5,7},{6,4},{7,5},{8,10},{9,11},{10,... | collective-permute-start | bytes 307208 | tf_op jit(solution)/shard_map/ppermute | solution.py:359
  23.2 10.9 %copy-start.7 = (f32[4,32,256]{2,1,0:T(8,128)S(1)}, f32[4,32,256]{2,1,0:T(8,128)}, u32[]{:S(2)}) copy-start(f32[4,32,256]{2,1,0:T(8,128)} %refs_1_.1) | copy-start | bytes 393220
  23.2 10.9 %copy-start.8 = (bf16[2,128,256]{2,1,0:T(8,128)(2,1)S(1)}, bf16[2,128,256]{2,1,0:T(8,128)(2,1)}, u32[]{:S(2)}) copy-start(bf16[2,128,256]{2,1,0:T(8,128)(2,1)} %constant.51.refs_7_) | copy-start | bytes 393220
  23.2 10.9 %copy-start.3 = (bf16[1024,256]{1,0:T(8,128)(2,1)S(1)}, bf16[1024,256]{1,0:T(8,128)(2,1)}, u32[]{:S(2)}) copy-start(bf16[1024,256]{1,0:T(8,128)(2,1)} %constant.47.refs_5_) | copy-start | bytes 1572868
  23.2 10.9 %copy-start.4 = (bf16[1024,256]{1,0:T(8,128)(2,1)S(1)}, bf16[1024,256]{1,0:T(8,128)(2,1)}, u32[]{:S(2)}) copy-start(bf16[1024,256]{1,0:T(8,128)(2,1)} %constant.50.refs_6_) | copy-start | bytes 1572868
  23.2 5.6 %collective-permute-start.6 = (f32[200,128]{1,0:T(8,128)S(1)}, f32[200,128]{1,0:T(8,128)S(1)}, u32[]{:S(2)}, u32[]{:S(2)}) collective-permute-start(f32[200,128]{1,0:T(8,128)S(1)} %add.14), channel_id=1, source_target_pairs={{0,4},{1,5},{2,6},{3,7},{4,0},{5,1},{6,2},{7,3},{8,12},{9,13},{10,... | collective-permute-start | bytes 307208 | tf_op jit(solution)/shard_map/ppermute | solution.py:359
  26.1 6.1 %collective-permute-start = (f32[4,32,256]{2,1,0:T(8,128)S(1)}, f32[4,32,256]{2,1,0:T(8,128)S(1)}, u32[]{:S(2)}, u32[]{:S(2)}) collective-permute-start(f32[4,32,256]{2,1,0:T(8,128)S(1)} %copy-done), channel_id=1, source_target_pairs={{0,1},{1,0},{2,3},{3,2},{4,5},{5,4},{6,7},{7,6},{8,9},{9,8},{10,11... | collective-permute-start | bytes 393224 | tf_op jit(solution)/shard_map/ppermute | solution.py:359
  28.9 5.1 %collective-permute-start.7 = (f32[200,128]{1,0:T(8,128)S(1)}, f32[200,128]{1,0:T(8,128)S(1)}, u32[]{:S(2)}, u32[]{:S(2)}) collective-permute-start(f32[200,128]{1,0:T(8,128)S(1)} %add.15), channel_id=1, source_target_pairs={{0,1},{1,0},{2,3},{3,2},{4,5},{5,4},{6,7},{7,6},{8,9},{9,8},{10,11... | collective-permute-start | bytes 307208 | tf_op jit(solution)/shard_map/ppermute | solution.py:359

commit v2 on v1

v2 whole, which is shorter than its diff:
```python
import math

import jax
import jax.numpy as jnp
import numpy as np
from jax import lax
from jax.experimental import pallas as pl
from jax.experimental.pallas import tpu as pltpu
from jax.sharding import PartitionSpec as P

DAUBECHIES = (
    (0.7071067811865476, 0.7071067811865476),
    (0.48296291314469025, 0.836516303737469, 0.22414386804185735, -0.12940952255092145),
    (
        0.3326705529509569,
        0.8068915093133388,
        0.4598775021193313,
        -0.13501102001039084,
        -0.08544127388224149,
        0.035226291882100656,
    ),
    (
        0.23037781330885523,
        0.7148465705525415,
        0.6308807679295904,
        -0.02798376941698385,
        -0.18703481171888114,
        0.030841381835986965,
        0.032883011666982945,
        -0.010597401784997278,
    ),
)
NDB = len(DAUBECHIES)
JACOBI_SWEEPS = 6
STEP_PRIMAL = 0.2
STEP_SPARSE = 0.5
SPARSE_SCALE = 0.5
LANES = 128
STRIP = 32
HALO = 8
MIB = 1 << 20
F32 = jnp.float32
BF16 = jnp.bfloat16


def band_taps(family):
    low = DAUBECHIES[family]
    high = [(-1.0) ** k * low[len(low) - 1 - k] for k in range(len(low))]
    return low, high


def phase_taps(family):
    low, high = band_taps(family)
    offset = len(low) // 2 - 1
    table = {}
    for k in range(len(low)):
        s, odd = divmod(k - offset, 2)
        entry = table.setdefault(s, [0.0, 0.0, 0.0, 0.0])
        entry[odd] = low[k]
        entry[2 + odd] = high[k]
    return table


def column_weight(family, band, coefs, pixels):
    taps = band_taps(family)[band]
    k = pixels[:, None] - 2 * coefs[None, :] + len(taps) // 2 - 1
    inside = (k >= 0) & (k < len(taps))
    return np.where(inside, np.asarray(taps)[np.clip(k, 0, len(taps) - 1)], 0.0)


def column_table(cols):
    half = cols // 2
    pixels = np.concatenate([np.arange(cols), np.arange(-LANES, 0), np.arange(cols, cols + LANES)])
    pairs = [(f, b) for b in range(2) for f in range(NDB)]
    beyond = np.array([-2, -1, half, half + 1])
    parts = [column_weight(f, b, np.arange(half), pixels) for f, b in pairs] + [column_weight(f, b, beyond, pixels) for f, b in pairs]
    table = np.concatenate(parts, 1)
    table = jnp.asarray(np.pad(table, ((0, 0), (0, LANES - 4 * len(pairs)))), F32)
    top = table.astype(BF16)
    return jnp.stack([top, (table - top.astype(F32)).astype(BF16)], 0)


def halves(values):
    top = values.astype(BF16)
    return top, (values - top.astype(F32)).astype(BF16)


def dot3(left, right, dims=((1,), (0,))):
    def dot(one, two):
        return lax.dot_general(one, two, (dims, ((), ())), preferred_element_type=F32)

    return dot(left[0], right[1]) + dot(left[1], right[0]) + dot(left[0], right[0])


def side_by_side(ref, tiles):
    return jnp.concatenate([ref[t] for t in tiles], 1)


def swap_halves(values):
    return pltpu.roll(values, 4, 0)


def sublane_taps(first, second):
    rows = lax.broadcasted_iota(jnp.int32, (8, LANES), 0)
    return jnp.where(rows < 4, F32(first), F32(second))


def strip_taps(pick_first, pick_second, s):
    family = lax.broadcasted_iota(jnp.int32, (8, LANES), 1) // 4 % 4
    total = jnp.zeros((8, LANES), F32)
    for f in range(NDB):
        entry = phase_taps(f).get(s)
        if entry is not None:
            total = jnp.where(family == f, sublane_taps(entry[pick_first], entry[pick_second]), total)
    return total


def row_taps(family, cross, scale):
    table = phase_taps(family)
    return {s: (sublane_taps(e[0] * scale, e[3] * scale), sublane_taps(e[cross[0]] * scale, e[cross[1]] * scale)) for s, e in table.items()}


def strip_row_taps(cross, scale):
    column = lax.broadcasted_iota(jnp.int32, (8, LANES), 1) % 4
    place, facets = lax.axis_index("fcol"), lax.axis_size("fcol")
    kept = jnp.where(column < 2, jnp.where(place > 0, F32(scale), F32(0.0)), jnp.where(place < facets - 1, F32(scale), F32(0.0)))
    return {s: (strip_taps(0, 3, s) * kept, strip_taps(*cross, s) * kept) for s in range(-2, 3)}


def filter_rows(taps, pairs, at):
    direct = crossed = None
    for s, (d, e) in taps.items():
        source = pairs[at(s)]
        direct = d * source if direct is None else direct + d * source
        crossed = e * source if crossed is None else crossed + e * source
    return direct + swap_halves(crossed)


def pack4(items):
    rows = lax.broadcasted_iota(jnp.int32, (8, LANES), 0)

    def merge(a, b, step):
        keep = rows % (2 * step) < step
        return jnp.where(keep, a, pltpu.roll(b, step, 0)) + jnp.where(keep, pltpu.roll(a, 8 - step, 0), b)

    return merge(merge(items[0], items[1], 1), merge(items[2], items[3], 1), 2)


def fill_rows(ext, row, count, start, sources):
    channels = 4
    t = 0
    for ref in sources:
        for u in range(ref.shape[-1] // LANES):
            for c in range(channels):
                value = ref[c, pl.ds(start, count), u * LANES : (u + 1) * LANES]
                ext[t, pl.ds(row * channels + c, count, stride=channels), :] = jnp.maximum(value, 0.0)
            t += 1


def filter_columns(ext, table, cols):
    left = halves(side_by_side(ext, range(ext.shape[0])))
    return dot3(left, [table[0], table[1]])


def coefficients(coef, u_ref, count, strip_item):
    tiles = 2 * NDB + 1
    squares = []
    for tile in range(tiles):
        lanes = slice(tile * LANES, (tile + 1) * LANES)
        taps = strip_row_taps((2, 1), STEP_SPARSE) if tile == tiles - 1 else row_taps(tile % NDB, (2, 1), STEP_SPARSE)
        pairs = [coef[8 * i : 8 * i + 8, lanes] for i in range(count + 4)]
        for j in range(count):
            value = filter_rows(taps, pairs, lambda s: j + 2 + s)
            u_ref[8 * j : 8 * j + 8, lanes] = value
            squares.append(value * value)
    packed = []
    for half in range(2):
        flat = squares[half * NDB * count : (half + 1) * NDB * count]
        packed.append([pack4(flat[g : g + 4]) for g in range(0, len(flat), 4)])
        strip = squares[2 * NDB * count + half * (count // 2) : 2 * NDB * count + (half + 1) * (count // 2)]
        items = [jnp.zeros((8, LANES), F32)] * strip_item
        for g in range(0, len(strip), 4):
            total = strip[g]
            for k in range(1, len(strip[g : g + 4])):
                total = total + pltpu.roll(strip[g + k], STRIP * k, 1)
            items.append(total)
        items += [jnp.zeros((8, LANES), F32)] * (4 - len(items))
        packed[half].append(pack4(items))
    return packed


def store_halves(packed, keep, send, base=0):
    y = lax.axis_index("chan") % 2
    for i, (a, b) in enumerate(zip(*packed)):
        keep[base + 8 * i : base + 8 * i + 8, :] = jnp.where(y == 0, a, b)
        send[base + 8 * i : base + 8 * i + 8, :] = jnp.where(y == 0, b, a)


def inner_kernel(own, *refs):
    *beside, table, u_ref, keep, send, ext, coef = refs
    channels, rows, cols = own.shape
    x = lax.axis_index("frow")
    edge = jnp.zeros((ext.shape[0], 4 * channels, LANES), F32)
    ext[:, pl.ds(pl.multiple_of(x * rows * channels, 16), 4 * channels), :] = edge
    fill_rows(ext, 4 * (1 - x), rows, 0, [own, *beside])
    coef[...] = filter_columns(ext, table, cols)
    packed = coefficients(coef, u_ref, rows // 2 - 2, 0)
    for half in range(2):
        for r in range(half * rows // 2, (half + 1) * rows // 2, 8):
            for t in range(cols // LANES):
                total = None
                for c in range(channels):
                    value = STEP_SPARSE * jnp.maximum(own[c, r : r + 8, t * LANES : (t + 1) * LANES], 0.0)
                    total = value * value if total is None else total + value * value
                packed[half].append(total)
    store_halves(packed, keep, send)


def border_kernel(sides, own, above, keep_inner, send_inner, *refs):
    beside, corner = refs[:sides], refs[sides : 2 * sides]
    table, u_ref, keep, send, ext, coef = refs[2 * sides :]
    rows, cols = own.shape[1:]
    x, y = lax.axis_index("frow"), lax.axis_index("chan") % 2
    places = Places(rows, cols)
    fill_rows(ext, HALO * x, HALO, (1 - x) * (rows - HALO), [own, *beside])
    fill_rows(ext, HALO * (1 - x), HALO, 0, [above, *corner])
    coef[...] = filter_columns(ext, table, cols)
    packed = coefficients(coef, u_ref, 4, 2)
    strips = [part.pop() for part in packed]
    store_halves(packed, keep, send, places.border)
    keep[: places.border, :] = keep_inner[...]
    send[: places.border, :] = send_inner[...]
    at = slice(places.strip, places.strip + 8)
    keep[at, :] = keep_inner[at, :] + jnp.where(y == 0, *strips)
    send[at, :] = send_inner[at, :] + jnp.where(y == 0, *strips[::-1])


def pairing_rounds(order):
    players = list(range(order))
    rounds = []
    for _ in range(order - 1):
        rounds.append([(min(a, b), max(a, b)) for a, b in zip(players[: order // 2], players[: order // 2 - 1 : -1])])
        players = [players[0]] + [players[-1]] + players[1:-1]
    return rounds


def down(values):
    for step in (4, 2, 1):
        values = values + pltpu.roll(values, step, 0)
    return values


def nuclear_kernel(limit, own, other, out, group, mix):
    channels, rows, cols = own.shape
    order = 2 * channels
    y = lax.axis_index("chan") % 2
    for c in range(channels):
        group[y * channels + c] = jnp.maximum(own[c], 0.0)
        group[(1 - y) * channels + c] = jnp.maximum(other[c], 0.0)
    blocks = [(slice(r, r + 8), slice(t, t + LANES)) for r in range(0, rows, 8) for t in range(0, cols, LANES)]
    partial = {}
    for at in blocks:
        held = [group[(c, *at)] for c in range(order)]
        for i in range(order):
            for j in range(i + 1):
                term = held[i] * held[j]
                partial[i, j] = partial[i, j] + term if (i, j) in partial else term
    row_sum = {key: jnp.sum(value, axis=0, keepdims=True) for key, value in partial.items()}
    sub = lax.broadcasted_iota(jnp.int32, (order, LANES), 0)
    turned, vectors, diag = [], [], []
    for j in range(order):
        stacked = jnp.concatenate([row_sum[max(i, j), min(i, j)] for i in range(order)], 0)
        column = jnp.broadcast_to(jnp.sum(stacked, axis=1, keepdims=True), (order, LANES))
        turned.append(column)
        unit = jnp.where(sub == j, F32(1.0), F32(0.0))
        vectors.append(unit)
        diag.append(down(column * unit))

    rounds = pairing_rounds(order)

    def sweep(_, state):
        turned, vectors, diag = (list(part) for part in state)
        for pairs in rounds:
            for p, q in pairs:
                coupling = down(vectors[p] * turned[q])
                spread = diag[q] - diag[p]
                square = spread * spread + 4.0 * coupling * coupling
                positive = square > 0.0
                inverse = jnp.where(positive, lax.rsqrt(jnp.where(positive, square, 1.0)), 0.0)
                cosine2 = jnp.where(positive, 0.5 + 0.5 * jnp.abs(spread) * inverse, 1.0)
                other = lax.rsqrt(cosine2)
                c = cosine2 * other
                s = jnp.where(spread >= 0.0, coupling, -coupling) * inverse * other
                shift = s * other * coupling
                diag[p], diag[q] = diag[p] - shift, diag[q] + shift
                turned[p], turned[q] = c * turned[p] - s * turned[q], s * turned[p] + c * turned[q]
                vectors[p], vectors[q] = c * vectors[p] - s * vectors[q], s * vectors[p] + c * vectors[q]
        return tuple(turned), tuple(vectors), tuple(diag)

    turned, vectors, _ = lax.fori_loop(0, JACOBI_SWEEPS, sweep, (tuple(turned), tuple(vectors), tuple(diag)))
    weighted = []
    for j in range(order):
        value = down(vectors[j] * turned[j])
        weighted.append(vectors[j] * (limit / jnp.maximum(jnp.sqrt(jnp.maximum(value, 0.0)), limit)))
    for k in range(order):
        total = None
        for j in range(order):
            term = weighted[j] * jnp.broadcast_to(vectors[j][k : k + 1, :], (order, LANES))
            total = term if total is None else total + term
        mix[k] = total
    for i in range(channels):
        row = [jnp.broadcast_to(mix[k, pl.ds(y * channels + i, 1), :], (order, LANES)) for k in range(order)]
        for at in blocks:
            total = None
            for k in range(order):
                term = row[k] * group[(k, *at)]
                total = term if total is None else total + term
            out[(i, *at)] = total


def scales(limit, norms):
    return limit * lax.rsqrt(jnp.maximum(norms, limit * limit))


def widen(scale, at, item):
    sub = lax.broadcasted_iota(jnp.int32, (8, LANES), 0)
    first = jnp.broadcast_to(scale[at + item : at + item + 1, :], (8, LANES))
    second = jnp.broadcast_to(scale[at + 4 + item : at + 5 + item, :], (8, LANES))
    return jnp.where(sub < 4, first, second)


def spread_rows(inner, border, taps, spread, lanes):
    x = lax.axis_index("frow")
    empty = jnp.zeros((8, LANES), F32)
    count = len(inner)
    upper = [empty, empty, *inner, *border]
    lower = [*border, *inner, empty, empty]
    padded = [jnp.where(x == 0, a, b) for a, b in zip(upper, lower)]
    for i in range(count + 2):
        spread[8 * i : 8 * i + 8, lanes] = filter_rows(taps, padded, lambda s: i + 2 - s)


class Places:
    def __init__(self, rows, cols):
        self.inner = rows // 2 - 2
        self.strip = 2 * NDB * self.inner
        self.dirac = self.strip + 8
        self.border = self.dirac + rows * cols // LANES // 2
        self.all = self.border + 2 * NDB * 4


def half_duals(places, half, scale, u_inner, u_border, spread):
    for family in range(NDB):
        if isinstance(half, int):
            lanes = slice((half * NDB + family) * LANES, (half * NDB + family + 1) * LANES)
        else:
            lanes = pl.ds(pl.multiple_of((half * NDB + family) * LANES, LANES), LANES)
        duals = []
        for ref, base, count in ((u_inner, 0, places.inner), (u_border, places.border, 4)):
            items = [(base + 8 * ((family * count + j) // 4), (family * count + j) % 4) for j in range(count)]
            duals.append([ref[8 * j : 8 * j + 8, lanes] * widen(scale, *items[j]) for j in range(count)])
        spread_rows(*duals, row_taps(family, (1, 2), 1.0), spread, slice(family * LANES, (family + 1) * LANES))


def first_kernel(limit, raw, density, nuclear, u_inner, u_border, mine, table, step, spread, scale):
    channels, rows, cols = raw.shape
    y = lax.axis_index("chan") % 2
    scale[...] = scales(limit, mine[...])
    half_duals(Places(rows, cols), y, scale, u_inner, u_border, spread)
    lanes = pl.ds(pl.multiple_of(y * NDB * LANES, NDB * LANES), NDB * LANES)
    result = dot3(halves(spread[...]), [table[i, :cols, lanes] for i in range(2)], ((1,), (1,)))
    for t in range(cols // LANES):
        step[cols // LANES + t] = result[:, t * LANES : (t + 1) * LANES]
    for c in range(channels):
        for t in range(cols // LANES):
            lanes = slice(t * LANES, (t + 1) * LANES)
            estimate = jnp.maximum(raw[c, :, lanes], 0.0)
            step[t, c * rows : (c + 1) * rows, :] = density[c, :, lanes] * estimate - raw[c, :, lanes] + nuclear[c, :, lanes]


def second_kernel(limit, raw, step, u_inner, u_border, mine, theirs, table, out, spread, image, scale):
    channels, rows, cols = raw.shape
    y = lax.axis_index("chan") % 2
    places = Places(rows, cols)
    scale[y] = scales(limit, mine[...])
    scale[1 - y] = scales(limit, theirs[...])
    half_duals(places, 1 - y, scale.at[1 - y], u_inner, u_border, spread)
    main = 2 * NDB * LANES
    duals = []
    for ref, item, count in ((u_inner, 0, places.inner), (u_border, 2, 4)):
        rolled = []
        for j in range(count):
            half, k = divmod(j, count // 2)
            factor = widen(scale.at[half], places.strip, item + k // 4)
            factor = factor if k % 4 == 0 else pltpu.roll(factor, LANES - STRIP * (k % 4), 1)
            rolled.append(ref[8 * j : 8 * j + 8, main:] * factor)
        duals.append(rolled)
    spread_rows(*duals, strip_row_taps((1, 2), 1.0), spread, slice(NDB * LANES, (NDB + 1) * LANES))
    lanes = pl.ds(pl.multiple_of((1 - y) * NDB * LANES, NDB * LANES), NDB * LANES)
    left = halves(spread[...])
    right = [jnp.concatenate([table[i, :cols, lanes], table[i, :cols, main:]], 1) for i in range(2)]
    result = dot3(left, right, ((1,), (1,)))
    for t in range(cols // LANES):
        image[t] = result[:, t * LANES : (t + 1) * LANES] + step[cols // LANES + t]
    for c in range(channels):
        for r in range(0, rows, 8):
            for t in range(cols // LANES):
                lanes = slice(t * LANES, (t + 1) * LANES)
                half, inside = divmod(r, rows // 2)
                at = places.dirac + 8 * (inside // 8 * (cols // LANES) + t)
                estimate = jnp.maximum(raw[c, r : r + 8, lanes], 0.0)
                dual = STEP_SPARSE * estimate * scale[half, at : at + 8, :]
                synthesis = dual + image[t, pl.ds(r * channels + c, 8, stride=channels), :]
                total = step[t, c * rows + r : c * rows + r + 8, :] + synthesis
                out[c, r : r + 8, lanes] = jnp.maximum(estimate - STEP_PRIMAL * total, 0.0)


def sent_tiles(cols):
    if lax.axis_size("fcol") == 2:
        return [pl.ds(pl.multiple_of((1 - lax.axis_index("fcol")) * (cols - LANES), LANES), LANES)]
    return [slice(cols - LANES, cols), slice(0, LANES)]


def edges_kernel(sides, dirty, own, edge, *refs):
    wings, corners = refs[:sides], refs[sides : 2 * sides]
    rows, cols = dirty.shape[1:]
    start = pl.ds(pl.multiple_of((1 - lax.axis_index("frow")) * (rows - HALO), HALO), HALO)
    own[...] = dirty[...]
    edge[...] = dirty[:, start, :]
    for wing, corner, lanes in zip(wings, corners, sent_tiles(cols)):
        wing[...] = dirty[:, :, lanes]
        corner[...] = dirty[:, start, lanes]


def load_kernel(sides, table, near, sems):
    if sides == 1:
        cols = table.shape[1] - 2 * LANES
        beyond = pl.multiple_of(cols + (1 - lax.axis_index("fcol")) * LANES, LANES)
        loads = [pltpu.make_async_copy(table.at[:, :cols, :], near.at[:, :cols, :], sems.at[0])]
        loads.append(pltpu.make_async_copy(table.at[:, pl.ds(beyond, LANES), :], near.at[:, cols:, :], sems.at[1]))
    else:
        loads = [pltpu.make_async_copy(table, near, sems.at[0])]
    for load in loads:
        load.start()
    for load in loads:
        load.wait()


def add_kernel(one, two, *refs):
    refs[-1][...] = one[...] + two[...]


def add_and_copy_kernel(one, two, image, total, again):
    total[...] = one[...] + two[...]
    again[...] = image[...]


def exchange(values, axis, bit):
    count = lax.axis_size(axis)
    return lax.ppermute(values, axis, [(i, i ^ bit) for i in range(count)])


def vmem(count):
    return [pl.BlockSpec(memory_space=pltpu.VMEM)] * count


def call(kernel, name, shapes, operands, scratch=(), limit=16, later=()):
    many = [jax.ShapeDtypeStruct(shape, F32) if isinstance(shape, tuple) else shape for shape in shapes]
    results = pl.pallas_call(
        kernel,
        name=name,
        out_shape=many,
        in_specs=vmem(len(operands)) + [pl.BlockSpec(memory_space=pl.ANY)] * len(later),
        out_specs=vmem(len(many)),
        scratch_shapes=[pltpu.VMEM(shape, F32) for shape in scratch],
        compiler_params=pltpu.CompilerParams(vmem_limit_bytes=limit * MIB),
    )(*operands, *later)
    return results if len(results) > 1 else results[0]


def to_neighbours(wings, other=None):
    facets = lax.axis_size("fcol")
    axes, flips = ("fcol", [0]) if other is None else (("frow", "fcol"), [0, 1])

    def pairs(moves):
        if other is None:
            return moves
        return [(f * facets + i, (1 - f) * facets + j) for f in flips for i, j in moves]

    if facets == 2:
        return [lax.ppermute(wings[0], axes, pairs([(0, 1), (1, 0)]))]
    return [
        lax.ppermute(wings[0], axes, pairs([(i, i + 1) for i in range(facets - 1)])),
        lax.ppermute(wings[1], axes, pairs([(i + 1, i) for i in range(facets - 1)])),
    ]


def on_device(dirty_image, density):
    channels, rows, cols = dirty_image.shape
    facets, chans = lax.axis_size("fcol"), lax.axis_size("chan")
    nuclear_limit = math.sqrt(rows * cols)
    sparse_limit = SPARSE_SCALE * math.sqrt(channels * chans)
    table = column_table(cols)
    sides = 1 if facets == 2 else 2
    places, tiles = Places(rows, cols), 2 * NDB + 1
    lane_tiles = cols // LANES + sides

    own, edge, *around = call(
        lambda *refs: edges_kernel(sides, *refs),
        "edges",
        [dirty_image.shape, (channels, HALO, cols)] + [(channels, rows, LANES)] * sides + [(channels, HALO, LANES)] * sides,
        [dirty_image],
    )
    near = pl.pallas_call(
        lambda *refs: load_kernel(sides, *refs),
        name="load",
        out_shape=jax.ShapeDtypeStruct((2, cols + sides * LANES, tiles * LANES), BF16),
        in_specs=[pl.BlockSpec(memory_space=pltpu.HBM)],
        out_specs=vmem(1)[0],
        scratch_shapes=[pltpu.SemaphoreType.DMA((2,))],
        compiler_params=pltpu.CompilerParams(vmem_limit_bytes=16 * MIB),
    )(table)
    beside = to_neighbours(around[:sides])
    above = exchange(edge, "frow", 1)
    corner = to_neighbours(around[sides:], "frow")
    u_inner, inner_keep, inner_send = call(
        inner_kernel,
        "inner",
        [(8 * places.inner, tiles * LANES), (places.border, LANES), (places.border, LANES)],
        [own, *beside, near],
        [(lane_tiles, 8 * (places.inner + 4), LANES), (8 * (places.inner + 4), tiles * LANES)],
        24,
    )
    u_border, keep, send = call(
        lambda *refs: border_kernel(sides, *refs),
        "border",
        [(8 * 4, tiles * LANES), (places.all, LANES), (places.all, LANES)],
        [own, above, inner_keep, inner_send, *beside, *corner, near],
        [(lane_tiles, 8 * 8, LANES), (8 * 8, tiles * LANES)],
        24,
    )
    received = exchange(send, "chan", 1)
    total, again = call(add_and_copy_kernel, "add", [(places.all, LANES), dirty_image.shape], [keep, received, own])
    other = exchange(again, "chan", 1)
    nuclear = call(
        lambda *refs: nuclear_kernel(nuclear_limit, *refs),
        "nuclear",
        [dirty_image.shape],
        [own, other],
        [(2 * channels, rows, cols), (2 * channels, 2 * channels, LANES)],
    )
    bit = 2
    while bit < chans:
        received = exchange(total, "chan", bit)
        total = call(add_kernel, "add", [(places.all, LANES)], [total, received], later=[other if 2 * bit < chans else nuclear])
        bit *= 2
    theirs = exchange(total, "chan", 1)
    step = call(
        lambda *refs: first_kernel(sparse_limit, *refs),
        "first",
        [(2 * cols // LANES, channels * rows, LANES)],
        [own, density, nuclear, u_inner, u_border, total, near],
        [(4 * rows, NDB * LANES), (places.all, LANES)],
        24,
    )
    return call(
        lambda *refs: second_kernel(sparse_limit, *refs),
        "second",
        [dirty_image.shape],
        [own, step, u_inner, u_border, total, theirs, near],
        [(4 * rows, (NDB + 1) * LANES), (cols // LANES, 4 * rows, LANES), (2, places.all, LANES)],
        24,
    )


def solution(mesh):
    return jax.shard_map(
        on_device,
        mesh=mesh,
        in_specs=(P("chan", "frow", "fcol"), P("chan", "frow", "fcol")),
        out_specs=P("chan", "frow", "fcol"),
        check_vma=False,
    )
```

time: 35.8 us -> 30.8 us (0.86)
  local copies, waits for them, and re-layouts: 5.95 us -> 2.57 us
  starting transfers between devices: 13.2 us -> 11.3 us
  Pallas kernels: 4.32 us -> 5.55 us
  other arithmetic: 0.96 us -> 0 us
    unnamed x24 -> x6, local copies, waits for them, and re-layouts: 5.14 us -> 2.57 us
    ppermute x8 -> x6, starting transfers between devices: 13.2 us -> 10.7 us  [exchange(): return lax.ppermute(values, axis, [(i, i ^ bit) for i in range(count)])]
    pallas_call x3 -> x10, Pallas kernels: 4.32 us -> 5.55 us  [the longest x9 5.3 us: call(): pl.pallas_call(kernel, name=name, out_shape=many, in_specs=vmem(len(opera...]
    select_n x2 -> x0, other arithmetic: 0.89 us -> none  [beside_columns(): jnp.where(lax.axis_index('fcol') == 0, last, first)]
    dynamic_slice x1 -> x0, local copies, waits for them, and re-layouts: 0.8 us -> none  [on_device(): lax.dynamic_slice_in_dim(dirty_image, (1 - x) * (rows - HALO), HALO, 1)]
    ppermute x0 -> x2, starting transfers between devices: none -> 0.59 us  [to_neighbours(): return [lax.ppermute(wings[0], axes, pairs([(0, 1), (1, 0)]))]]
    ppermute x8 -> x6, waiting for transfers between devices: 10.9 us -> 11 us  [exchange(): return lax.ppermute(values, axis, [(i, i ^ bit) for i in range(count)])]
  transfers between devices with their start and end apart: 8 -> 8, of which waited for: 6 -> 5; matrix products, arithmetic and copies ran while one was open for 3% -> 0% of each run, Pallas kernels for 5% -> 12%
where the time goes in v2:
time: 30.8 us; the launch traced here: 30.6 us
  starting transfers between devices  11.3 us (37%)
  waiting for transfers between devices  11.1 us (36%)
  Pallas kernels  5.55 us (18%)
  local copies, waits for them, and re-layouts  2.57 us (8%)
    ppermute x6, waiting for transfers between devices, exchange(): return lax.ppermute(values, axis, [(i, i ^ bit) for i in range(count)])  11 us
    ppermute x6, starting transfers between devices, exchange(): return lax.ppermute(values, axis, [(i, i ^ bit) for i in range(count)])  10.7 us
    pallas_call x9, Pallas kernels, call(): pl.pallas_call(kernel, name=name, out_shape=many, in_specs=vmem(len(opera...  5.3 us
    unnamed x6, local copies, waits for them, and re-layouts  2.57 us
  transfers between devices with their start and end apart: 8, of which 5 were waited for; matrix products, arithmetic and copies ran while one was open for 0% of the time, Pallas kernels for 12%

profile of v2, /device:TPU:0, one launch (start us, length us, event | category | flops | bytes accessed | tf_op | source)
XLA Modules:
  0.0 30.6 jit_solution(3216233700023739235)
XLA Ops:
  0.0 0.9 %copy-done.2 = f32[4,32,256]{2,1,0:T(8,128)S(1)} copy-done((f32[4,32,256]{2,1,0:T(8,128)S(1)}, f32[4,32,256]{2,1,0:T(8,128)}, u32[]{:S(2)}) %copy-start.2) | copy-done | bytes 131096
  0.9 0.5 %collective-permute-start.1 = (f32[4,32,128]{2,1,0:T(8,128)S(1)}, f32[4,32,128]{2,1,0:T(8,128)S(1)}, u32[]{:S(2)}, u32[]{:S(2)}) collective-permute-start(f32[4,32,128]{2,1,0:T(8,128)S(1)} %get-tuple-element.19), channel_id=1, source_target_pairs={{0,8},{8,0},{1,9},{9,1},{2,10},{10,2},{3,11},{11,3},{4,12},{12,4},... | collective-permute-start | bytes 196616 | tf_op jit(solution)/shard_map/ppermute | solution.py:491
  1.4 2.6 %collective-permute-start = (f32[4,8,256]{2,1,0:T(8,128)S(1)}, f32[4,8,256]{2,1,0:T(8,128)S(1)}, u32[]{:S(2)}, u32[]{:S(2)}) collective-permute-start(f32[4,8,256]{2,1,0:T(8,128)S(1)} %get-tuple-element.18), channel_id=1, source_target_pairs={{0,16},{16,0},{1,17},{17,1},{2,18},{18,2},{3,19},{19,3},{4,20},{20... | collective-permute-start | bytes 98312 | tf_op jit(solution)/shard_map/ppermute | solution.py:460
  4.0 0.1 collective-permute-start.2
  4.1 1.7 %copy-done = bf16[2,512,1152]{2,1,0:T(8,128)(2,1)S(1)} copy-done((bf16[2,512,1152]{2,1,0:T(8,128)(2,1)S(1)}, bf16[2,512,1152]{2,1,0:T(8,128)(2,1)}, u32[]{:S(2)}) %copy-start) | copy-done | bytes 2359320
  5.7 0.3 load.1.refs_1_.refs_6_
  6.0 0.0 collective-permute-done.1.refs_0_.refs_4_
  6.0 0.0 copy-start.1
  6.0 1.0 %inner.1 = (f32[112,1152]{1,0:T(8,128)S(1)}, f32[152,128]{1,0:T(8,128)S(1)}, f32[152,128]{1,0:T(8,128)S(1)}) custom-call(f32[4,32,256]{2,1,0:T(8,128)S(1)} %get-tuple-element.17.own.refs_0_.image, f32[4,32,128]{2,1,0:T(8,128)S(1)} %collective-permute-done.1.refs_0_.refs_4_, bf16[2,384,1152]{2,1,0:T(8,128)(2,1)S(1)} %load.1.refs_1_.refs_6_), custom_call_target="tpu_custom_call" | custom-call | tf_op jit(solution)/shard_map/inner/pallas_call | solution.py:469
  7.0 0.1 collective-permute-done.2.refs_5_
  7.2 0.0 collective-permute-done.refs_1_
  7.2 0.7 %border.1 = (f32[32,1152]{1,0:T(8,128)S(1)}, f32[184,128]{1,0:T(8,128)S(1)}, f32[184,128]{1,0:T(8,128)S(1)}) custom-call(f32[4,32,256]{2,1,0:T(8,128)S(1)} %get-tuple-element.17.own.refs_0_.image, f32[4,8,256]{2,1,0:T(8,128)S(1)} %collective-permute-done.refs_1_, f32[152,128]{1,0:T(8,128)S(1)} %get-tuple-element.20.refs_2_, ...), custom_call_target="tpu_custom_call" | custom-call | tf_op jit(solution)/shard_map/border/pallas_call | solution.py:469
  7.9 1.7 %collective-permute-start.3 = (f32[184,128]{1,0:T(8,128)S(1)}, f32[184,128]{1,0:T(8,128)S(1)}, u32[]{:S(2)}, u32[]{:S(2)}) collective-permute-start(f32[184,128]{1,0:T(8,128)S(1)} %get-tuple-element.24), channel_id=1, source_target_pairs={{0,1},{1,0},{2,3},{3,2},{4,5},{5,4},{6,7},{7,6},{8,9},{9,8},{10,11... | collective-permute-start | bytes 282632 | tf_op jit(solution)/shard_map/ppermute | solution.py:460
  9.6 3.2 %collective-permute-done.3.two = f32[184,128]{1,0:T(8,128)S(1)} collective-permute-done((f32[184,128]{1,0:T(8,128)S(1)}, f32[184,128]{1,0:T(8,128)S(1)}, u32[]{:S(2)}, u32[]{:S(2)}) %collective-permute-start.3) | collective-permute-done | bytes 94240 | tf_op jit(solution)/shard_map/ppermute | solution.py:460
  12.8 1.8 %collective-permute-start.4 = (f32[4,32,256]{2,1,0:T(8,128)S(1)}, f32[4,32,256]{2,1,0:T(8,128)S(1)}, u32[]{:S(2)}, u32[]{:S(2)}) collective-permute-start(f32[4,32,256]{2,1,0:T(8,128)S(1)} %get-tuple-element.25), channel_id=1, source_target_pairs={{0,1},{1,0},{2,3},{3,2},{4,5},{5,4},{6,7},{7,6},{8,9},{9,8},{10,11... | collective-permute-start | bytes 393224 | tf_op jit(solution)/shard_map/ppermute | solution.py:460
  14.6 1.6 %collective-permute-start.5 = (f32[184,128]{1,0:T(8,128)S(1)}, f32[184,128]{1,0:T(8,128)S(1)}, u32[]{:S(2)}, u32[]{:S(2)}) collective-permute-start(f32[184,128]{1,0:T(8,128)S(1)} %get-tuple-element.28.one), channel_id=1, source_target_pairs={{0,2},{1,3},{2,0},{3,1},{4,6},{5,7},{6,4},{7,5},{8,10},{9,11},{10,... | collective-permute-start | bytes 282632 | tf_op jit(solution)/shard_map/ppermute | solution.py:460
  16.2 3.0 %collective-permute-done.5.two = f32[184,128]{1,0:T(8,128)S(1)} collective-permute-done((f32[184,128]{1,0:T(8,128)S(1)}, f32[184,128]{1,0:T(8,128)S(1)}, u32[]{:S(2)}, u32[]{:S(2)}) %collective-permute-start.5) | collective-permute-done | bytes 94240 | tf_op jit(solution)/shard_map/ppermute | solution.py:460
  19.2 2.6 %collective-permute-start.6 = (f32[184,128]{1,0:T(8,128)S(1)}, f32[184,128]{1,0:T(8,128)S(1)}, u32[]{:S(2)}, u32[]{:S(2)}) collective-permute-start(f32[184,128]{1,0:T(8,128)S(1)} %add.4.one), channel_id=1, source_target_pairs={{0,4},{1,5},{2,6},{3,7},{4,0},{5,1},{6,2},{7,3},{8,12},{9,13},{10,... | collective-permute-start | bytes 282632 | tf_op jit(solution)/shard_map/ppermute | solution.py:460
  21.9 1.8 %nuclear.1.refs_0_.refs_2_ = f32[4,32,256]{2,1,0:T(8,128)S(1)} custom-call(f32[4,32,256]{2,1,0:T(8,128)S(1)} %get-tuple-element.17.own.refs_0_.image, f32[4,32,256]{2,1,0:T(8,128)S(1)} %collective-permute-done.4.refs_1_.refs_0_), custom_call_target="tpu_custom_call" | custom-call | tf_op jit(solution)/shard_map/nuclear/pallas_call | solution.py:469
  23.7 1.1 %collective-permute-done.6.two = f32[184,128]{1,0:T(8,128)S(1)} collective-permute-done((f32[184,128]{1,0:T(8,128)S(1)}, f32[184,128]{1,0:T(8,128)S(1)}, u32[]{:S(2)}, u32[]{:S(2)}) %collective-permute-start.6) | collective-permute-done | bytes 94240 | tf_op jit(solution)/shard_map/ppermute | solution.py:460
  24.8 0.5 %collective-permute-start.7 = (f32[184,128]{1,0:T(8,128)S(1)}, f32[184,128]{1,0:T(8,128)S(1)}, u32[]{:S(2)}, u32[]{:S(2)}) collective-permute-start(f32[184,128]{1,0:T(8,128)S(1)} %add.5.refs_5_.refs_4_), channel_id=1, source_target_pairs={{0,1},{1,0},{2,3},{3,2},{4,5},{5,4},{6,7},{7,6},{8,9},{9,8},{10,11... | collective-permute-start | bytes 282632 | tf_op jit(solution)/shard_map/ppermute | solution.py:460
  25.2 0.5 %first.1.refs_1_ = f32[4,128,128]{2,1,0:T(8,128)S(1)} custom-call(f32[4,32,256]{2,1,0:T(8,128)S(1)} %get-tuple-element.17.own.refs_0_.image, f32[4,32,256]{2,1,0:T(8,128)S(1)} %copy-done.1, f32[4,32,256]{2,1,0:T(8,128)S(1)} %nuclear.1.refs_0_.refs_2_, f32[112,1152]{1,0:T(8,128)S(1)} %get-tuple-element.26.refs_3_.refs_2_, ...), custom_call_target="tpu_custom_call" | custom-call | tf_op jit(solution)/shard_map/first/pallas_call | solution.py:469
  25.7 3.7 %collective-permute-done.7.refs_5_ = f32[184,128]{1,0:T(8,128)S(1)} collective-permute-done((f32[184,128]{1,0:T(8,128)S(1)}, f32[184,128]{1,0:T(8,128)S(1)}, u32[]{:S(2)}, u32[]{:S(2)}) %collective-permute-start.7) | collective-permute-done | bytes 94240 | tf_op jit(solution)/shard_map/ppermute | solution.py:460
  29.4 1.2 %second.1 = f32[4,32,256]{2,1,0:T(8,128)} custom-call(f32[4,32,256]{2,1,0:T(8,128)S(1)} %get-tuple-element.17.own.refs_0_.image, f32[4,128,128]{2,1,0:T(8,128)S(1)} %first.1.refs_1_, f32[112,1152]{1,0:T(8,128)S(1)} %get-tuple-element.26.refs_3_.refs_2_, f32[32,1152]{1,0:T(8,128)S(1)} %get-tuple-element.27.refs_4_.refs_3_, ...), custom_call_target="tpu_custom_call" | custom-call | tf_op jit(solution)/shard_map/second/pallas_call | solution.py:469
  (8 shorter events, 0.1 us)
Async XLA Ops:
  0.0 0.9 %copy-start.2 = (f32[4,32,256]{2,1,0:T(8,128)S(1)}, f32[4,32,256]{2,1,0:T(8,128)}, u32[]{:S(2)}) copy-start(f32[4,32,256]{2,1,0:T(8,128)} %refs_0_.1) | copy-start | bytes 393220
  0.9 5.1 %collective-permute-start.1 = (f32[4,32,128]{2,1,0:T(8,128)S(1)}, f32[4,32,128]{2,1,0:T(8,128)S(1)}, u32[]{:S(2)}, u32[]{:S(2)}) collective-permute-start(f32[4,32,128]{2,1,0:T(8,128)S(1)} %get-tuple-element.19), channel_id=1, source_target_pairs={{0,8},{8,0},{1,9},{9,1},{2,10},{10,2},{3,11},{11,3},{4,12},{12,4},... | collective-permute-start | bytes 196616 | tf_op jit(solution)/shard_map/ppermute | solution.py:491
  1.4 5.7 %collective-permute-start = (f32[4,8,256]{2,1,0:T(8,128)S(1)}, f32[4,8,256]{2,1,0:T(8,128)S(1)}, u32[]{:S(2)}, u32[]{:S(2)}) collective-permute-start(f32[4,8,256]{2,1,0:T(8,128)S(1)} %get-tuple-element.18), channel_id=1, source_target_pairs={{0,16},{16,0},{1,17},{17,1},{2,18},{18,2},{3,19},{19,3},{4,20},{20... | collective-permute-start | bytes 98312 | tf_op jit(solution)/shard_map/ppermute | solution.py:460
  4.0 3.2 %collective-permute-start.2 = (f32[4,8,128]{2,1,0:T(8,128)S(1)}, f32[4,8,128]{2,1,0:T(8,128)S(1)}, u32[]{:S(2)}, u32[]{:S(2)}) collective-permute-start(f32[4,8,128]{2,1,0:T(8,128)S(1)} %get-tuple-element.22), channel_id=1, source_target_pairs={{0,24},{8,16},{16,8},{24,0},{1,25},{9,17},{17,9},{25,1},{2,26},{10... | collective-permute-start | bytes 49160 | tf_op jit(solution)/shard_map/ppermute | solution.py:491
  4.1 1.7 %copy-start = (bf16[2,512,1152]{2,1,0:T(8,128)(2,1)S(1)}, bf16[2,512,1152]{2,1,0:T(8,128)(2,1)}, u32[]{:S(2)}) copy-start(bf16[2,512,1152]{2,1,0:T(8,128)(2,1)} %constant.11.refs_0_) | copy-start | bytes 7077892
  6.0 19.2 %copy-start.1 = (f32[4,32,256]{2,1,0:T(8,128)S(1)}, f32[4,32,256]{2,1,0:T(8,128)}, u32[]{:S(2)}) copy-start(f32[4,32,256]{2,1,0:T(8,128)} %refs_1_.1) | copy-start | bytes 393220
  7.9 4.9 %collective-permute-start.3 = (f32[184,128]{1,0:T(8,128)S(1)}, f32[184,128]{1,0:T(8,128)S(1)}, u32[]{:S(2)}, u32[]{:S(2)}) collective-permute-start(f32[184,128]{1,0:T(8,128)S(1)} %get-tuple-element.24), channel_id=1, source_target_pairs={{0,1},{1,0},{2,3},{3,2},{4,5},{5,4},{6,7},{7,6},{8,9},{9,8},{10,11... | collective-permute-start | bytes 282632 | tf_op jit(solution)/shard_map/ppermute | solution.py:460
  12.8 6.4 %collective-permute-start.4 = (f32[4,32,256]{2,1,0:T(8,128)S(1)}, f32[4,32,256]{2,1,0:T(8,128)S(1)}, u32[]{:S(2)}, u32[]{:S(2)}) collective-permute-start(f32[4,32,256]{2,1,0:T(8,128)S(1)} %get-tuple-element.25), channel_id=1, source_target_pairs={{0,1},{1,0},{2,3},{3,2},{4,5},{5,4},{6,7},{7,6},{8,9},{9,8},{10,11... | collective-permute-start | bytes 393224 | tf_op jit(solution)/shard_map/ppermute | solution.py:460
  14.6 4.6 %collective-permute-start.5 = (f32[184,128]{1,0:T(8,128)S(1)}, f32[184,128]{1,0:T(8,128)S(1)}, u32[]{:S(2)}, u32[]{:S(2)}) collective-permute-start(f32[184,128]{1,0:T(8,128)S(1)} %get-tuple-element.28.one), channel_id=1, source_target_pairs={{0,2},{1,3},{2,0},{3,1},{4,6},{5,7},{6,4},{7,5},{8,10},{9,11},{10,... | collective-permute-start | bytes 282632 | tf_op jit(solution)/shard_map/ppermute | solution.py:460
  19.2 5.5 %collective-permute-start.6 = (f32[184,128]{1,0:T(8,128)S(1)}, f32[184,128]{1,0:T(8,128)S(1)}, u32[]{:S(2)}, u32[]{:S(2)}) collective-permute-start(f32[184,128]{1,0:T(8,128)S(1)} %add.4.one), channel_id=1, source_target_pairs={{0,4},{1,5},{2,6},{3,7},{4,0},{5,1},{6,2},{7,3},{8,12},{9,13},{10,... | collective-permute-start | bytes 282632 | tf_op jit(solution)/shard_map/ppermute | solution.py:460
  24.8 4.6 %collective-permute-start.7 = (f32[184,128]{1,0:T(8,128)S(1)}, f32[184,128]{1,0:T(8,128)S(1)}, u32[]{:S(2)}, u32[]{:S(2)}) collective-permute-start(f32[184,128]{1,0:T(8,128)S(1)} %add.5.refs_5_.refs_4_), channel_id=1, source_target_pairs={{0,1},{1,0},{2,3},{3,2},{4,5},{5,4},{6,7},{7,6},{8,9},{9,8},{10,11... | collective-permute-start | bytes 282632 | tf_op jit(solution)/shard_map/ppermute | solution.py:460

commit v3 on v2

--- a/solution.py
+++ b/solution.py
@@ -37,6 +37,7 @@
 SPARSE_SCALE = 0.5
 LANES = 128
 STRIP = 32
+NEAR = 16
 HALO = 8
 MIB = 1 << 20
 F32 = jnp.float32
@@ -70,7 +71,7 @@
 
 def column_table(cols):
     half = cols // 2
-    pixels = np.concatenate([np.arange(cols), np.arange(-LANES, 0), np.arange(cols, cols + LANES)])
+    pixels = np.concatenate([np.arange(cols), np.arange(-NEAR, 0), np.arange(cols, cols + NEAR)])
     pairs = [(f, b) for b in range(2) for f in range(NDB)]
     beyond = np.array([-2, -1, half, half + 1])
     parts = [column_weight(f, b, np.arange(half), pixels) for f, b in pairs] + [column_weight(f, b, beyond, pixels) for f, b in pairs]
@@ -89,7 +90,9 @@
     def dot(one, two):
         return lax.dot_general(one, two, (dims, ((), ())), preferred_element_type=F32)
 
-    return dot(left[0], right[1]) + dot(left[1], right[0]) + dot(left[0], right[0])
+    count = left[0].shape[0]
+    both = dot(jnp.concatenate(left, 0), right[0])
+    return both[:count] + (both[count:] + dot(left[0], right[1]))
 
 
 def side_by_side(ref, tiles):
@@ -146,46 +149,68 @@
     return merge(merge(items[0], items[1], 1), merge(items[2], items[3], 1), 2)
 
 
-def fill_rows(ext, row, count, start, sources):
-    channels = 4
-    t = 0
-    for ref in sources:
-        for u in range(ref.shape[-1] // LANES):
-            for c in range(channels):
-                value = ref[c, pl.ds(start, count), u * LANES : (u + 1) * LANES]
-                ext[t, pl.ds(row * channels + c, count, stride=channels), :] = jnp.maximum(value, 0.0)
-            t += 1
-
-
-def filter_columns(ext, table, cols):
-    left = halves(side_by_side(ext, range(ext.shape[0])))
-    return dot3(left, [table[0], table[1]])
-
-
-def coefficients(coef, u_ref, count, strip_item):
-    tiles = 2 * NDB + 1
+def near_columns(sources, c, at):
+    def last(ref):
+        return pltpu.roll(ref[c, at, ref.shape[2] - LANES :], NEAR, 1)
+
+    if len(sources) == 1:
+        return [jnp.where(lax.axis_index("fcol") == 0, sources[0][c, at, :LANES], last(sources[0]))]
+    return [last(sources[0]), sources[1][c, at, :LANES]]
+
+
+def fill_rows(ext, row, count, start, own, around):
+    channels, _, cols = own.shape
+    rows = pl.ds(start, count)
+    for c in range(channels):
+        at = pl.ds(row * channels + c, count, stride=channels)
+        for t in range(cols // LANES):
+            ext[t, at, :] = jnp.maximum(own[c, rows, t * LANES : (t + 1) * LANES], 0.0)
+        for t, value in enumerate(near_columns(around, c, rows)):
+            ext[cols // LANES + t, at, :] = jnp.maximum(value, 0.0)
+
+
+def filter_columns(ext, table, cols, lanes):
+    tiles = cols // LANES
+    total = dot3(halves(side_by_side(ext, range(tiles))), [table[i, :cols, lanes] for i in range(2)])
+    if ext.shape[0] - tiles == 1:
+        starts = [pl.multiple_of(cols + (1 - lax.axis_index("fcol")) * NEAR, NEAR)]
+    else:
+        starts = [cols, cols + NEAR]
+    for t, start in enumerate(starts):
+        total += dot3(halves(ext[tiles + t][:, :NEAR]), [table[i, pl.ds(start, NEAR), lanes] for i in range(2)])
+    return total
+
+
+def coefficients(coef, first, tiles, u_ref, count):
     squares = []
-    for tile in range(tiles):
-        lanes = slice(tile * LANES, (tile + 1) * LANES)
-        taps = strip_row_taps((2, 1), STEP_SPARSE) if tile == tiles - 1 else row_taps(tile % NDB, (2, 1), STEP_SPARSE)
+    for tile in tiles:
+        lanes = slice((tile - first) * LANES, (tile - first + 1) * LANES)
+        taps = strip_row_taps((2, 1), STEP_SPARSE) if tile == 2 * NDB else row_taps(tile % NDB, (2, 1), STEP_SPARSE)
         pairs = [coef[8 * i : 8 * i + 8, lanes] for i in range(count + 4)]
         for j in range(count):
             value = filter_rows(taps, pairs, lambda s: j + 2 + s)
-            u_ref[8 * j : 8 * j + 8, lanes] = value
+            u_ref[8 * j : 8 * j + 8, tile * LANES : (tile + 1) * LANES] = value
             squares.append(value * value)
+    return squares
+
+
+def pack_half(squares):
+    return [pack4(squares[g : g + 4]) for g in range(0, len(squares), 4)]
+
+
+def pack_strip(squares, item):
     packed = []
+    count = len(squares) // 2
     for half in range(2):
-        flat = squares[half * NDB * count : (half + 1) * NDB * count]
-        packed.append([pack4(flat[g : g + 4]) for g in range(0, len(flat), 4)])
-        strip = squares[2 * NDB * count + half * (count // 2) : 2 * NDB * count + (half + 1) * (count // 2)]
-        items = [jnp.zeros((8, LANES), F32)] * strip_item
-        for g in range(0, len(strip), 4):
+        strip = squares[half * count : (half + 1) * count]
+        items = [jnp.zeros((8, LANES), F32)] * item
+        for g in range(0, count, 4):
             total = strip[g]
             for k in range(1, len(strip[g : g + 4])):
                 total = total + pltpu.roll(strip[g + k], STRIP * k, 1)
             items.append(total)
         items += [jnp.zeros((8, LANES), F32)] * (4 - len(items))
-        packed[half].append(pack4(items))
+        packed.append(pack4(items))
     return packed
 
 
@@ -197,37 +222,49 @@
 
 
 def inner_kernel(own, *refs):
-    *beside, table, u_ref, keep, send, ext, coef = refs
+    *around, table, u_ref, keep, send, ext, coef = refs
     channels, rows, cols = own.shape
     x = lax.axis_index("frow")
     edge = jnp.zeros((ext.shape[0], 4 * channels, LANES), F32)
     ext[:, pl.ds(pl.multiple_of(x * rows * channels, 16), 4 * channels), :] = edge
-    fill_rows(ext, 4 * (1 - x), rows, 0, [own, *beside])
-    coef[...] = filter_columns(ext, table, cols)
-    packed = coefficients(coef, u_ref, rows // 2 - 2, 0)
-    for half in range(2):
-        for r in range(half * rows // 2, (half + 1) * rows // 2, 8):
+    fill_rows(ext, 4 * (1 - x), rows, 0, own, around)
+    coef[...] = filter_columns(ext, table, cols, slice(0, coef.shape[1]))
+    count = rows // 2 - 2
+    squares = coefficients(coef, 0, range(2 * NDB + 1), u_ref, count)
+    strips = pack_strip(squares[2 * NDB * count :], 0)
+    packed = []
+    for i in range(2):
+        packed.append(pack_half(squares[i * NDB * count : (i + 1) * NDB * count]) + [strips[i]])
+        for r in range(i * rows // 2, (i + 1) * rows // 2, 8):
             for t in range(cols // LANES):
                 total = None
                 for c in range(channels):
                     value = STEP_SPARSE * jnp.maximum(own[c, r : r + 8, t * LANES : (t + 1) * LANES], 0.0)
                     total = value * value if total is None else total + value * value
-                packed[half].append(total)
+                packed[i].append(total)
     store_halves(packed, keep, send)
 
 
 def border_kernel(sides, own, above, keep_inner, send_inner, *refs):
-    beside, corner = refs[:sides], refs[sides : 2 * sides]
-    table, u_ref, keep, send, ext, coef = refs[2 * sides :]
-    rows, cols = own.shape[1:]
+    around = refs[:sides]
+    table, u_ref, keep, send, ext, coef = refs[sides:]
+    channels, rows, cols = own.shape
     x, y = lax.axis_index("frow"), lax.axis_index("chan") % 2
     places = Places(rows, cols)
-    fill_rows(ext, HALO * x, HALO, (1 - x) * (rows - HALO), [own, *beside])
-    fill_rows(ext, HALO * (1 - x), HALO, 0, [above, *corner])
-    coef[...] = filter_columns(ext, table, cols)
-    packed = coefficients(coef, u_ref, 4, 2)
-    strips = [part.pop() for part in packed]
-    store_halves(packed, keep, send, places.border)
+    fill_rows(ext, HALO * x, HALO, pl.multiple_of((1 - x) * (rows - HALO), HALO), own, around)
+    for c in range(channels):
+        at = pl.ds(HALO * (1 - x) * channels + c, HALO, stride=channels)
+        for t in range(cols // LANES):
+            start = (c * (cols // LANES) + t) * HALO
+            ext[t, at, :] = jnp.maximum(above[start : start + HALO, :], 0.0)
+        for t in range(sides):
+            start = (channels * (cols // LANES) + t) * HALO
+            corner = jnp.maximum(above[start : start + HALO, :], 0.0)
+            ext[cols // LANES + t, at, :] = corner if c == 0 else pltpu.roll(corner, LANES - NEAR * c, 1)
+    coef[...] = filter_columns(ext, table, cols, slice(0, coef.shape[1]))
+    squares = coefficients(coef, 0, range(2 * NDB + 1), u_ref, 4)
+    strips = pack_strip(squares[8 * NDB :], 2)
+    store_halves([pack_half(squares[: 4 * NDB]), pack_half(squares[4 * NDB : 8 * NDB])], keep, send, places.border)
     keep[: places.border, :] = keep_inner[...]
     send[: places.border, :] = send_inner[...]
     at = slice(places.strip, places.strip + 8)
@@ -415,44 +452,31 @@
                 out[c, r : r + 8, lanes] = jnp.maximum(estimate - STEP_PRIMAL * total, 0.0)
 
 
-def sent_tiles(cols):
-    if lax.axis_size("fcol") == 2:
-        return [pl.ds(pl.multiple_of((1 - lax.axis_index("fcol")) * (cols - LANES), LANES), LANES)]
-    return [slice(cols - LANES, cols), slice(0, LANES)]
-
-
-def edges_kernel(sides, dirty, own, edge, *refs):
-    wings, corners = refs[:sides], refs[sides : 2 * sides]
-    rows, cols = dirty.shape[1:]
+def hold_kernel(dirty, own):
+    own[...] = dirty[...]
+
+
+def rows_kernel(own, *refs):
+    *around, edge = refs
+    channels, rows, cols = own.shape
     start = pl.ds(pl.multiple_of((1 - lax.axis_index("frow")) * (rows - HALO), HALO), HALO)
-    own[...] = dirty[...]
-    edge[...] = dirty[:, start, :]
-    for wing, corner, lanes in zip(wings, corners, sent_tiles(cols)):
-        wing[...] = dirty[:, :, lanes]
-        corner[...] = dirty[:, start, lanes]
-
-
-def load_kernel(sides, table, near, sems):
-    if sides == 1:
-        cols = table.shape[1] - 2 * LANES
-        beyond = pl.multiple_of(cols + (1 - lax.axis_index("fcol")) * LANES, LANES)
-        loads = [pltpu.make_async_copy(table.at[:, :cols, :], near.at[:, :cols, :], sems.at[0])]
-        loads.append(pltpu.make_async_copy(table.at[:, pl.ds(beyond, LANES), :], near.at[:, cols:, :], sems.at[1]))
-    else:
-        loads = [pltpu.make_async_copy(table, near, sems.at[0])]
-    for load in loads:
-        load.start()
-    for load in loads:
-        load.wait()
+    at = 0
+    for c in range(channels):
+        for t in range(cols // LANES):
+            edge[at : at + HALO, :] = own[c, start, t * LANES : (t + 1) * LANES]
+            at += HALO
+    lane = lax.broadcasted_iota(jnp.int32, (HALO, LANES), 1) // NEAR
+    totals = near_columns(around, 0, start)
+    for c in range(1, channels):
+        parts = near_columns(around, c, start)
+        totals = [jnp.where(lane == c, pltpu.roll(part, NEAR * c, 1), total) for part, total in zip(parts, totals)]
+    for total in totals:
+        edge[at : at + HALO, :] = total
+        at += HALO
 
 
 def add_kernel(one, two, *refs):
     refs[-1][...] = one[...] + two[...]
-
-
-def add_and_copy_kernel(one, two, image, total, again):
-    total[...] = one[...] + two[...]
-    again[...] = image[...]
 
 
 def exchange(values, axis, bit):
@@ -478,20 +502,13 @@
     return results if len(results) > 1 else results[0]
 
 
-def to_neighbours(wings, other=None):
+def from_neighbours(values):
     facets = lax.axis_size("fcol")
-    axes, flips = ("fcol", [0]) if other is None else (("frow", "fcol"), [0, 1])
-
-    def pairs(moves):
-        if other is None:
-            return moves
-        return [(f * facets + i, (1 - f) * facets + j) for f in flips for i, j in moves]
-
     if facets == 2:
-        return [lax.ppermute(wings[0], axes, pairs([(0, 1), (1, 0)]))]
+        return [exchange(values, "fcol", 1)]
     return [
-        lax.ppermute(wings[0], axes, pairs([(i, i + 1) for i in range(facets - 1)])),
-        lax.ppermute(wings[1], axes, pairs([(i + 1, i) for i in range(facets - 1)])),
+        lax.ppermute(values, "fcol", [(i, i + 1) for i in range(facets - 1)]),
+        lax.ppermute(values, "fcol", [(i + 1, i) for i in range(facets - 1)]),
     ]
 
 
@@ -505,29 +522,15 @@
     places, tiles = Places(rows, cols), 2 * NDB + 1
     lane_tiles = cols // LANES + sides
 
-    own, edge, *around = call(
-        lambda *refs: edges_kernel(sides, *refs),
-        "edges",
-        [dirty_image.shape, (channels, HALO, cols)] + [(channels, rows, LANES)] * sides + [(channels, HALO, LANES)] * sides,
-        [dirty_image],
-    )
-    near = pl.pallas_call(
-        lambda *refs: load_kernel(sides, *refs),
-        name="load",
-        out_shape=jax.ShapeDtypeStruct((2, cols + sides * LANES, tiles * LANES), BF16),
-        in_specs=[pl.BlockSpec(memory_space=pltpu.HBM)],
-        out_specs=vmem(1)[0],
-        scratch_shapes=[pltpu.SemaphoreType.DMA((2,))],
-        compiler_params=pltpu.CompilerParams(vmem_limit_bytes=16 * MIB),
-    )(table)
-    beside = to_neighbours(around[:sides])
+    around = from_neighbours(dirty_image)
+    own = call(hold_kernel, "hold", [dirty_image.shape], [dirty_image])
+    edge = call(rows_kernel, "rows", [((channels * (cols // LANES) + sides) * HALO, LANES)], [own, *around])
     above = exchange(edge, "frow", 1)
-    corner = to_neighbours(around[sides:], "frow")
-    u_inner, inner_keep, inner_send = call(
+    u_inner, keep, send = call(
         inner_kernel,
         "inner",
         [(8 * places.inner, tiles * LANES), (places.border, LANES), (places.border, LANES)],
-        [own, *beside, near],
+        [own, *around, table],
         [(lane_tiles, 8 * (places.inner + 4), LANES), (8 * (places.inner + 4), tiles * LANES)],
         24,
     )
@@ -535,13 +538,13 @@
         lambda *refs: border_kernel(sides, *refs),
         "border",
         [(8 * 4, tiles * LANES), (places.all, LANES), (places.all, LANES)],
-        [own, above, inner_keep, inner_send, *beside, *corner, near],
+        [own, above, keep, send, *around, table],
         [(lane_tiles, 8 * 8, LANES), (8 * 8, tiles * LANES)],
         24,
     )
     received = exchange(send, "chan", 1)
-    total, again = call(add_and_copy_kernel, "add", [(places.all, LANES), dirty_image.shape], [keep, received, own])
-    other = exchange(again, "chan", 1)
+    total = call(add_kernel, "add", [(places.all, LANES)], [keep, received])
+    other = exchange(own, "chan", 1)
     nuclear = call(
         lambda *refs: nuclear_kernel(nuclear_limit, *refs),
         "nuclear",
@@ -552,14 +555,14 @@
     bit = 2
     while bit < chans:
         received = exchange(total, "chan", bit)
-        total = call(add_kernel, "add", [(places.all, LANES)], [total, received], later=[other if 2 * bit < chans else nuclear])
+        total = call(add_kernel, "add", [(places.all, LANES)], [total, received], later=[] if 2 * bit < chans else [nuclear])
         bit *= 2
     theirs = exchange(total, "chan", 1)
     step = call(
         lambda *refs: first_kernel(sparse_limit, *refs),
         "first",
         [(2 * cols // LANES, channels * rows, LANES)],
-        [own, density, nuclear, u_inner, u_border, total, near],
+        [own, density, nuclear, u_inner, u_border, total, table],
         [(4 * rows, NDB * LANES), (places.all, LANES)],
         24,
     )
@@ -567,7 +570,7 @@
         lambda *refs: second_kernel(sparse_limit, *refs),
         "second",
         [dirty_image.shape],
-        [own, step, u_inner, u_border, total, theirs, near],
+        [own, step, u_inner, u_border, total, theirs, table],
         [(4 * rows, (NDB + 1) * LANES), (cols // LANES, 4 * rows, LANES), (2, places.all, LANES)],
         24,
     )

time: 30.8 us -> 28.5 us (0.925)
  waiting for transfers between devices: 11.1 us -> 8.09 us
  starting transfers between devices: 11.3 us -> 12.7 us
  local copies, waits for them, and re-layouts: 2.57 us -> 2.24 us
    ppermute x6 -> x7, waiting for transfers between devices: 11 us -> 8.09 us  [exchange(): return lax.ppermute(values, axis, [(i, i ^ bit) for i in range(count)])]
    ppermute x6 -> x7, starting transfers between devices: 10.7 us -> 12.7 us  [exchange(): return lax.ppermute(values, axis, [(i, i ^ bit) for i in range(count)])]
    ppermute x2 -> x0, starting transfers between devices: 0.59 us -> none  [to_neighbours(): return [lax.ppermute(wings[0], axes, pairs([(0, 1), (1, 0)]))]]
    unnamed x6 -> x8, local copies, waits for them, and re-layouts: 2.57 us -> 2.24 us
    pallas_call x9 -> x10, Pallas kernels: 5.3 us -> 5.25 us  [call(): pl.pallas_call(kernel, name=name, out_shape=many, in_specs=vmem(len(opera...]
  transfers between devices with their start and end apart: 8 -> 7, of which waited for: 5 -> 5; matrix products, arithmetic and copies ran while one was open for 0% -> 0% of each run, Pallas kernels for 12% -> 12%
where the time goes in v3:
time: 28.5 us; the launch traced here: 28.3 us
  starting transfers between devices  12.7 us (45%)
  waiting for transfers between devices  8.09 us (28%)
  Pallas kernels  5.25 us (18%)
  local copies, waits for them, and re-layouts  2.24 us (8%)
    ppermute x7, starting transfers between devices, exchange(): return lax.ppermute(values, axis, [(i, i ^ bit) for i in range(count)])  12.7 us
    ppermute x7, waiting for transfers between devices, exchange(): return lax.ppermute(values, axis, [(i, i ^ bit) for i in range(count)])  8.09 us
    pallas_call x10, Pallas kernels, call(): pl.pallas_call(kernel, name=name, out_shape=many, in_specs=vmem(len(opera...  5.25 us
    unnamed x8, local copies, waits for them, and re-layouts  2.24 us
  transfers between devices with their start and end apart: 7, of which 5 were waited for; matrix products, arithmetic and copies ran while one was open for 0% of the time, Pallas kernels for 12%

profile of v3, /device:TPU:0, one launch (start us, length us, event | category | flops | bytes accessed | tf_op | source)
XLA Modules:
  0.0 28.3 jit_solution(6519142896651661040)
XLA Ops:
  0.0 0.5 %collective-permute-start.1 = (f32[4,32,256]{2,1,0:T(8,128)}, f32[4,32,256]{2,1,0:T(8,128)S(1)}, u32[]{:S(2)}, u32[]{:S(2)}) collective-permute-start(f32[4,32,256]{2,1,0:T(8,128)} %dirty.1), channel_id=1, source_target_pairs={{0,8},{8,0},{1,9},{9,1},{2,10},{10,2},{3,11},{11,3},{4,12},{12,4},... | collective-permute-start | bytes 393224 | tf_op jit(solution)/shard_map/ppermute | solution.py:484
  0.5 0.9 %copy-done.2 = f32[4,32,256]{2,1,0:T(8,128)S(1)} copy-done((f32[4,32,256]{2,1,0:T(8,128)S(1)}, f32[4,32,256]{2,1,0:T(8,128)}, u32[]{:S(2)}) %copy-start.2) | copy-done | bytes 131096
  1.4 0.3 collective-permute-done.1.refs_0_.refs_4_
  1.7 0.1 rows.1
  1.8 2.8 %collective-permute-start.2 = (f32[72,128]{1,0:T(8,128)S(1)}, f32[72,128]{1,0:T(8,128)S(1)}, u32[]{:S(2)}, u32[]{:S(2)}) collective-permute-start(f32[72,128]{1,0:T(8,128)S(1)} %rows.1), channel_id=1, source_target_pairs={{0,16},{16,0},{1,17},{17,1},{2,18},{18,2},{3,19},{19,3},{4,20},{20... | collective-permute-start | bytes 110600 | tf_op jit(solution)/shard_map/ppermute | solution.py:484
  4.6 1.3 %copy-done = bf16[2,288,1152]{2,1,0:T(8,128)(2,1)S(1)} copy-done((bf16[2,288,1152]{2,1,0:T(8,128)(2,1)S(1)}, bf16[2,288,1152]{2,1,0:T(8,128)(2,1)}, u32[]{:S(2)}) %copy-start) | copy-done | bytes 1327128
  6.0 1.0 %inner.1 = (f32[112,1152]{1,0:T(8,128)S(1)}, f32[152,128]{1,0:T(8,128)S(1)}, f32[152,128]{1,0:T(8,128)S(1)}) custom-call(f32[4,32,256]{2,1,0:T(8,128)S(1)} %hold.1.refs_0_.own, f32[4,32,256]{2,1,0:T(8,128)S(1)} %collective-permute-done.1.refs_0_.refs_4_, bf16[2,288,1152]{2,1,0:T(8,128)(2,1)S(1)} %copy-done), custom_call_target="tpu_custom_call" | custom-call | tf_op jit(solution)/shard_map/inner/pallas_call | solution.py:493
  7.0 0.0 collective-permute-done.2.refs_1_
  7.0 0.0 copy-start.3
  7.0 0.6 %border.1 = (f32[32,1152]{1,0:T(8,128)S(1)}, f32[184,128]{1,0:T(8,128)S(1)}, f32[184,128]{1,0:T(8,128)S(1)}) custom-call(f32[4,32,256]{2,1,0:T(8,128)S(1)} %hold.1.refs_0_.own, f32[72,128]{1,0:T(8,128)S(1)} %collective-permute-done.2.refs_1_, f32[152,128]{1,0:T(8,128)S(1)} %get-tuple-element.12.refs_2_, f32[152,128]{1,0:T(8,128)S(1)} %get-tuple-element.13.refs_3_, ...), custom_call_target="tpu_custom_call" | custom-call | tf_op jit(solution)/shard_map/border/pallas_call | solution.py:493
  7.7 1.7 %collective-permute-start.3 = (f32[184,128]{1,0:T(8,128)S(1)}, f32[184,128]{1,0:T(8,128)S(1)}, u32[]{:S(2)}, u32[]{:S(2)}) collective-permute-start(f32[184,128]{1,0:T(8,128)S(1)} %get-tuple-element.16), channel_id=1, source_target_pairs={{0,1},{1,0},{2,3},{3,2},{4,5},{5,4},{6,7},{7,6},{8,9},{9,8},{10,11... | collective-permute-start | bytes 282632 | tf_op jit(solution)/shard_map/ppermute | solution.py:484
  9.3 3.0 %collective-permute-done.3.two = f32[184,128]{1,0:T(8,128)S(1)} collective-permute-done((f32[184,128]{1,0:T(8,128)S(1)}, f32[184,128]{1,0:T(8,128)S(1)}, u32[]{:S(2)}, u32[]{:S(2)}) %collective-permute-start.3) | collective-permute-done | bytes 94240 | tf_op jit(solution)/shard_map/ppermute | solution.py:484
  12.3 1.7 %collective-permute-start.4 = (f32[184,128]{1,0:T(8,128)S(1)}, f32[184,128]{1,0:T(8,128)S(1)}, u32[]{:S(2)}, u32[]{:S(2)}) collective-permute-start(f32[184,128]{1,0:T(8,128)S(1)} %add.3.one), channel_id=1, source_target_pairs={{0,2},{1,3},{2,0},{3,1},{4,6},{5,7},{6,4},{7,5},{8,10},{9,11},{10,... | collective-permute-start | bytes 282632 | tf_op jit(solution)/shard_map/ppermute | solution.py:484
  14.0 1.5 %collective-permute-start = (f32[4,32,256]{2,1,0:T(8,128)S(1)}, f32[4,32,256]{2,1,0:T(8,128)S(1)}, u32[]{:S(2)}, u32[]{:S(2)}) collective-permute-start(f32[4,32,256]{2,1,0:T(8,128)S(1)} %hold.1.refs_0_.own), channel_id=1, source_target_pairs={{0,1},{1,0},{2,3},{3,2},{4,5},{5,4},{6,7},{7,6},{8,9},{9,8},{10,11... | collective-permute-start | bytes 393224 | tf_op jit(solution)/shard_map/ppermute | solution.py:484
  15.5 1.4 %collective-permute-done.4.two = f32[184,128]{1,0:T(8,128)S(1)} collective-permute-done((f32[184,128]{1,0:T(8,128)S(1)}, f32[184,128]{1,0:T(8,128)S(1)}, u32[]{:S(2)}, u32[]{:S(2)}) %collective-permute-start.4) | collective-permute-done | bytes 94240 | tf_op jit(solution)/shard_map/ppermute | solution.py:484
  16.9 2.8 %collective-permute-start.5 = (f32[184,128]{1,0:T(8,128)S(1)}, f32[184,128]{1,0:T(8,128)S(1)}, u32[]{:S(2)}, u32[]{:S(2)}) collective-permute-start(f32[184,128]{1,0:T(8,128)S(1)} %add.4.one), channel_id=1, source_target_pairs={{0,4},{1,5},{2,6},{3,7},{4,0},{5,1},{6,2},{7,3},{8,12},{9,13},{10,... | collective-permute-start | bytes 282632 | tf_op jit(solution)/shard_map/ppermute | solution.py:484
  19.7 0.0 collective-permute-done.refs_1_
  19.7 1.8 %nuclear.1.refs_0_.refs_2_ = f32[4,32,256]{2,1,0:T(8,128)S(1)} custom-call(f32[4,32,256]{2,1,0:T(8,128)S(1)} %hold.1.refs_0_.own, f32[4,32,256]{2,1,0:T(8,128)S(1)} %collective-permute-done.refs_1_), custom_call_target="tpu_custom_call" | custom-call | tf_op jit(solution)/shard_map/nuclear/pallas_call | solution.py:493
  21.5 0.9 %collective-permute-done.5.two = f32[184,128]{1,0:T(8,128)S(1)} collective-permute-done((f32[184,128]{1,0:T(8,128)S(1)}, f32[184,128]{1,0:T(8,128)S(1)}, u32[]{:S(2)}, u32[]{:S(2)}) %collective-permute-start.5) | collective-permute-done | bytes 94240 | tf_op jit(solution)/shard_map/ppermute | solution.py:484
  22.5 1.7 %collective-permute-start.6 = (f32[184,128]{1,0:T(8,128)S(1)}, f32[184,128]{1,0:T(8,128)S(1)}, u32[]{:S(2)}, u32[]{:S(2)}) collective-permute-start(f32[184,128]{1,0:T(8,128)S(1)} %add.5.refs_5_.refs_4_), channel_id=1, source_target_pairs={{0,1},{1,0},{2,3},{3,2},{4,5},{5,4},{6,7},{7,6},{8,9},{9,8},{10,11... | collective-permute-start | bytes 282632 | tf_op jit(solution)/shard_map/ppermute | solution.py:484
  24.2 0.4 %first.1.refs_1_ = f32[4,128,128]{2,1,0:T(8,128)S(1)} custom-call(f32[4,32,256]{2,1,0:T(8,128)S(1)} %hold.1.refs_0_.own, f32[4,32,256]{2,1,0:T(8,128)S(1)} %copy-done.3, f32[4,32,256]{2,1,0:T(8,128)S(1)} %nuclear.1.refs_0_.refs_2_, f32[112,1152]{1,0:T(8,128)S(1)} %get-tuple-element.11.refs_3_.refs_2_, f32[32,1152]{1,0:T(8,128)S(1)} %get-tuple-element.14.refs_4_.refs_3_, ...), custom_call_target="tpu_custom_call" | custom-call | tf_op jit(solution)/shard_map/first/pallas_call | solution.py:493
  24.6 2.5 %collective-permute-done.6.refs_5_ = f32[184,128]{1,0:T(8,128)S(1)} collective-permute-done((f32[184,128]{1,0:T(8,128)S(1)}, f32[184,128]{1,0:T(8,128)S(1)}, u32[]{:S(2)}, u32[]{:S(2)}) %collective-permute-start.6) | collective-permute-done | bytes 94240 | tf_op jit(solution)/shard_map/ppermute | solution.py:484
  27.1 0.0 copy-done.1
  27.1 1.2 %second.1 = f32[4,32,256]{2,1,0:T(8,128)} custom-call(f32[4,32,256]{2,1,0:T(8,128)S(1)} %hold.1.refs_0_.own, f32[4,128,128]{2,1,0:T(8,128)S(1)} %first.1.refs_1_, f32[112,1152]{1,0:T(8,128)S(1)} %get-tuple-element.11.refs_3_.refs_2_, f32[32,1152]{1,0:T(8,128)S(1)} %get-tuple-element.14.refs_4_.refs_3_, f32[184,128]{1,0:T(8,128)S(1)} %add.5.refs_5_.refs_4_, ...), custom_call_target="tpu_custom_call" | custom-call | tf_op jit(solution)/shard_map/second/pallas_call | solution.py:493
  (8 shorter events, 0.1 us)
Async XLA Ops:
  0.0 1.6 %collective-permute-start.1 = (f32[4,32,256]{2,1,0:T(8,128)}, f32[4,32,256]{2,1,0:T(8,128)S(1)}, u32[]{:S(2)}, u32[]{:S(2)}) collective-permute-start(f32[4,32,256]{2,1,0:T(8,128)} %dirty.1), channel_id=1, source_target_pairs={{0,8},{8,0},{1,9},{9,1},{2,10},{10,2},{3,11},{11,3},{4,12},{12,4},... | collective-permute-start | bytes 393224 | tf_op jit(solution)/shard_map/ppermute | solution.py:484
  0.5 0.9 %copy-start.2 = (f32[4,32,256]{2,1,0:T(8,128)S(1)}, f32[4,32,256]{2,1,0:T(8,128)}, u32[]{:S(2)}) copy-start(f32[4,32,256]{2,1,0:T(8,128)} %dirty.1) | copy-start | bytes 393220
  1.8 5.2 %collective-permute-start.2 = (f32[72,128]{1,0:T(8,128)S(1)}, f32[72,128]{1,0:T(8,128)S(1)}, u32[]{:S(2)}, u32[]{:S(2)}) collective-permute-start(f32[72,128]{1,0:T(8,128)S(1)} %rows.1), channel_id=1, source_target_pairs={{0,16},{16,0},{1,17},{17,1},{2,18},{18,2},{3,19},{19,3},{4,20},{20... | collective-permute-start | bytes 110600 | tf_op jit(solution)/shard_map/ppermute | solution.py:484
  4.6 1.3 %copy-start = (bf16[2,288,1152]{2,1,0:T(8,128)(2,1)S(1)}, bf16[2,288,1152]{2,1,0:T(8,128)(2,1)}, u32[]{:S(2)}) copy-start(bf16[2,288,1152]{2,1,0:T(8,128)(2,1)} %constant.11.refs_1_.refs_5_.refs_6_) | copy-start | bytes 3981316
  7.0 17.2 %copy-start.3 = (f32[4,32,256]{2,1,0:T(8,128)S(1)}, f32[4,32,256]{2,1,0:T(8,128)}, u32[]{:S(2)}) copy-start(f32[4,32,256]{2,1,0:T(8,128)} %refs_1_.1) | copy-start | bytes 393220
  7.7 4.6 %collective-permute-start.3 = (f32[184,128]{1,0:T(8,128)S(1)}, f32[184,128]{1,0:T(8,128)S(1)}, u32[]{:S(2)}, u32[]{:S(2)}) collective-permute-start(f32[184,128]{1,0:T(8,128)S(1)} %get-tuple-element.16), channel_id=1, source_target_pairs={{0,1},{1,0},{2,3},{3,2},{4,5},{5,4},{6,7},{7,6},{8,9},{9,8},{10,11... | collective-permute-start | bytes 282632 | tf_op jit(solution)/shard_map/ppermute | solution.py:484
  12.3 4.6 %collective-permute-start.4 = (f32[184,128]{1,0:T(8,128)S(1)}, f32[184,128]{1,0:T(8,128)S(1)}, u32[]{:S(2)}, u32[]{:S(2)}) collective-permute-start(f32[184,128]{1,0:T(8,128)S(1)} %add.3.one), channel_id=1, source_target_pairs={{0,2},{1,3},{2,0},{3,1},{4,6},{5,7},{6,4},{7,5},{8,10},{9,11},{10,... | collective-permute-start | bytes 282632 | tf_op jit(solution)/shard_map/ppermute | solution.py:484
  14.0 5.7 %collective-permute-start = (f32[4,32,256]{2,1,0:T(8,128)S(1)}, f32[4,32,256]{2,1,0:T(8,128)S(1)}, u32[]{:S(2)}, u32[]{:S(2)}) collective-permute-start(f32[4,32,256]{2,1,0:T(8,128)S(1)} %hold.1.refs_0_.own), channel_id=1, source_target_pairs={{0,1},{1,0},{2,3},{3,2},{4,5},{5,4},{6,7},{7,6},{8,9},{9,8},{10,11... | collective-permute-start | bytes 393224 | tf_op jit(solution)/shard_map/ppermute | solution.py:484
  16.9 5.5 %collective-permute-start.5 = (f32[184,128]{1,0:T(8,128)S(1)}, f32[184,128]{1,0:T(8,128)S(1)}, u32[]{:S(2)}, u32[]{:S(2)}) collective-permute-start(f32[184,128]{1,0:T(8,128)S(1)} %add.4.one), channel_id=1, source_target_pairs={{0,4},{1,5},{2,6},{3,7},{4,0},{5,1},{6,2},{7,3},{8,12},{9,13},{10,... | collective-permute-start | bytes 282632 | tf_op jit(solution)/shard_map/ppermute | solution.py:484
  22.5 4.6 %collective-permute-start.6 = (f32[184,128]{1,0:T(8,128)S(1)}, f32[184,128]{1,0:T(8,128)S(1)}, u32[]{:S(2)}, u32[]{:S(2)}) collective-permute-start(f32[184,128]{1,0:T(8,128)S(1)} %add.5.refs_5_.refs_4_), channel_id=1, source_target_pairs={{0,1},{1,0},{2,3},{3,2},{4,5},{5,4},{6,7},{7,6},{8,9},{9,8},{10,11... | collective-permute-start | bytes 282632 | tf_op jit(solution)/shard_map/ppermute | solution.py:484
  24.2 3.0 %copy-start.1 = (bf16[2,288,1152]{2,1,0:T(8,128)(2,1)S(1)}, bf16[2,288,1152]{2,1,0:T(8,128)(2,1)}, u32[]{:S(2)}) copy-start(bf16[2,288,1152]{2,1,0:T(8,128)(2,1)} %constant.11.refs_1_.refs_5_.refs_6_) | copy-start | bytes 3981316

commit v4 on v3

--- a/solution.py
+++ b/solution.py
@@ -2,7 +2,6 @@
 
 import jax
 import jax.numpy as jnp
-import numpy as np
 from jax import lax
 from jax.experimental import pallas as pl
 from jax.experimental.pallas import tpu as pltpu
@@ -62,25 +61,6 @@
     return table
 
 
-def column_weight(family, band, coefs, pixels):
-    taps = band_taps(family)[band]
-    k = pixels[:, None] - 2 * coefs[None, :] + len(taps) // 2 - 1
-    inside = (k >= 0) & (k < len(taps))
-    return np.where(inside, np.asarray(taps)[np.clip(k, 0, len(taps) - 1)], 0.0)
-
-
-def column_table(cols):
-    half = cols // 2
-    pixels = np.concatenate([np.arange(cols), np.arange(-NEAR, 0), np.arange(cols, cols + NEAR)])
-    pairs = [(f, b) for b in range(2) for f in range(NDB)]
-    beyond = np.array([-2, -1, half, half + 1])
-    parts = [column_weight(f, b, np.arange(half), pixels) for f, b in pairs] + [column_weight(f, b, beyond, pixels) for f, b in pairs]
-    table = np.concatenate(parts, 1)
-    table = jnp.asarray(np.pad(table, ((0, 0), (0, LANES - 4 * len(pairs)))), F32)
-    top = table.astype(BF16)
-    return jnp.stack([top, (table - top.astype(F32)).astype(BF16)], 0)
-
-
 def halves(values):
     top = values.astype(BF16)
     return top, (values - top.astype(F32)).astype(BF16)
@@ -222,7 +202,7 @@
 
 
 def inner_kernel(own, *refs):
-    *around, table, u_ref, keep, send, ext, coef = refs
+    *around, table, u_ref, keep, send, keep_more, send_more, ext, coef = refs
     channels, rows, cols = own.shape
     x = lax.axis_index("frow")
     edge = jnp.zeros((ext.shape[0], 4 * channels, LANES), F32)
@@ -231,10 +211,9 @@
     coef[...] = filter_columns(ext, table, cols, slice(0, coef.shape[1]))
     count = rows // 2 - 2
     squares = coefficients(coef, 0, range(2 * NDB + 1), u_ref, count)
-    strips = pack_strip(squares[2 * NDB * count :], 0)
-    packed = []
+    store_halves([pack_half(squares[i * NDB * count : (i + 1) * NDB * count]) for i in range(2)], keep, send)
+    packed = [[strip] for strip in pack_strip(squares[2 * NDB * count :], 0)]
     for i in range(2):
-        packed.append(pack_half(squares[i * NDB * count : (i + 1) * NDB * count]) + [strips[i]])
         for r in range(i * rows // 2, (i + 1) * rows // 2, 8):
             for t in range(cols // LANES):
                 total = None
@@ -242,10 +221,10 @@
                     value = STEP_SPARSE * jnp.maximum(own[c, r : r + 8, t * LANES : (t + 1) * LANES], 0.0)
                     total = value * value if total is None else total + value * value
                 packed[i].append(total)
-    store_halves(packed, keep, send)
-
-
-def border_kernel(sides, own, above, keep_inner, send_inner, *refs):
+    store_halves(packed, keep_more, send_more)
+
+
+def border_kernel(sides, own, above, keep_more, send_more, *refs):
     around = refs[:sides]
     table, u_ref, keep, send, ext, coef = refs[sides:]
     channels, rows, cols = own.shape
@@ -264,12 +243,11 @@
     coef[...] = filter_columns(ext, table, cols, slice(0, coef.shape[1]))
     squares = coefficients(coef, 0, range(2 * NDB + 1), u_ref, 4)
     strips = pack_strip(squares[8 * NDB :], 2)
-    store_halves([pack_half(squares[: 4 * NDB]), pack_half(squares[4 * NDB : 8 * NDB])], keep, send, places.border)
-    keep[: places.border, :] = keep_inner[...]
-    send[: places.border, :] = send_inner[...]
-    at = slice(places.strip, places.strip + 8)
-    keep[at, :] = keep_inner[at, :] + jnp.where(y == 0, *strips)
-    send[at, :] = send_inner[at, :] + jnp.where(y == 0, *strips[::-1])
+    store_halves([pack_half(squares[: 4 * NDB]), pack_half(squares[4 * NDB : 8 * NDB])], keep, send, places.border - places.strip)
+    keep[: places.border - places.strip, :] = keep_more[...]
+    send[: places.border - places.strip, :] = send_more[...]
+    keep[:8, :] = keep_more[:8, :] + jnp.where(y == 0, *strips)
+    send[:8, :] = send_more[:8, :] + jnp.where(y == 0, *strips[::-1])
 
 
 def pairing_rounds(order):
@@ -452,8 +430,46 @@
                 out[c, r : r + 8, lanes] = jnp.maximum(estimate - STEP_PRIMAL * total, 0.0)
 
 
-def hold_kernel(dirty, own):
+def fixed_taps(family, band, index):
+    total = jnp.zeros(index.shape, F32)
+    for k, tap in enumerate(band_taps(family)[band]):
+        total = jnp.where(index == k, F32(tap), total)
+    return total
+
+
+def hold_kernel(dirty, own, table):
     own[...] = dirty[...]
+    cols = dirty.shape[2]
+    blocks = cols // NEAR
+    rows = {block: block * NEAR for block in range(blocks)} | {-1: cols, blocks: cols + NEAR}
+    row = lax.broadcasted_iota(jnp.int32, (NEAR, LANES), 0)
+    lane = lax.broadcasted_iota(jnp.int32, (NEAR, LANES), 1)
+
+    def put(block, tile, value):
+        at, lanes = slice(rows[block], rows[block] + NEAR), slice(tile * LANES, (tile + 1) * LANES)
+        top = value.astype(BF16)
+        table[0, at, lanes] = top
+        table[1, at, lanes] = (value - top.astype(F32)).astype(BF16)
+
+    pairs = [(f, b) for b in range(2) for f in range(NDB)]
+    for tile, (f, b) in enumerate(pairs):
+        base = fixed_taps(f, b, row - 2 * (lane - 2) + len(DAUBECHIES[f]) // 2 - 1)
+        for block in rows:
+            value = pltpu.roll(base, (block * NEAR // 2 - 2) % LANES, 1)
+            if block <= 0:
+                value = jnp.where(lane < LANES // 2, value, 0.0)
+            if block >= blocks - 1:
+                value = jnp.where(lane < LANES // 2, 0.0, value)
+            put(block, tile, value)
+    column = lane % 4
+    position = jnp.where(column < 2, column - 2, column + cols // 2 - 2)
+    for block in rows:
+        value = jnp.zeros((NEAR, LANES), F32)
+        if block in (-1, 0, blocks - 1, blocks):
+            for tile, (f, b) in enumerate(pairs):
+                part = fixed_taps(f, b, row + block * NEAR - 2 * position + len(DAUBECHIES[f]) // 2 - 1)
+                value = jnp.where(lane // 4 == tile, part, value)
+        put(block, len(pairs), value)
 
 
 def rows_kernel(own, *refs):
@@ -479,6 +495,12 @@
     refs[-1][...] = one[...] + two[...]
 
 
+def add_parts_kernel(one, two, three, four, out):
+    count = one.shape[0]
+    out[:count, :] = one[...] + two[...]
+    out[count:, :] = three[...] + four[...]
+
+
 def exchange(values, axis, bit):
     count = lax.axis_size(axis)
     return lax.ppermute(values, axis, [(i, i ^ bit) for i in range(count)])
@@ -517,33 +539,35 @@
     facets, chans = lax.axis_size("fcol"), lax.axis_size("chan")
     nuclear_limit = math.sqrt(rows * cols)
     sparse_limit = SPARSE_SCALE * math.sqrt(channels * chans)
-    table = column_table(cols)
     sides = 1 if facets == 2 else 2
     places, tiles = Places(rows, cols), 2 * NDB + 1
     lane_tiles = cols // LANES + sides
 
     around = from_neighbours(dirty_image)
-    own = call(hold_kernel, "hold", [dirty_image.shape], [dirty_image])
+    near = jax.ShapeDtypeStruct((2, cols + 2 * NEAR, tiles * LANES), BF16)
+    own, near = call(hold_kernel, "hold", [dirty_image.shape, near], [dirty_image])
     edge = call(rows_kernel, "rows", [((channels * (cols // LANES) + sides) * HALO, LANES)], [own, *around])
     above = exchange(edge, "frow", 1)
-    u_inner, keep, send = call(
+    main, more = (places.strip, LANES), (places.border - places.strip, LANES)
+    u_inner, keep, send, keep_more, send_more = call(
         inner_kernel,
         "inner",
-        [(8 * places.inner, tiles * LANES), (places.border, LANES), (places.border, LANES)],
-        [own, *around, table],
+        [(8 * places.inner, tiles * LANES), main, main, more, more],
+        [own, *around, near],
         [(lane_tiles, 8 * (places.inner + 4), LANES), (8 * (places.inner + 4), tiles * LANES)],
         24,
     )
-    u_border, keep, send = call(
+    received = exchange(send, "chan", 1)
+    u_border, keep_more, send_more = call(
         lambda *refs: border_kernel(sides, *refs),
         "border",
-        [(8 * 4, tiles * LANES), (places.all, LANES), (places.all, LANES)],
-        [own, above, keep, send, *around, table],
+        [(8 * 4, tiles * LANES)] + [(places.all - places.strip, LANES)] * 2,
+        [own, above, keep_more, send_more, *around, near],
         [(lane_tiles, 8 * 8, LANES), (8 * 8, tiles * LANES)],
         24,
     )
-    received = exchange(send, "chan", 1)
-    total = call(add_kernel, "add", [(places.all, LANES)], [keep, received])
+    received_more = exchange(send_more, "chan", 1)
+    total = call(add_parts_kernel, "add", [(places.all, LANES)], [keep, received, keep_more, received_more])
     other = exchange(own, "chan", 1)
     nuclear = call(
         lambda *refs: nuclear_kernel(nuclear_limit, *refs),
@@ -562,7 +586,7 @@
         lambda *refs: first_kernel(sparse_limit, *refs),
         "first",
         [(2 * cols // LANES, channels * rows, LANES)],
-        [own, density, nuclear, u_inner, u_border, total, table],
+        [own, density, nuclear, u_inner, u_border, total, near],
         [(4 * rows, NDB * LANES), (places.all, LANES)],
         24,
     )
@@ -570,7 +594,7 @@
         lambda *refs: second_kernel(sparse_limit, *refs),
         "second",
         [dirty_image.shape],
-        [own, step, u_inner, u_border, total, theirs, table],
+        [own, step, u_inner, u_border, total, theirs, near],
         [(4 * rows, (NDB + 1) * LANES), (cols // LANES, 4 * rows, LANES), (2, places.all, LANES)],
         24,
     )

time: 28.5 us -> 28 us (0.982)
  local copies, waits for them, and re-layouts: 2.24 us -> 0.91 us
  starting transfers between devices: 12.7 us -> 13.3 us
  Pallas kernels: 5.25 us -> 5.67 us
    unnamed x8 -> x4, local copies, waits for them, and re-layouts: 2.24 us -> 0.91 us
    ppermute x7 -> x8, starting transfers between devices: 12.7 us -> 13.3 us  [exchange(): return lax.ppermute(values, axis, [(i, i ^ bit) for i in range(count)])]
    pallas_call x10, Pallas kernels: 5.25 us -> 5.67 us  [call(): pl.pallas_call(kernel, name=name, out_shape=many, in_specs=vmem(len(opera...]
    ppermute x7 -> x8, waiting for transfers between devices: 8.09 us -> 7.97 us  [exchange(): return lax.ppermute(values, axis, [(i, i ^ bit) for i in range(count)])]
  transfers between devices with their start and end apart: 7 -> 8, of which waited for: 5 -> 5; matrix products, arithmetic and copies ran while one was open for 0% -> 0% of each run, Pallas kernels for 12% -> 15%
where the time goes in v4:
time: 28 us; the launch traced here: 27.9 us
  starting transfers between devices  13.3 us (48%)
  waiting for transfers between devices  7.97 us (28%)
  Pallas kernels  5.67 us (20%)
  local copies, waits for them, and re-layouts  0.91 us (3%)
    ppermute x8, starting transfers between devices, exchange(): return lax.ppermute(values, axis, [(i, i ^ bit) for i in range(count)])  13.3 us
    ppermute x8, waiting for transfers between devices, exchange(): return lax.ppermute(values, axis, [(i, i ^ bit) for i in range(count)])  7.97 us
    pallas_call x10, Pallas kernels, call(): pl.pallas_call(kernel, name=name, out_shape=many, in_specs=vmem(len(opera...  5.67 us
    unnamed x4, local copies, waits for them, and re-layouts  0.91 us
  transfers between devices with their start and end apart: 8, of which 5 were waited for; matrix products, arithmetic and copies ran while one was open for 0% of the time, Pallas kernels for 15%

profile of v4, /device:TPU:0, one launch (start us, length us, event | category | flops | bytes accessed | tf_op | source)
XLA Modules:
  0.0 27.9 jit_solution(2437283538880787807)
XLA Ops:
  0.0 0.5 %collective-permute-start.1 = (f32[4,32,256]{2,1,0:T(8,128)}, f32[4,32,256]{2,1,0:T(8,128)S(1)}, u32[]{:S(2)}, u32[]{:S(2)}) collective-permute-start(f32[4,32,256]{2,1,0:T(8,128)} %dirty.1), channel_id=1, source_target_pairs={{0,8},{8,0},{1,9},{9,1},{2,10},{10,2},{3,11},{11,3},{4,12},{12,4},... | collective-permute-start | bytes 393224 | tf_op jit(solution)/shard_map/ppermute | solution.py:506
  0.5 0.9 %copy-done = f32[4,32,256]{2,1,0:T(8,128)S(1)} copy-done((f32[4,32,256]{2,1,0:T(8,128)S(1)}, f32[4,32,256]{2,1,0:T(8,128)}, u32[]{:S(2)}) %copy-start) | copy-done | bytes 131096
  1.4 0.4 %hold.1 = (f32[4,32,256]{2,1,0:T(8,128)S(1)}, bf16[2,288,1152]{2,1,0:T(8,128)(2,1)S(1)}) custom-call(f32[4,32,256]{2,1,0:T(8,128)S(1)} %copy-done), custom_call_target="tpu_custom_call" | custom-call | tf_op jit(solution)/shard_map/hold/pallas_call | solution.py:515
  1.8 0.0 collective-permute-done.1.refs_0_.refs_4_
  1.8 0.2 rows.1
  2.0 2.7 %collective-permute-start.2 = (f32[72,128]{1,0:T(8,128)S(1)}, f32[72,128]{1,0:T(8,128)S(1)}, u32[]{:S(2)}, u32[]{:S(2)}) collective-permute-start(f32[72,128]{1,0:T(8,128)S(1)} %rows.1), channel_id=1, source_target_pairs={{0,16},{16,0},{1,17},{17,1},{2,18},{18,2},{3,19},{19,3},{4,20},{20... | collective-permute-start | bytes 110600 | tf_op jit(solution)/shard_map/ppermute | solution.py:506
  4.6 1.0 %inner.1 = (f32[112,1152]{1,0:T(8,128)S(1)}, f32[112,128]{1,0:T(8,128)S(1)}, f32[112,128]{1,0:T(8,128)S(1)}, f32[40,128]{1,0:T(8,128)S(1)}, f32[40,128]{1,0:T(8,128)S(1)}) custom-call(f32[4,32,256]{2,1,0:T(8,128)S(1)} %get-tuple-element.15.refs_0_.own, f32[4,32,256]{2,1,0:T(8,128)S(1)} %collective-permute-done.1.refs_0_.refs_4_, ...), custom_call_target="tpu_custom_call" | custom-call | tf_op jit(solution)/shard_map/inner/pallas_call | solution.py:515
  5.7 1.6 %collective-permute-start.3 = (f32[112,128]{1,0:T(8,128)S(1)}, f32[112,128]{1,0:T(8,128)S(1)}, u32[]{:S(2)}, u32[]{:S(2)}) collective-permute-start(f32[112,128]{1,0:T(8,128)S(1)} %get-tuple-element.22), channel_id=1, source_target_pairs={{0,1},{1,0},{2,3},{3,2},{4,5},{5,4},{6,7},{7,6},{8,9},{9,8},{10,11... | collective-permute-start | bytes 172040 | tf_op jit(solution)/shard_map/ppermute | solution.py:506
  7.2 0.0 collective-permute-done.2.refs_1_
  7.2 0.6 %border.1 = (f32[32,1152]{1,0:T(8,128)S(1)}, f32[72,128]{1,0:T(8,128)S(1)}, f32[72,128]{1,0:T(8,128)S(1)}) custom-call(f32[4,32,256]{2,1,0:T(8,128)S(1)} %get-tuple-element.15.refs_0_.own, f32[72,128]{1,0:T(8,128)S(1)} %collective-permute-done.2.refs_1_, f32[40,128]{1,0:T(8,128)S(1)} %get-tuple-element.18.refs_2_, f32[40,128]{1,0:T(8,128)S(1)} %get-tuple-element.19.refs_3_, ...), custom_call_target="tpu_custom_call" | custom-call | tf_op jit(solution)/shard_map/border/pallas_call | solution.py:515
  7.9 1.4 %collective-permute-start.4 = (f32[72,128]{1,0:T(8,128)S(1)}, f32[72,128]{1,0:T(8,128)S(1)}, u32[]{:S(2)}, u32[]{:S(2)}) collective-permute-start(f32[72,128]{1,0:T(8,128)S(1)} %get-tuple-element.24), channel_id=1, source_target_pairs={{0,1},{1,0},{2,3},{3,2},{4,5},{5,4},{6,7},{7,6},{8,9},{9,8},{10,11... | collective-permute-start | bytes 110600 | tf_op jit(solution)/shard_map/ppermute | solution.py:506
  9.3 0.6 %collective-permute-done.3.two = f32[112,128]{1,0:T(8,128)S(1)} collective-permute-done((f32[112,128]{1,0:T(8,128)S(1)}, f32[112,128]{1,0:T(8,128)S(1)}, u32[]{:S(2)}, u32[]{:S(2)}) %collective-permute-start.3) | collective-permute-done | bytes 57376 | tf_op jit(solution)/shard_map/ppermute | solution.py:506
  9.9 2.0 %collective-permute-done.4.four = f32[72,128]{1,0:T(8,128)S(1)} collective-permute-done((f32[72,128]{1,0:T(8,128)S(1)}, f32[72,128]{1,0:T(8,128)S(1)}, u32[]{:S(2)}, u32[]{:S(2)}) %collective-permute-start.4) | collective-permute-done | bytes 36896 | tf_op jit(solution)/shard_map/ppermute | solution.py:506
  11.9 1.6 %collective-permute-start.5 = (f32[184,128]{1,0:T(8,128)S(1)}, f32[184,128]{1,0:T(8,128)S(1)}, u32[]{:S(2)}, u32[]{:S(2)}) collective-permute-start(f32[184,128]{1,0:T(8,128)S(1)} %add.3.one), channel_id=1, source_target_pairs={{0,2},{1,3},{2,0},{3,1},{4,6},{5,7},{6,4},{7,5},{8,10},{9,11},{10,... | collective-permute-start | bytes 282632 | tf_op jit(solution)/shard_map/ppermute | solution.py:506
  13.5 1.4 %collective-permute-start = (f32[4,32,256]{2,1,0:T(8,128)S(1)}, f32[4,32,256]{2,1,0:T(8,128)S(1)}, u32[]{:S(2)}, u32[]{:S(2)}) collective-permute-start(f32[4,32,256]{2,1,0:T(8,128)S(1)} %get-tuple-element.15.refs_0_.own), channel_id=1, source_target_pairs={{0,1},{1,0},{2,3},{3,2},{4,5},{5,4},{6,7},{7,6},{8,9},{9,8},{10,11... | collective-permute-start | bytes 393224 | tf_op jit(solution)/shard_map/ppermute | solution.py:506
  14.9 1.6 %collective-permute-done.5.two = f32[184,128]{1,0:T(8,128)S(1)} collective-permute-done((f32[184,128]{1,0:T(8,128)S(1)}, f32[184,128]{1,0:T(8,128)S(1)}, u32[]{:S(2)}, u32[]{:S(2)}) %collective-permute-start.5) | collective-permute-done | bytes 94240 | tf_op jit(solution)/shard_map/ppermute | solution.py:506
  16.5 2.6 %collective-permute-start.6 = (f32[184,128]{1,0:T(8,128)S(1)}, f32[184,128]{1,0:T(8,128)S(1)}, u32[]{:S(2)}, u32[]{:S(2)}) collective-permute-start(f32[184,128]{1,0:T(8,128)S(1)} %add.4.one), channel_id=1, source_target_pairs={{0,4},{1,5},{2,6},{3,7},{4,0},{5,1},{6,2},{7,3},{8,12},{9,13},{10,... | collective-permute-start | bytes 282632 | tf_op jit(solution)/shard_map/ppermute | solution.py:506
  19.2 0.0 collective-permute-done.refs_1_
  19.2 1.8 %nuclear.1.refs_0_.refs_2_ = f32[4,32,256]{2,1,0:T(8,128)S(1)} custom-call(f32[4,32,256]{2,1,0:T(8,128)S(1)} %get-tuple-element.15.refs_0_.own, f32[4,32,256]{2,1,0:T(8,128)S(1)} %collective-permute-done.refs_1_), custom_call_target="tpu_custom_call" | custom-call | tf_op jit(solution)/shard_map/nuclear/pallas_call | solution.py:515
  21.0 1.0 %collective-permute-done.6.two = f32[184,128]{1,0:T(8,128)S(1)} collective-permute-done((f32[184,128]{1,0:T(8,128)S(1)}, f32[184,128]{1,0:T(8,128)S(1)}, u32[]{:S(2)}, u32[]{:S(2)}) %collective-permute-start.6) | collective-permute-done | bytes 94240 | tf_op jit(solution)/shard_map/ppermute | solution.py:506
  22.1 1.5 %collective-permute-start.7 = (f32[184,128]{1,0:T(8,128)S(1)}, f32[184,128]{1,0:T(8,128)S(1)}, u32[]{:S(2)}, u32[]{:S(2)}) collective-permute-start(f32[184,128]{1,0:T(8,128)S(1)} %add.5.refs_5_.refs_4_), channel_id=1, source_target_pairs={{0,1},{1,0},{2,3},{3,2},{4,5},{5,4},{6,7},{7,6},{8,9},{9,8},{10,11... | collective-permute-start | bytes 282632 | tf_op jit(solution)/shard_map/ppermute | solution.py:506
  23.6 0.4 %first.1.refs_1_ = f32[4,128,128]{2,1,0:T(8,128)S(1)} custom-call(f32[4,32,256]{2,1,0:T(8,128)S(1)} %get-tuple-element.15.refs_0_.own, f32[4,32,256]{2,1,0:T(8,128)S(1)} %copy-done.1, f32[4,32,256]{2,1,0:T(8,128)S(1)} %nuclear.1.refs_0_.refs_2_, f32[112,1152]{1,0:T(8,128)S(1)} %get-tuple-element.17.refs_3_.refs_2_, ...), custom_call_target="tpu_custom_call" | custom-call | tf_op jit(solution)/shard_map/first/pallas_call | solution.py:515
  24.0 2.8 %collective-permute-done.7.refs_5_ = f32[184,128]{1,0:T(8,128)S(1)} collective-permute-done((f32[184,128]{1,0:T(8,128)S(1)}, f32[184,128]{1,0:T(8,128)S(1)}, u32[]{:S(2)}, u32[]{:S(2)}) %collective-permute-start.7) | collective-permute-done | bytes 94240 | tf_op jit(solution)/shard_map/ppermute | solution.py:506
  26.7 1.2 %second.1 = f32[4,32,256]{2,1,0:T(8,128)} custom-call(f32[4,32,256]{2,1,0:T(8,128)S(1)} %get-tuple-element.15.refs_0_.own, f32[4,128,128]{2,1,0:T(8,128)S(1)} %first.1.refs_1_, f32[112,1152]{1,0:T(8,128)S(1)} %get-tuple-element.17.refs_3_.refs_2_, f32[32,1152]{1,0:T(8,128)S(1)} %get-tuple-element.20.refs_4_.refs_3_, f32[184,128]{1,0:T(8,128)S(1)} %add.5.refs_5_.refs_4_, ...), custom_call_target="tpu_custom_call" | custom-call | tf_op jit(solution)/shard_map/second/pallas_call | solution.py:515
  (6 shorter events, 0.0 us)
Async XLA Ops:
  0.0 1.8 %collective-permute-start.1 = (f32[4,32,256]{2,1,0:T(8,128)}, f32[4,32,256]{2,1,0:T(8,128)S(1)}, u32[]{:S(2)}, u32[]{:S(2)}) collective-permute-start(f32[4,32,256]{2,1,0:T(8,128)} %dirty.1), channel_id=1, source_target_pairs={{0,8},{8,0},{1,9},{9,1},{2,10},{10,2},{3,11},{11,3},{4,12},{12,4},... | collective-permute-start | bytes 393224 | tf_op jit(solution)/shard_map/ppermute | solution.py:506
  0.5 0.9 %copy-start = (f32[4,32,256]{2,1,0:T(8,128)S(1)}, f32[4,32,256]{2,1,0:T(8,128)}, u32[]{:S(2)}) copy-start(f32[4,32,256]{2,1,0:T(8,128)} %dirty.1) | copy-start | bytes 393220
  2.0 5.3 %collective-permute-start.2 = (f32[72,128]{1,0:T(8,128)S(1)}, f32[72,128]{1,0:T(8,128)S(1)}, u32[]{:S(2)}, u32[]{:S(2)}) collective-permute-start(f32[72,128]{1,0:T(8,128)S(1)} %rows.1), channel_id=1, source_target_pairs={{0,16},{16,0},{1,17},{17,1},{2,18},{18,2},{3,19},{19,3},{4,20},{20... | collective-permute-start | bytes 110600 | tf_op jit(solution)/shard_map/ppermute | solution.py:506
  5.7 4.2 %collective-permute-start.3 = (f32[112,128]{1,0:T(8,128)S(1)}, f32[112,128]{1,0:T(8,128)S(1)}, u32[]{:S(2)}, u32[]{:S(2)}) collective-permute-start(f32[112,128]{1,0:T(8,128)S(1)} %get-tuple-element.22), channel_id=1, source_target_pairs={{0,1},{1,0},{2,3},{3,2},{4,5},{5,4},{6,7},{7,6},{8,9},{9,8},{10,11... | collective-permute-start | bytes 172040 | tf_op jit(solution)/shard_map/ppermute | solution.py:506
  7.2 16.3 %copy-start.1 = (f32[4,32,256]{2,1,0:T(8,128)S(1)}, f32[4,32,256]{2,1,0:T(8,128)}, u32[]{:S(2)}) copy-start(f32[4,32,256]{2,1,0:T(8,128)} %refs_1_.1) | copy-start | bytes 393220
  7.9 4.0 %collective-permute-start.4 = (f32[72,128]{1,0:T(8,128)S(1)}, f32[72,128]{1,0:T(8,128)S(1)}, u32[]{:S(2)}, u32[]{:S(2)}) collective-permute-start(f32[72,128]{1,0:T(8,128)S(1)} %get-tuple-element.24), channel_id=1, source_target_pairs={{0,1},{1,0},{2,3},{3,2},{4,5},{5,4},{6,7},{7,6},{8,9},{9,8},{10,11... | collective-permute-start | bytes 110600 | tf_op jit(solution)/shard_map/ppermute | solution.py:506
  11.9 4.6 %collective-permute-start.5 = (f32[184,128]{1,0:T(8,128)S(1)}, f32[184,128]{1,0:T(8,128)S(1)}, u32[]{:S(2)}, u32[]{:S(2)}) collective-permute-start(f32[184,128]{1,0:T(8,128)S(1)} %add.3.one), channel_id=1, source_target_pairs={{0,2},{1,3},{2,0},{3,1},{4,6},{5,7},{6,4},{7,5},{8,10},{9,11},{10,... | collective-permute-start | bytes 282632 | tf_op jit(solution)/shard_map/ppermute | solution.py:506
  13.5 5.7 %collective-permute-start = (f32[4,32,256]{2,1,0:T(8,128)S(1)}, f32[4,32,256]{2,1,0:T(8,128)S(1)}, u32[]{:S(2)}, u32[]{:S(2)}) collective-permute-start(f32[4,32,256]{2,1,0:T(8,128)S(1)} %get-tuple-element.15.refs_0_.own), channel_id=1, source_target_pairs={{0,1},{1,0},{2,3},{3,2},{4,5},{5,4},{6,7},{7,6},{8,9},{9,8},{10,11... | collective-permute-start | bytes 393224 | tf_op jit(solution)/shard_map/ppermute | solution.py:506
  16.5 5.5 %collective-permute-start.6 = (f32[184,128]{1,0:T(8,128)S(1)}, f32[184,128]{1,0:T(8,128)S(1)}, u32[]{:S(2)}, u32[]{:S(2)}) collective-permute-start(f32[184,128]{1,0:T(8,128)S(1)} %add.4.one), channel_id=1, source_target_pairs={{0,4},{1,5},{2,6},{3,7},{4,0},{5,1},{6,2},{7,3},{8,12},{9,13},{10,... | collective-permute-start | bytes 282632 | tf_op jit(solution)/shard_map/ppermute | solution.py:506
  22.1 4.6 %collective-permute-start.7 = (f32[184,128]{1,0:T(8,128)S(1)}, f32[184,128]{1,0:T(8,128)S(1)}, u32[]{:S(2)}, u32[]{:S(2)}) collective-permute-start(f32[184,128]{1,0:T(8,128)S(1)} %add.5.refs_5_.refs_4_), channel_id=1, source_target_pairs={{0,1},{1,0},{2,3},{3,2},{4,5},{5,4},{6,7},{7,6},{8,9},{9,8},{10,11... | collective-permute-start | bytes 282632 | tf_op jit(solution)/shard_map/ppermute | solution.py:506

commit v5 on v4

--- a/solution.py
+++ b/solution.py
@@ -35,6 +35,7 @@
 STEP_SPARSE = 0.5
 SPARSE_SCALE = 0.5
 LANES = 128
+BORDER_ROWS = [2 + len(taps) // 4 for taps in DAUBECHIES]
 STRIP = 32
 NEAR = 16
 HALO = 8
@@ -149,16 +150,23 @@
             ext[cols // LANES + t, at, :] = jnp.maximum(value, 0.0)
 
 
-def filter_columns(ext, table, cols, lanes):
-    tiles = cols // LANES
-    total = dot3(halves(side_by_side(ext, range(tiles))), [table[i, :cols, lanes] for i in range(2)])
-    if ext.shape[0] - tiles == 1:
-        starts = [pl.multiple_of(cols + (1 - lax.axis_index("fcol")) * NEAR, NEAR)]
-    else:
-        starts = [cols, cols + NEAR]
-    for t, start in enumerate(starts):
-        total += dot3(halves(ext[tiles + t][:, :NEAR]), [table[i, pl.ds(start, NEAR), lanes] for i in range(2)])
-    return total
+def filter_columns(ext, table, cols, coef):
+    tiles, main = cols // LANES, 2 * NDB * LANES
+    coef[...] = dot3(halves(side_by_side(ext, range(tiles))), [table[i, :cols, :] for i in range(2)])
+    place = lax.axis_index("fcol")
+    lane = lax.broadcasted_iota(jnp.int32, (ext.shape[1], LANES), 1)
+    right = [place == 0] if ext.shape[0] - tiles == 1 else [False, True]
+    for t, last in enumerate(right):
+        start = cols + NEAR * t if len(right) > 1 else pl.multiple_of(cols + NEAR * (1 - place), NEAR)
+        rows = pl.ds(start, NEAR)
+        weights = [jnp.concatenate([table[i, rows, :LANES], table[i, rows, main:]], 1) for i in range(2)]
+        part = dot3(halves(ext[tiles + t][:, :NEAR]), weights)
+        coef[:, main:] += part[:, LANES:]
+        first = jnp.where(last, LANES - 2, 0)
+        for tile in range(2 * NDB):
+            turn = lax.rem(jnp.where(last, LANES - NEAR, 0) + LANES - NEAR * tile, LANES)
+            moved = pltpu.roll(part[:, :LANES], turn, 1)
+            coef[:, tile * LANES : (tile + 1) * LANES] += jnp.where((lane >= first) & (lane < first + 2), moved, 0.0)
 
 
 def coefficients(coef, first, tiles, u_ref, count):
@@ -208,7 +216,7 @@
     edge = jnp.zeros((ext.shape[0], 4 * channels, LANES), F32)
     ext[:, pl.ds(pl.multiple_of(x * rows * channels, 16), 4 * channels), :] = edge
     fill_rows(ext, 4 * (1 - x), rows, 0, own, around)
-    coef[...] = filter_columns(ext, table, cols, slice(0, coef.shape[1]))
+    filter_columns(ext, table, cols, coef)
     count = rows // 2 - 2
     squares = coefficients(coef, 0, range(2 * NDB + 1), u_ref, count)
     store_halves([pack_half(squares[i * NDB * count : (i + 1) * NDB * count]) for i in range(2)], keep, send)
@@ -240,10 +248,16 @@
             start = (channels * (cols // LANES) + t) * HALO
             corner = jnp.maximum(above[start : start + HALO, :], 0.0)
             ext[cols // LANES + t, at, :] = corner if c == 0 else pltpu.roll(corner, LANES - NEAR * c, 1)
-    coef[...] = filter_columns(ext, table, cols, slice(0, coef.shape[1]))
+    filter_columns(ext, table, cols, coef)
     squares = coefficients(coef, 0, range(2 * NDB + 1), u_ref, 4)
     strips = pack_strip(squares[8 * NDB :], 2)
-    store_halves([pack_half(squares[: 4 * NDB]), pack_half(squares[4 * NDB : 8 * NDB])], keep, send, places.border - places.strip)
+    needed = []
+    for tile in range(2 * NDB):
+        rows_here = squares[4 * tile : 4 * tile + 4]
+        count = BORDER_ROWS[tile % NDB]
+        needed += [jnp.where(x == 0, a, b) for a, b in zip(rows_here[:count], rows_here[4 - count :])]
+    middle = len(needed) // 2
+    store_halves([pack_half(needed[:middle]), pack_half(needed[middle:])], keep, send, places.border - places.strip)
     keep[: places.border - places.strip, :] = keep_more[...]
     send[: places.border - places.strip, :] = send_more[...]
     keep[:8, :] = keep_more[:8, :] + jnp.where(y == 0, *strips)
@@ -361,19 +375,24 @@
         self.strip = 2 * NDB * self.inner
         self.dirac = self.strip + 8
         self.border = self.dirac + rows * cols // LANES // 2
-        self.all = self.border + 2 * NDB * 4
+        self.all = self.border + 2 * sum(BORDER_ROWS)
 
 
 def half_duals(places, half, scale, u_inner, u_border, spread):
+    x = lax.axis_index("frow")
     for family in range(NDB):
         if isinstance(half, int):
             lanes = slice((half * NDB + family) * LANES, (half * NDB + family + 1) * LANES)
         else:
             lanes = pl.ds(pl.multiple_of((half * NDB + family) * LANES, LANES), LANES)
-        duals = []
-        for ref, base, count in ((u_inner, 0, places.inner), (u_border, places.border, 4)):
-            items = [(base + 8 * ((family * count + j) // 4), (family * count + j) % 4) for j in range(count)]
-            duals.append([ref[8 * j : 8 * j + 8, lanes] * widen(scale, *items[j]) for j in range(count)])
+        count = places.inner
+        factors = [widen(scale, 8 * ((family * count + j) // 4), (family * count + j) % 4) for j in range(count)]
+        inner = [u_inner[8 * j : 8 * j + 8, lanes] * factors[j] for j in range(count)]
+        first, count = sum(BORDER_ROWS[:family]), BORDER_ROWS[family]
+        factors = [widen(scale, places.border + 8 * (k // 4), k % 4) for k in range(first, first + count)]
+        spare = [jnp.zeros((8, LANES), F32)] * (4 - count)
+        factors = [jnp.where(x == 0, a, b) for a, b in zip(factors + spare, spare + factors)] if spare else factors
+        duals = inner, [u_border[8 * j : 8 * j + 8, lanes] * factors[j] for j in range(4)]
         spread_rows(*duals, row_taps(family, (1, 2), 1.0), spread, slice(family * LANES, (family + 1) * LANES))
 
 
@@ -454,22 +473,30 @@
     pairs = [(f, b) for b in range(2) for f in range(NDB)]
     for tile, (f, b) in enumerate(pairs):
         base = fixed_taps(f, b, row - 2 * (lane - 2) + len(DAUBECHIES[f]) // 2 - 1)
-        for block in rows:
+        for block in range(blocks):
             value = pltpu.roll(base, (block * NEAR // 2 - 2) % LANES, 1)
-            if block <= 0:
+            if block == 0:
                 value = jnp.where(lane < LANES // 2, value, 0.0)
-            if block >= blocks - 1:
+            if block == blocks - 1:
                 value = jnp.where(lane < LANES // 2, 0.0, value)
             put(block, tile, value)
+
+    def chosen(block, position, tile_of):
+        value = jnp.zeros((NEAR, LANES), F32)
+        for tile, (f, b) in enumerate(pairs):
+            part = fixed_taps(f, b, row + block * NEAR - 2 * position + len(DAUBECHIES[f]) // 2 - 1)
+            value = jnp.where(tile_of == tile, part, value)
+        return value
+
     column = lane % 4
     position = jnp.where(column < 2, column - 2, column + cols // 2 - 2)
     for block in rows:
-        value = jnp.zeros((NEAR, LANES), F32)
-        if block in (-1, 0, blocks - 1, blocks):
-            for tile, (f, b) in enumerate(pairs):
-                part = fixed_taps(f, b, row + block * NEAR - 2 * position + len(DAUBECHIES[f]) // 2 - 1)
-                value = jnp.where(lane // 4 == tile, part, value)
-        put(block, len(pairs), value)
+        inside = block in (-1, 0, blocks - 1, blocks)
+        put(block, len(pairs), chosen(block, position, lane // 4) if inside else jnp.zeros((NEAR, LANES), F32))
+    column = lane % NEAR
+    position = jnp.where(column < NEAR // 2, column, column + cols // 2 - NEAR)
+    for block in (-1, blocks):
+        put(block, 0, chosen(block, position, lane // NEAR))
 
 
 def rows_kernel(own, *refs):

time: 28 us -> 27.7 us (0.989)
  waiting for transfers between devices: 7.97 us -> 7.42 us
  starting transfers between devices: 13.3 us -> 13.7 us
    ppermute x8, waiting for transfers between devices: 7.97 us -> 7.42 us  [exchange(): return lax.ppermute(values, axis, [(i, i ^ bit) for i in range(count)])]
    ppermute x8, starting transfers between devices: 13.3 us -> 13.7 us  [exchange(): return lax.ppermute(values, axis, [(i, i ^ bit) for i in range(count)])]
where the time goes in v5:
time: 27.7 us; the launch traced here: 27.6 us
  starting transfers between devices  13.7 us (49%)
  waiting for transfers between devices  7.42 us (27%)
  Pallas kernels  5.52 us (20%)
  local copies, waits for them, and re-layouts  0.91 us (3%)
    ppermute x8, starting transfers between devices, exchange(): return lax.ppermute(values, axis, [(i, i ^ bit) for i in range(count)])  13.7 us
    ppermute x8, waiting for transfers between devices, exchange(): return lax.ppermute(values, axis, [(i, i ^ bit) for i in range(count)])  7.42 us
    pallas_call x10, Pallas kernels, call(): pl.pallas_call(kernel, name=name, out_shape=many, in_specs=vmem(len(opera...  5.52 us
    unnamed x4, local copies, waits for them, and re-layouts  0.91 us
  transfers between devices with their start and end apart: 8, of which 5 were waited for; matrix products, arithmetic and copies ran while one was open for 0% of the time, Pallas kernels for 15%

profile of v5, /device:TPU:0, one launch (start us, length us, event | category | flops | bytes accessed | tf_op | source)
XLA Modules:
  0.0 27.6 jit_solution(6141762331633724481)
XLA Ops:
  0.0 0.5 %collective-permute-start.1 = (f32[4,32,256]{2,1,0:T(8,128)}, f32[4,32,256]{2,1,0:T(8,128)S(1)}, u32[]{:S(2)}, u32[]{:S(2)}) collective-permute-start(f32[4,32,256]{2,1,0:T(8,128)} %dirty.1), channel_id=1, source_target_pairs={{0,8},{8,0},{1,9},{9,1},{2,10},{10,2},{3,11},{11,3},{4,12},{12,4},... | collective-permute-start | bytes 393224 | tf_op jit(solution)/shard_map/ppermute | solution.py:533
  0.5 0.9 %copy-done = f32[4,32,256]{2,1,0:T(8,128)S(1)} copy-done((f32[4,32,256]{2,1,0:T(8,128)S(1)}, f32[4,32,256]{2,1,0:T(8,128)}, u32[]{:S(2)}) %copy-start) | copy-done | bytes 131096
  1.4 0.5 %hold.1 = (f32[4,32,256]{2,1,0:T(8,128)S(1)}, bf16[2,288,1152]{2,1,0:T(8,128)(2,1)S(1)}) custom-call(f32[4,32,256]{2,1,0:T(8,128)S(1)} %copy-done), custom_call_target="tpu_custom_call" | custom-call | tf_op jit(solution)/shard_map/hold/pallas_call | solution.py:542
  1.8 0.0 collective-permute-done.1.refs_0_.refs_4_
  1.8 0.2 rows.1
  2.0 2.6 %collective-permute-start.2 = (f32[72,128]{1,0:T(8,128)S(1)}, f32[72,128]{1,0:T(8,128)S(1)}, u32[]{:S(2)}, u32[]{:S(2)}) collective-permute-start(f32[72,128]{1,0:T(8,128)S(1)} %rows.1), channel_id=1, source_target_pairs={{0,16},{16,0},{1,17},{17,1},{2,18},{18,2},{3,19},{19,3},{4,20},{20... | collective-permute-start | bytes 110600 | tf_op jit(solution)/shard_map/ppermute | solution.py:533
  4.6 0.9 %inner.1 = (f32[112,1152]{1,0:T(8,128)S(1)}, f32[112,128]{1,0:T(8,128)S(1)}, f32[112,128]{1,0:T(8,128)S(1)}, f32[40,128]{1,0:T(8,128)S(1)}, f32[40,128]{1,0:T(8,128)S(1)}) custom-call(f32[4,32,256]{2,1,0:T(8,128)S(1)} %get-tuple-element.15.refs_0_.own, f32[4,32,256]{2,1,0:T(8,128)S(1)} %collective-permute-done.1.refs_0_.refs_4_, ...), custom_call_target="tpu_custom_call" | custom-call | tf_op jit(solution)/shard_map/inner/pallas_call | solution.py:542
  5.5 1.6 %collective-permute-start.3 = (f32[112,128]{1,0:T(8,128)S(1)}, f32[112,128]{1,0:T(8,128)S(1)}, u32[]{:S(2)}, u32[]{:S(2)}) collective-permute-start(f32[112,128]{1,0:T(8,128)S(1)} %get-tuple-element.22), channel_id=1, source_target_pairs={{0,1},{1,0},{2,3},{3,2},{4,5},{5,4},{6,7},{7,6},{8,9},{9,8},{10,11... | collective-permute-start | bytes 172040 | tf_op jit(solution)/shard_map/ppermute | solution.py:533
  7.1 0.0 collective-permute-done.2.refs_1_
  7.1 0.6 %border.1 = (f32[32,1152]{1,0:T(8,128)S(1)}, f32[64,128]{1,0:T(8,128)S(1)}, f32[64,128]{1,0:T(8,128)S(1)}) custom-call(f32[4,32,256]{2,1,0:T(8,128)S(1)} %get-tuple-element.15.refs_0_.own, f32[72,128]{1,0:T(8,128)S(1)} %collective-permute-done.2.refs_1_, f32[40,128]{1,0:T(8,128)S(1)} %get-tuple-element.18.refs_2_, f32[40,128]{1,0:T(8,128)S(1)} %get-tuple-element.19.refs_3_, ...), custom_call_target="tpu_custom_call" | custom-call | tf_op jit(solution)/shard_map/border/pallas_call | solution.py:542
  7.7 1.6 %collective-permute-start.4 = (f32[64,128]{1,0:T(8,128)S(1)}, f32[64,128]{1,0:T(8,128)S(1)}, u32[]{:S(2)}, u32[]{:S(2)}) collective-permute-start(f32[64,128]{1,0:T(8,128)S(1)} %get-tuple-element.24), channel_id=1, source_target_pairs={{0,1},{1,0},{2,3},{3,2},{4,5},{5,4},{6,7},{7,6},{8,9},{9,8},{10,11... | collective-permute-start | bytes 98312 | tf_op jit(solution)/shard_map/ppermute | solution.py:533
  9.3 0.5 %collective-permute-done.3.two = f32[112,128]{1,0:T(8,128)S(1)} collective-permute-done((f32[112,128]{1,0:T(8,128)S(1)}, f32[112,128]{1,0:T(8,128)S(1)}, u32[]{:S(2)}, u32[]{:S(2)}) %collective-permute-start.3) | collective-permute-done | bytes 57376 | tf_op jit(solution)/shard_map/ppermute | solution.py:533
  9.8 1.9 %collective-permute-done.4.four = f32[64,128]{1,0:T(8,128)S(1)} collective-permute-done((f32[64,128]{1,0:T(8,128)S(1)}, f32[64,128]{1,0:T(8,128)S(1)}, u32[]{:S(2)}, u32[]{:S(2)}) %collective-permute-start.4) | collective-permute-done | bytes 32800 | tf_op jit(solution)/shard_map/ppermute | solution.py:533
  11.7 1.6 %collective-permute-start.5 = (f32[176,128]{1,0:T(8,128)S(1)}, f32[176,128]{1,0:T(8,128)S(1)}, u32[]{:S(2)}, u32[]{:S(2)}) collective-permute-start(f32[176,128]{1,0:T(8,128)S(1)} %add.3.one), channel_id=1, source_target_pairs={{0,2},{1,3},{2,0},{3,1},{4,6},{5,7},{6,4},{7,5},{8,10},{9,11},{10,... | collective-permute-start | bytes 270344 | tf_op jit(solution)/shard_map/ppermute | solution.py:533
  13.3 1.5 %collective-permute-start = (f32[4,32,256]{2,1,0:T(8,128)S(1)}, f32[4,32,256]{2,1,0:T(8,128)S(1)}, u32[]{:S(2)}, u32[]{:S(2)}) collective-permute-start(f32[4,32,256]{2,1,0:T(8,128)S(1)} %get-tuple-element.15.refs_0_.own), channel_id=1, source_target_pairs={{0,1},{1,0},{2,3},{3,2},{4,5},{5,4},{6,7},{7,6},{8,9},{9,8},{10,11... | collective-permute-start | bytes 393224 | tf_op jit(solution)/shard_map/ppermute | solution.py:533
  14.8 1.4 %collective-permute-done.5.two = f32[176,128]{1,0:T(8,128)S(1)} collective-permute-done((f32[176,128]{1,0:T(8,128)S(1)}, f32[176,128]{1,0:T(8,128)S(1)}, u32[]{:S(2)}, u32[]{:S(2)}) %collective-permute-start.5) | collective-permute-done | bytes 90144 | tf_op jit(solution)/shard_map/ppermute | solution.py:533
  16.3 2.7 %collective-permute-start.6 = (f32[176,128]{1,0:T(8,128)S(1)}, f32[176,128]{1,0:T(8,128)S(1)}, u32[]{:S(2)}, u32[]{:S(2)}) collective-permute-start(f32[176,128]{1,0:T(8,128)S(1)} %add.4.one), channel_id=1, source_target_pairs={{0,4},{1,5},{2,6},{3,7},{4,0},{5,1},{6,2},{7,3},{8,12},{9,13},{10,... | collective-permute-start | bytes 270344 | tf_op jit(solution)/shard_map/ppermute | solution.py:533
  19.0 0.0 collective-permute-done.refs_1_
  19.0 1.8 %nuclear.1.refs_0_.refs_2_ = f32[4,32,256]{2,1,0:T(8,128)S(1)} custom-call(f32[4,32,256]{2,1,0:T(8,128)S(1)} %get-tuple-element.15.refs_0_.own, f32[4,32,256]{2,1,0:T(8,128)S(1)} %collective-permute-done.refs_1_), custom_call_target="tpu_custom_call" | custom-call | tf_op jit(solution)/shard_map/nuclear/pallas_call | solution.py:542
  20.8 1.0 %collective-permute-done.6.two = f32[176,128]{1,0:T(8,128)S(1)} collective-permute-done((f32[176,128]{1,0:T(8,128)S(1)}, f32[176,128]{1,0:T(8,128)S(1)}, u32[]{:S(2)}, u32[]{:S(2)}) %collective-permute-start.6) | collective-permute-done | bytes 90144 | tf_op jit(solution)/shard_map/ppermute | solution.py:533
  21.8 1.6 %collective-permute-start.7 = (f32[176,128]{1,0:T(8,128)S(1)}, f32[176,128]{1,0:T(8,128)S(1)}, u32[]{:S(2)}, u32[]{:S(2)}) collective-permute-start(f32[176,128]{1,0:T(8,128)S(1)} %add.5.refs_5_.refs_4_), channel_id=1, source_target_pairs={{0,1},{1,0},{2,3},{3,2},{4,5},{5,4},{6,7},{7,6},{8,9},{9,8},{10,11... | collective-permute-start | bytes 270344 | tf_op jit(solution)/shard_map/ppermute | solution.py:533
  23.4 0.4 %first.1.refs_1_ = f32[4,128,128]{2,1,0:T(8,128)S(1)} custom-call(f32[4,32,256]{2,1,0:T(8,128)S(1)} %get-tuple-element.15.refs_0_.own, f32[4,32,256]{2,1,0:T(8,128)S(1)} %copy-done.1, f32[4,32,256]{2,1,0:T(8,128)S(1)} %nuclear.1.refs_0_.refs_2_, f32[112,1152]{1,0:T(8,128)S(1)} %get-tuple-element.17.refs_3_.refs_2_, ...), custom_call_target="tpu_custom_call" | custom-call | tf_op jit(solution)/shard_map/first/pallas_call | solution.py:542
  23.8 2.6 %collective-permute-done.7.refs_5_ = f32[176,128]{1,0:T(8,128)S(1)} collective-permute-done((f32[176,128]{1,0:T(8,128)S(1)}, f32[176,128]{1,0:T(8,128)S(1)}, u32[]{:S(2)}, u32[]{:S(2)}) %collective-permute-start.7) | collective-permute-done | bytes 90144 | tf_op jit(solution)/shard_map/ppermute | solution.py:533
  26.4 1.2 %second.1 = f32[4,32,256]{2,1,0:T(8,128)} custom-call(f32[4,32,256]{2,1,0:T(8,128)S(1)} %get-tuple-element.15.refs_0_.own, f32[4,128,128]{2,1,0:T(8,128)S(1)} %first.1.refs_1_, f32[112,1152]{1,0:T(8,128)S(1)} %get-tuple-element.17.refs_3_.refs_2_, f32[32,1152]{1,0:T(8,128)S(1)} %get-tuple-element.20.refs_4_.refs_3_, f32[176,128]{1,0:T(8,128)S(1)} %add.5.refs_5_.refs_4_, ...), custom_call_target="tpu_custom_call" | custom-call | tf_op jit(solution)/shard_map/second/pallas_call | solution.py:542
  (6 shorter events, 0.0 us)
Async XLA Ops:
  0.0 1.8 %collective-permute-start.1 = (f32[4,32,256]{2,1,0:T(8,128)}, f32[4,32,256]{2,1,0:T(8,128)S(1)}, u32[]{:S(2)}, u32[]{:S(2)}) collective-permute-start(f32[4,32,256]{2,1,0:T(8,128)} %dirty.1), channel_id=1, source_target_pairs={{0,8},{8,0},{1,9},{9,1},{2,10},{10,2},{3,11},{11,3},{4,12},{12,4},... | collective-permute-start | bytes 393224 | tf_op jit(solution)/shard_map/ppermute | solution.py:533
  0.5 0.9 %copy-start = (f32[4,32,256]{2,1,0:T(8,128)S(1)}, f32[4,32,256]{2,1,0:T(8,128)}, u32[]{:S(2)}) copy-start(f32[4,32,256]{2,1,0:T(8,128)} %dirty.1) | copy-start | bytes 393220
  2.0 5.1 %collective-permute-start.2 = (f32[72,128]{1,0:T(8,128)S(1)}, f32[72,128]{1,0:T(8,128)S(1)}, u32[]{:S(2)}, u32[]{:S(2)}) collective-permute-start(f32[72,128]{1,0:T(8,128)S(1)} %rows.1), channel_id=1, source_target_pairs={{0,16},{16,0},{1,17},{17,1},{2,18},{18,2},{3,19},{19,3},{4,20},{20... | collective-permute-start | bytes 110600 | tf_op jit(solution)/shard_map/ppermute | solution.py:533
  5.5 4.2 %collective-permute-start.3 = (f32[112,128]{1,0:T(8,128)S(1)}, f32[112,128]{1,0:T(8,128)S(1)}, u32[]{:S(2)}, u32[]{:S(2)}) collective-permute-start(f32[112,128]{1,0:T(8,128)S(1)} %get-tuple-element.22), channel_id=1, source_target_pairs={{0,1},{1,0},{2,3},{3,2},{4,5},{5,4},{6,7},{7,6},{8,9},{9,8},{10,11... | collective-permute-start | bytes 172040 | tf_op jit(solution)/shard_map/ppermute | solution.py:533
  7.1 16.3 %copy-start.1 = (f32[4,32,256]{2,1,0:T(8,128)S(1)}, f32[4,32,256]{2,1,0:T(8,128)}, u32[]{:S(2)}) copy-start(f32[4,32,256]{2,1,0:T(8,128)} %refs_1_.1) | copy-start | bytes 393220
  7.7 4.0 %collective-permute-start.4 = (f32[64,128]{1,0:T(8,128)S(1)}, f32[64,128]{1,0:T(8,128)S(1)}, u32[]{:S(2)}, u32[]{:S(2)}) collective-permute-start(f32[64,128]{1,0:T(8,128)S(1)} %get-tuple-element.24), channel_id=1, source_target_pairs={{0,1},{1,0},{2,3},{3,2},{4,5},{5,4},{6,7},{7,6},{8,9},{9,8},{10,11... | collective-permute-start | bytes 98312 | tf_op jit(solution)/shard_map/ppermute | solution.py:533
  11.7 4.6 %collective-permute-start.5 = (f32[176,128]{1,0:T(8,128)S(1)}, f32[176,128]{1,0:T(8,128)S(1)}, u32[]{:S(2)}, u32[]{:S(2)}) collective-permute-start(f32[176,128]{1,0:T(8,128)S(1)} %add.3.one), channel_id=1, source_target_pairs={{0,2},{1,3},{2,0},{3,1},{4,6},{5,7},{6,4},{7,5},{8,10},{9,11},{10,... | collective-permute-start | bytes 270344 | tf_op jit(solution)/shard_map/ppermute | solution.py:533
  13.3 5.6 %collective-permute-start = (f32[4,32,256]{2,1,0:T(8,128)S(1)}, f32[4,32,256]{2,1,0:T(8,128)S(1)}, u32[]{:S(2)}, u32[]{:S(2)}) collective-permute-start(f32[4,32,256]{2,1,0:T(8,128)S(1)} %get-tuple-element.15.refs_0_.own), channel_id=1, source_target_pairs={{0,1},{1,0},{2,3},{3,2},{4,5},{5,4},{6,7},{7,6},{8,9},{9,8},{10,11... | collective-permute-start | bytes 393224 | tf_op jit(solution)/shard_map/ppermute | solution.py:533
  16.3 5.5 %collective-permute-start.6 = (f32[176,128]{1,0:T(8,128)S(1)}, f32[176,128]{1,0:T(8,128)S(1)}, u32[]{:S(2)}, u32[]{:S(2)}) collective-permute-start(f32[176,128]{1,0:T(8,128)S(1)} %add.4.one), channel_id=1, source_target_pairs={{0,4},{1,5},{2,6},{3,7},{4,0},{5,1},{6,2},{7,3},{8,12},{9,13},{10,... | collective-permute-start | bytes 270344 | tf_op jit(solution)/shard_map/ppermute | solution.py:533
  21.8 4.6 %collective-permute-start.7 = (f32[176,128]{1,0:T(8,128)S(1)}, f32[176,128]{1,0:T(8,128)S(1)}, u32[]{:S(2)}, u32[]{:S(2)}) collective-permute-start(f32[176,128]{1,0:T(8,128)S(1)} %add.5.refs_5_.refs_4_), channel_id=1, source_target_pairs={{0,1},{1,0},{2,3},{3,2},{4,5},{5,4},{6,7},{7,6},{8,9},{9,8},{10,11... | collective-permute-start | bytes 270344 | tf_op jit(solution)/shard_map/ppermute | solution.py:533

commit v6 on v5

--- a/solution.py
+++ b/solution.py
@@ -130,13 +130,18 @@
     return merge(merge(items[0], items[1], 1), merge(items[2], items[3], 1), 2)
 
 
-def near_columns(sources, c, at):
+def near_columns(sources, c, at, lane=0):
     def last(ref):
-        return pltpu.roll(ref[c, at, ref.shape[2] - LANES :], NEAR, 1)
-
-    if len(sources) == 1:
-        return [jnp.where(lax.axis_index("fcol") == 0, sources[0][c, at, :LANES], last(sources[0]))]
-    return [last(sources[0]), sources[1][c, at, :LANES]]
+        return pltpu.roll(ref[c, at, ref.shape[2] - LANES :], lane + NEAR, 1)
+
+    def first(ref):
+        return pltpu.roll(ref[c, at, :LANES], lane, 1) if lane else ref[c, at, :LANES]
+
+    if len(sources) > 1:
+        return [last(sources[0]), first(sources[1])]
+    place = lax.axis_index("fcol")
+    start = pl.multiple_of(place * (sources[0].shape[2] - LANES), LANES)
+    return [pltpu.roll(sources[0][c, at, pl.ds(start, LANES)], lane + NEAR * place, 1)]
 
 
 def fill_rows(ext, row, count, start, own, around):
@@ -416,7 +421,8 @@
     channels, rows, cols = raw.shape
     y = lax.axis_index("chan") % 2
     places = Places(rows, cols)
-    scale[y] = scales(limit, mine[...])
+    both = slice(places.strip, places.border)
+    scale[y, both, :] = scales(limit, mine[both, :])
     scale[1 - y] = scales(limit, theirs[...])
     half_duals(places, 1 - y, scale.at[1 - y], u_inner, u_border, spread)
     main = 2 * NDB * LANES
@@ -511,8 +517,8 @@
     lane = lax.broadcasted_iota(jnp.int32, (HALO, LANES), 1) // NEAR
     totals = near_columns(around, 0, start)
     for c in range(1, channels):
-        parts = near_columns(around, c, start)
-        totals = [jnp.where(lane == c, pltpu.roll(part, NEAR * c, 1), total) for part, total in zip(parts, totals)]
+        parts = near_columns(around, c, start, NEAR * c)
+        totals = [jnp.where(lane == c, part, total) for part, total in zip(parts, totals)]
     for total in totals:
         edge[at : at + HALO, :] = total
         at += HALO

time: 27.7 us -> 27.7 us (level)
  no operation moved by 1% of the time
where the time goes in v6:
time: 27.7 us; the launch traced here: 27.5 us
  starting transfers between devices  13.7 us (49%)
  waiting for transfers between devices  7.45 us (27%)
  Pallas kernels  5.44 us (20%)
  local copies, waits for them, and re-layouts  0.91 us (3%)
    ppermute x8, starting transfers between devices, exchange(): return lax.ppermute(values, axis, [(i, i ^ bit) for i in range(count)])  13.7 us
    ppermute x8, waiting for transfers between devices, exchange(): return lax.ppermute(values, axis, [(i, i ^ bit) for i in range(count)])  7.45 us
    pallas_call x10, Pallas kernels, call(): pl.pallas_call(kernel, name=name, out_shape=many, in_specs=vmem(len(opera...  5.44 us
    unnamed x4, local copies, waits for them, and re-layouts  0.91 us
  transfers between devices with their start and end apart: 8, of which 5 were waited for; matrix products, arithmetic and copies ran while one was open for 0% of the time, Pallas kernels for 15%

profile of v6, /device:TPU:0, one launch (start us, length us, event | category | flops | bytes accessed | tf_op | source)
XLA Modules:
  0.0 27.5 jit_solution(1666505143557397285)
XLA Ops:
  0.0 0.5 %collective-permute-start.1 = (f32[4,32,256]{2,1,0:T(8,128)}, f32[4,32,256]{2,1,0:T(8,128)S(1)}, u32[]{:S(2)}, u32[]{:S(2)}) collective-permute-start(f32[4,32,256]{2,1,0:T(8,128)} %dirty.1), channel_id=1, source_target_pairs={{0,8},{8,0},{1,9},{9,1},{2,10},{10,2},{3,11},{11,3},{4,12},{12,4},... | collective-permute-start | bytes 393224 | tf_op jit(solution)/shard_map/ppermute | solution.py:539
  0.5 0.9 %copy-done = f32[4,32,256]{2,1,0:T(8,128)S(1)} copy-done((f32[4,32,256]{2,1,0:T(8,128)S(1)}, f32[4,32,256]{2,1,0:T(8,128)}, u32[]{:S(2)}) %copy-start) | copy-done | bytes 131096
  1.4 0.5 %hold.1 = (f32[4,32,256]{2,1,0:T(8,128)S(1)}, bf16[2,288,1152]{2,1,0:T(8,128)(2,1)S(1)}) custom-call(f32[4,32,256]{2,1,0:T(8,128)S(1)} %copy-done), custom_call_target="tpu_custom_call" | custom-call | tf_op jit(solution)/shard_map/hold/pallas_call | solution.py:548
  1.8 0.0 collective-permute-done.1.refs_0_.refs_4_
  1.8 0.1 rows.1
  1.9 2.7 %collective-permute-start.2 = (f32[72,128]{1,0:T(8,128)S(1)}, f32[72,128]{1,0:T(8,128)S(1)}, u32[]{:S(2)}, u32[]{:S(2)}) collective-permute-start(f32[72,128]{1,0:T(8,128)S(1)} %rows.1), channel_id=1, source_target_pairs={{0,16},{16,0},{1,17},{17,1},{2,18},{18,2},{3,19},{19,3},{4,20},{20... | collective-permute-start | bytes 110600 | tf_op jit(solution)/shard_map/ppermute | solution.py:539
  4.6 0.9 %inner.1 = (f32[112,1152]{1,0:T(8,128)S(1)}, f32[112,128]{1,0:T(8,128)S(1)}, f32[112,128]{1,0:T(8,128)S(1)}, f32[40,128]{1,0:T(8,128)S(1)}, f32[40,128]{1,0:T(8,128)S(1)}) custom-call(f32[4,32,256]{2,1,0:T(8,128)S(1)} %get-tuple-element.15.refs_0_.own, f32[4,32,256]{2,1,0:T(8,128)S(1)} %collective-permute-done.1.refs_0_.refs_4_, ...), custom_call_target="tpu_custom_call" | custom-call | tf_op jit(solution)/shard_map/inner/pallas_call | solution.py:548
  5.5 1.6 %collective-permute-start.3 = (f32[112,128]{1,0:T(8,128)S(1)}, f32[112,128]{1,0:T(8,128)S(1)}, u32[]{:S(2)}, u32[]{:S(2)}) collective-permute-start(f32[112,128]{1,0:T(8,128)S(1)} %get-tuple-element.22), channel_id=1, source_target_pairs={{0,1},{1,0},{2,3},{3,2},{4,5},{5,4},{6,7},{7,6},{8,9},{9,8},{10,11... | collective-permute-start | bytes 172040 | tf_op jit(solution)/shard_map/ppermute | solution.py:539
  7.1 0.0 collective-permute-done.2.refs_1_
  7.1 0.6 %border.1 = (f32[32,1152]{1,0:T(8,128)S(1)}, f32[64,128]{1,0:T(8,128)S(1)}, f32[64,128]{1,0:T(8,128)S(1)}) custom-call(f32[4,32,256]{2,1,0:T(8,128)S(1)} %get-tuple-element.15.refs_0_.own, f32[72,128]{1,0:T(8,128)S(1)} %collective-permute-done.2.refs_1_, f32[40,128]{1,0:T(8,128)S(1)} %get-tuple-element.18.refs_2_, f32[40,128]{1,0:T(8,128)S(1)} %get-tuple-element.19.refs_3_, ...), custom_call_target="tpu_custom_call" | custom-call | tf_op jit(solution)/shard_map/border/pallas_call | solution.py:548
  7.6 1.6 %collective-permute-start.4 = (f32[64,128]{1,0:T(8,128)S(1)}, f32[64,128]{1,0:T(8,128)S(1)}, u32[]{:S(2)}, u32[]{:S(2)}) collective-permute-start(f32[64,128]{1,0:T(8,128)S(1)} %get-tuple-element.24), channel_id=1, source_target_pairs={{0,1},{1,0},{2,3},{3,2},{4,5},{5,4},{6,7},{7,6},{8,9},{9,8},{10,11... | collective-permute-start | bytes 98312 | tf_op jit(solution)/shard_map/ppermute | solution.py:539
  9.2 0.5 %collective-permute-done.3.two = f32[112,128]{1,0:T(8,128)S(1)} collective-permute-done((f32[112,128]{1,0:T(8,128)S(1)}, f32[112,128]{1,0:T(8,128)S(1)}, u32[]{:S(2)}, u32[]{:S(2)}) %collective-permute-start.3) | collective-permute-done | bytes 57376 | tf_op jit(solution)/shard_map/ppermute | solution.py:539
  9.7 1.9 %collective-permute-done.4.four = f32[64,128]{1,0:T(8,128)S(1)} collective-permute-done((f32[64,128]{1,0:T(8,128)S(1)}, f32[64,128]{1,0:T(8,128)S(1)}, u32[]{:S(2)}, u32[]{:S(2)}) %collective-permute-start.4) | collective-permute-done | bytes 32800 | tf_op jit(solution)/shard_map/ppermute | solution.py:539
  11.6 1.6 %collective-permute-start.5 = (f32[176,128]{1,0:T(8,128)S(1)}, f32[176,128]{1,0:T(8,128)S(1)}, u32[]{:S(2)}, u32[]{:S(2)}) collective-permute-start(f32[176,128]{1,0:T(8,128)S(1)} %add.3.one), channel_id=1, source_target_pairs={{0,2},{1,3},{2,0},{3,1},{4,6},{5,7},{6,4},{7,5},{8,10},{9,11},{10,... | collective-permute-start | bytes 270344 | tf_op jit(solution)/shard_map/ppermute | solution.py:539
  13.3 1.5 %collective-permute-start = (f32[4,32,256]{2,1,0:T(8,128)S(1)}, f32[4,32,256]{2,1,0:T(8,128)S(1)}, u32[]{:S(2)}, u32[]{:S(2)}) collective-permute-start(f32[4,32,256]{2,1,0:T(8,128)S(1)} %get-tuple-element.15.refs_0_.own), channel_id=1, source_target_pairs={{0,1},{1,0},{2,3},{3,2},{4,5},{5,4},{6,7},{7,6},{8,9},{9,8},{10,11... | collective-permute-start | bytes 393224 | tf_op jit(solution)/shard_map/ppermute | solution.py:539
  14.8 1.4 %collective-permute-done.5.two = f32[176,128]{1,0:T(8,128)S(1)} collective-permute-done((f32[176,128]{1,0:T(8,128)S(1)}, f32[176,128]{1,0:T(8,128)S(1)}, u32[]{:S(2)}, u32[]{:S(2)}) %collective-permute-start.5) | collective-permute-done | bytes 90144 | tf_op jit(solution)/shard_map/ppermute | solution.py:539
  16.2 2.7 %collective-permute-start.6 = (f32[176,128]{1,0:T(8,128)S(1)}, f32[176,128]{1,0:T(8,128)S(1)}, u32[]{:S(2)}, u32[]{:S(2)}) collective-permute-start(f32[176,128]{1,0:T(8,128)S(1)} %add.4.one), channel_id=1, source_target_pairs={{0,4},{1,5},{2,6},{3,7},{4,0},{5,1},{6,2},{7,3},{8,12},{9,13},{10,... | collective-permute-start | bytes 270344 | tf_op jit(solution)/shard_map/ppermute | solution.py:539
  18.9 0.0 collective-permute-done.refs_1_
  18.9 1.8 %nuclear.1.refs_0_.refs_2_ = f32[4,32,256]{2,1,0:T(8,128)S(1)} custom-call(f32[4,32,256]{2,1,0:T(8,128)S(1)} %get-tuple-element.15.refs_0_.own, f32[4,32,256]{2,1,0:T(8,128)S(1)} %collective-permute-done.refs_1_), custom_call_target="tpu_custom_call" | custom-call | tf_op jit(solution)/shard_map/nuclear/pallas_call | solution.py:548
  20.7 1.0 %collective-permute-done.6.two = f32[176,128]{1,0:T(8,128)S(1)} collective-permute-done((f32[176,128]{1,0:T(8,128)S(1)}, f32[176,128]{1,0:T(8,128)S(1)}, u32[]{:S(2)}, u32[]{:S(2)}) %collective-permute-start.6) | collective-permute-done | bytes 90144 | tf_op jit(solution)/shard_map/ppermute | solution.py:539
  21.8 1.6 %collective-permute-start.7 = (f32[176,128]{1,0:T(8,128)S(1)}, f32[176,128]{1,0:T(8,128)S(1)}, u32[]{:S(2)}, u32[]{:S(2)}) collective-permute-start(f32[176,128]{1,0:T(8,128)S(1)} %add.5.refs_5_.refs_4_), channel_id=1, source_target_pairs={{0,1},{1,0},{2,3},{3,2},{4,5},{5,4},{6,7},{7,6},{8,9},{9,8},{10,11... | collective-permute-start | bytes 270344 | tf_op jit(solution)/shard_map/ppermute | solution.py:539
  23.3 0.4 %first.1.refs_1_ = f32[4,128,128]{2,1,0:T(8,128)S(1)} custom-call(f32[4,32,256]{2,1,0:T(8,128)S(1)} %get-tuple-element.15.refs_0_.own, f32[4,32,256]{2,1,0:T(8,128)S(1)} %copy-done.1, f32[4,32,256]{2,1,0:T(8,128)S(1)} %nuclear.1.refs_0_.refs_2_, f32[112,1152]{1,0:T(8,128)S(1)} %get-tuple-element.17.refs_3_.refs_2_, ...), custom_call_target="tpu_custom_call" | custom-call | tf_op jit(solution)/shard_map/first/pallas_call | solution.py:548
  23.7 2.6 %collective-permute-done.7.refs_5_ = f32[176,128]{1,0:T(8,128)S(1)} collective-permute-done((f32[176,128]{1,0:T(8,128)S(1)}, f32[176,128]{1,0:T(8,128)S(1)}, u32[]{:S(2)}, u32[]{:S(2)}) %collective-permute-start.7) | collective-permute-done | bytes 90144 | tf_op jit(solution)/shard_map/ppermute | solution.py:539
  26.4 1.2 %second.1 = f32[4,32,256]{2,1,0:T(8,128)} custom-call(f32[4,32,256]{2,1,0:T(8,128)S(1)} %get-tuple-element.15.refs_0_.own, f32[4,128,128]{2,1,0:T(8,128)S(1)} %first.1.refs_1_, f32[112,1152]{1,0:T(8,128)S(1)} %get-tuple-element.17.refs_3_.refs_2_, f32[32,1152]{1,0:T(8,128)S(1)} %get-tuple-element.20.refs_4_.refs_3_, f32[176,128]{1,0:T(8,128)S(1)} %add.5.refs_5_.refs_4_, ...), custom_call_target="tpu_custom_call" | custom-call | tf_op jit(solution)/shard_map/second/pallas_call | solution.py:548
  (6 shorter events, 0.0 us)
Async XLA Ops:
  0.0 1.8 %collective-permute-start.1 = (f32[4,32,256]{2,1,0:T(8,128)}, f32[4,32,256]{2,1,0:T(8,128)S(1)}, u32[]{:S(2)}, u32[]{:S(2)}) collective-permute-start(f32[4,32,256]{2,1,0:T(8,128)} %dirty.1), channel_id=1, source_target_pairs={{0,8},{8,0},{1,9},{9,1},{2,10},{10,2},{3,11},{11,3},{4,12},{12,4},... | collective-permute-start | bytes 393224 | tf_op jit(solution)/shard_map/ppermute | solution.py:539
  0.5 0.9 %copy-start = (f32[4,32,256]{2,1,0:T(8,128)S(1)}, f32[4,32,256]{2,1,0:T(8,128)}, u32[]{:S(2)}) copy-start(f32[4,32,256]{2,1,0:T(8,128)} %dirty.1) | copy-start | bytes 393220
  1.9 5.1 %collective-permute-start.2 = (f32[72,128]{1,0:T(8,128)S(1)}, f32[72,128]{1,0:T(8,128)S(1)}, u32[]{:S(2)}, u32[]{:S(2)}) collective-permute-start(f32[72,128]{1,0:T(8,128)S(1)} %rows.1), channel_id=1, source_target_pairs={{0,16},{16,0},{1,17},{17,1},{2,18},{18,2},{3,19},{19,3},{4,20},{20... | collective-permute-start | bytes 110600 | tf_op jit(solution)/shard_map/ppermute | solution.py:539
  5.5 4.2 %collective-permute-start.3 = (f32[112,128]{1,0:T(8,128)S(1)}, f32[112,128]{1,0:T(8,128)S(1)}, u32[]{:S(2)}, u32[]{:S(2)}) collective-permute-start(f32[112,128]{1,0:T(8,128)S(1)} %get-tuple-element.22), channel_id=1, source_target_pairs={{0,1},{1,0},{2,3},{3,2},{4,5},{5,4},{6,7},{7,6},{8,9},{9,8},{10,11... | collective-permute-start | bytes 172040 | tf_op jit(solution)/shard_map/ppermute | solution.py:539
  7.1 16.3 %copy-start.1 = (f32[4,32,256]{2,1,0:T(8,128)S(1)}, f32[4,32,256]{2,1,0:T(8,128)}, u32[]{:S(2)}) copy-start(f32[4,32,256]{2,1,0:T(8,128)} %refs_1_.1) | copy-start | bytes 393220
  7.6 4.0 %collective-permute-start.4 = (f32[64,128]{1,0:T(8,128)S(1)}, f32[64,128]{1,0:T(8,128)S(1)}, u32[]{:S(2)}, u32[]{:S(2)}) collective-permute-start(f32[64,128]{1,0:T(8,128)S(1)} %get-tuple-element.24), channel_id=1, source_target_pairs={{0,1},{1,0},{2,3},{3,2},{4,5},{5,4},{6,7},{7,6},{8,9},{9,8},{10,11... | collective-permute-start | bytes 98312 | tf_op jit(solution)/shard_map/ppermute | solution.py:539
  11.6 4.6 %collective-permute-start.5 = (f32[176,128]{1,0:T(8,128)S(1)}, f32[176,128]{1,0:T(8,128)S(1)}, u32[]{:S(2)}, u32[]{:S(2)}) collective-permute-start(f32[176,128]{1,0:T(8,128)S(1)} %add.3.one), channel_id=1, source_target_pairs={{0,2},{1,3},{2,0},{3,1},{4,6},{5,7},{6,4},{7,5},{8,10},{9,11},{10,... | collective-permute-start | bytes 270344 | tf_op jit(solution)/shard_map/ppermute | solution.py:539
  13.3 5.6 %collective-permute-start = (f32[4,32,256]{2,1,0:T(8,128)S(1)}, f32[4,32,256]{2,1,0:T(8,128)S(1)}, u32[]{:S(2)}, u32[]{:S(2)}) collective-permute-start(f32[4,32,256]{2,1,0:T(8,128)S(1)} %get-tuple-element.15.refs_0_.own), channel_id=1, source_target_pairs={{0,1},{1,0},{2,3},{3,2},{4,5},{5,4},{6,7},{7,6},{8,9},{9,8},{10,11... | collective-permute-start | bytes 393224 | tf_op jit(solution)/shard_map/ppermute | solution.py:539
  16.2 5.5 %collective-permute-start.6 = (f32[176,128]{1,0:T(8,128)S(1)}, f32[176,128]{1,0:T(8,128)S(1)}, u32[]{:S(2)}, u32[]{:S(2)}) collective-permute-start(f32[176,128]{1,0:T(8,128)S(1)} %add.4.one), channel_id=1, source_target_pairs={{0,4},{1,5},{2,6},{3,7},{4,0},{5,1},{6,2},{7,3},{8,12},{9,13},{10,... | collective-permute-start | bytes 270344 | tf_op jit(solution)/shard_map/ppermute | solution.py:539
  21.8 4.6 %collective-permute-start.7 = (f32[176,128]{1,0:T(8,128)S(1)}, f32[176,128]{1,0:T(8,128)S(1)}, u32[]{:S(2)}, u32[]{:S(2)}) collective-permute-start(f32[176,128]{1,0:T(8,128)S(1)} %add.5.refs_5_.refs_4_), channel_id=1, source_target_pairs={{0,1},{1,0},{2,3},{3,2},{4,5},{5,4},{6,7},{7,6},{8,9},{9,8},{10,11... | collective-permute-start | bytes 270344 | tf_op jit(solution)/shard_map/ppermute | solution.py:539

commit v7 on v6

--- a/solution.py
+++ b/solution.py
@@ -612,7 +612,7 @@
     bit = 2
     while bit < chans:
         received = exchange(total, "chan", bit)
-        total = call(add_kernel, "add", [(places.all, LANES)], [total, received], later=[] if 2 * bit < chans else [nuclear])
+        total = call(add_kernel, "add", [(places.all, LANES)], [total, received])
         bit *= 2
     theirs = exchange(total, "chan", 1)
     step = call(

time: 27.7 us -> 27.7 us (level)
  transfers between devices with their start and end apart: 8 -> 8, of which waited for: 5 -> 6; matrix products, arithmetic and copies ran while one was open for 0% -> 0% of each run, Pallas kernels for 15% -> 15%
where the time goes in v7:
time: 27.7 us; the launch traced here: 27.5 us
  starting transfers between devices  13.7 us (49%)
  waiting for transfers between devices  7.38 us (27%)
  Pallas kernels  5.43 us (20%)
  local copies, waits for them, and re-layouts  0.91 us (3%)
    ppermute x8, starting transfers between devices, exchange(): return lax.ppermute(values, axis, [(i, i ^ bit) for i in range(count)])  13.7 us
    ppermute x8, waiting for transfers between devices, exchange(): return lax.ppermute(values, axis, [(i, i ^ bit) for i in range(count)])  7.38 us
    pallas_call x10, Pallas kernels, call(): pl.pallas_call(kernel, name=name, out_shape=many, in_specs=vmem(len(opera...  5.43 us
    unnamed x4, local copies, waits for them, and re-layouts  0.91 us
  transfers between devices with their start and end apart: 8, of which 6 were waited for; matrix products, arithmetic and copies ran while one was open for 0% of the time, Pallas kernels for 15%

profile of v7, /device:TPU:0, one launch (start us, length us, event | category | flops | bytes accessed | tf_op | source)
XLA Modules:
  0.0 27.5 jit_solution(11940820234418731448)
XLA Ops:
  0.0 0.5 %collective-permute-start.1 = (f32[4,32,256]{2,1,0:T(8,128)}, f32[4,32,256]{2,1,0:T(8,128)S(1)}, u32[]{:S(2)}, u32[]{:S(2)}) collective-permute-start(f32[4,32,256]{2,1,0:T(8,128)} %dirty.1), channel_id=1, source_target_pairs={{0,8},{8,0},{1,9},{9,1},{2,10},{10,2},{3,11},{11,3},{4,12},{12,4},... | collective-permute-start | bytes 393224 | tf_op jit(solution)/shard_map/ppermute | solution.py:539
  0.5 0.9 %copy-done = f32[4,32,256]{2,1,0:T(8,128)S(1)} copy-done((f32[4,32,256]{2,1,0:T(8,128)S(1)}, f32[4,32,256]{2,1,0:T(8,128)}, u32[]{:S(2)}) %copy-start) | copy-done | bytes 131096
  1.4 0.5 %hold.1 = (f32[4,32,256]{2,1,0:T(8,128)S(1)}, bf16[2,288,1152]{2,1,0:T(8,128)(2,1)S(1)}) custom-call(f32[4,32,256]{2,1,0:T(8,128)S(1)} %copy-done), custom_call_target="tpu_custom_call" | custom-call | tf_op jit(solution)/shard_map/hold/pallas_call | solution.py:548
  1.8 0.0 collective-permute-done.1.refs_0_.refs_4_
  1.8 0.1 rows.1
  1.9 2.7 %collective-permute-start.2 = (f32[72,128]{1,0:T(8,128)S(1)}, f32[72,128]{1,0:T(8,128)S(1)}, u32[]{:S(2)}, u32[]{:S(2)}) collective-permute-start(f32[72,128]{1,0:T(8,128)S(1)} %rows.1), channel_id=1, source_target_pairs={{0,16},{16,0},{1,17},{17,1},{2,18},{18,2},{3,19},{19,3},{4,20},{20... | collective-permute-start | bytes 110600 | tf_op jit(solution)/shard_map/ppermute | solution.py:539
  4.6 0.9 %inner.1 = (f32[112,1152]{1,0:T(8,128)S(1)}, f32[112,128]{1,0:T(8,128)S(1)}, f32[112,128]{1,0:T(8,128)S(1)}, f32[40,128]{1,0:T(8,128)S(1)}, f32[40,128]{1,0:T(8,128)S(1)}) custom-call(f32[4,32,256]{2,1,0:T(8,128)S(1)} %get-tuple-element.15.refs_0_.own, f32[4,32,256]{2,1,0:T(8,128)S(1)} %collective-permute-done.1.refs_0_.refs_4_, ...), custom_call_target="tpu_custom_call" | custom-call | tf_op jit(solution)/shard_map/inner/pallas_call | solution.py:548
  5.5 1.6 %collective-permute-start.3 = (f32[112,128]{1,0:T(8,128)S(1)}, f32[112,128]{1,0:T(8,128)S(1)}, u32[]{:S(2)}, u32[]{:S(2)}) collective-permute-start(f32[112,128]{1,0:T(8,128)S(1)} %get-tuple-element.22), channel_id=1, source_target_pairs={{0,1},{1,0},{2,3},{3,2},{4,5},{5,4},{6,7},{7,6},{8,9},{9,8},{10,11... | collective-permute-start | bytes 172040 | tf_op jit(solution)/shard_map/ppermute | solution.py:539
  7.1 0.0 collective-permute-done.2.refs_1_
  7.1 0.6 %border.1 = (f32[32,1152]{1,0:T(8,128)S(1)}, f32[64,128]{1,0:T(8,128)S(1)}, f32[64,128]{1,0:T(8,128)S(1)}) custom-call(f32[4,32,256]{2,1,0:T(8,128)S(1)} %get-tuple-element.15.refs_0_.own, f32[72,128]{1,0:T(8,128)S(1)} %collective-permute-done.2.refs_1_, f32[40,128]{1,0:T(8,128)S(1)} %get-tuple-element.18.refs_2_, f32[40,128]{1,0:T(8,128)S(1)} %get-tuple-element.19.refs_3_, ...), custom_call_target="tpu_custom_call" | custom-call | tf_op jit(solution)/shard_map/border/pallas_call | solution.py:548
  7.6 1.6 %collective-permute-start.4 = (f32[64,128]{1,0:T(8,128)S(1)}, f32[64,128]{1,0:T(8,128)S(1)}, u32[]{:S(2)}, u32[]{:S(2)}) collective-permute-start(f32[64,128]{1,0:T(8,128)S(1)} %get-tuple-element.24), channel_id=1, source_target_pairs={{0,1},{1,0},{2,3},{3,2},{4,5},{5,4},{6,7},{7,6},{8,9},{9,8},{10,11... | collective-permute-start | bytes 98312 | tf_op jit(solution)/shard_map/ppermute | solution.py:539
  9.2 0.5 %collective-permute-done.3.two = f32[112,128]{1,0:T(8,128)S(1)} collective-permute-done((f32[112,128]{1,0:T(8,128)S(1)}, f32[112,128]{1,0:T(8,128)S(1)}, u32[]{:S(2)}, u32[]{:S(2)}) %collective-permute-start.3) | collective-permute-done | bytes 57376 | tf_op jit(solution)/shard_map/ppermute | solution.py:539
  9.7 1.9 %collective-permute-done.4.four = f32[64,128]{1,0:T(8,128)S(1)} collective-permute-done((f32[64,128]{1,0:T(8,128)S(1)}, f32[64,128]{1,0:T(8,128)S(1)}, u32[]{:S(2)}, u32[]{:S(2)}) %collective-permute-start.4) | collective-permute-done | bytes 32800 | tf_op jit(solution)/shard_map/ppermute | solution.py:539
  11.6 1.6 %collective-permute-start.5 = (f32[176,128]{1,0:T(8,128)S(1)}, f32[176,128]{1,0:T(8,128)S(1)}, u32[]{:S(2)}, u32[]{:S(2)}) collective-permute-start(f32[176,128]{1,0:T(8,128)S(1)} %add.3.one), channel_id=1, source_target_pairs={{0,2},{1,3},{2,0},{3,1},{4,6},{5,7},{6,4},{7,5},{8,10},{9,11},{10,... | collective-permute-start | bytes 270344 | tf_op jit(solution)/shard_map/ppermute | solution.py:539
  13.3 3.0 %collective-permute-done.5.two = f32[176,128]{1,0:T(8,128)S(1)} collective-permute-done((f32[176,128]{1,0:T(8,128)S(1)}, f32[176,128]{1,0:T(8,128)S(1)}, u32[]{:S(2)}, u32[]{:S(2)}) %collective-permute-start.5) | collective-permute-done | bytes 90144 | tf_op jit(solution)/shard_map/ppermute | solution.py:539
  16.2 2.7 %collective-permute-start.6 = (f32[176,128]{1,0:T(8,128)S(1)}, f32[176,128]{1,0:T(8,128)S(1)}, u32[]{:S(2)}, u32[]{:S(2)}) collective-permute-start(f32[176,128]{1,0:T(8,128)S(1)} %add.4.one), channel_id=1, source_target_pairs={{0,4},{1,5},{2,6},{3,7},{4,0},{5,1},{6,2},{7,3},{8,12},{9,13},{10,... | collective-permute-start | bytes 270344 | tf_op jit(solution)/shard_map/ppermute | solution.py:539
  18.9 1.6 %collective-permute-start = (f32[4,32,256]{2,1,0:T(8,128)S(1)}, f32[4,32,256]{2,1,0:T(8,128)S(1)}, u32[]{:S(2)}, u32[]{:S(2)}) collective-permute-start(f32[4,32,256]{2,1,0:T(8,128)S(1)} %get-tuple-element.15.refs_0_.own), channel_id=1, source_target_pairs={{0,1},{1,0},{2,3},{3,2},{4,5},{5,4},{6,7},{7,6},{8,9},{9,8},{10,11... | collective-permute-start | bytes 393224 | tf_op jit(solution)/shard_map/ppermute | solution.py:539
  20.5 1.3 %collective-permute-done.6.two = f32[176,128]{1,0:T(8,128)S(1)} collective-permute-done((f32[176,128]{1,0:T(8,128)S(1)}, f32[176,128]{1,0:T(8,128)S(1)}, u32[]{:S(2)}, u32[]{:S(2)}) %collective-permute-start.6) | collective-permute-done | bytes 90144 | tf_op jit(solution)/shard_map/ppermute | solution.py:539
  21.8 1.6 %collective-permute-start.7 = (f32[176,128]{1,0:T(8,128)S(1)}, f32[176,128]{1,0:T(8,128)S(1)}, u32[]{:S(2)}, u32[]{:S(2)}) collective-permute-start(f32[176,128]{1,0:T(8,128)S(1)} %add.5.refs_5_.refs_4_), channel_id=1, source_target_pairs={{0,1},{1,0},{2,3},{3,2},{4,5},{5,4},{6,7},{7,6},{8,9},{9,8},{10,11... | collective-permute-start | bytes 270344 | tf_op jit(solution)/shard_map/ppermute | solution.py:539
  23.3 0.5 %collective-permute-done.refs_1_ = f32[4,32,256]{2,1,0:T(8,128)S(1)} collective-permute-done((f32[4,32,256]{2,1,0:T(8,128)S(1)}, f32[4,32,256]{2,1,0:T(8,128)S(1)}, u32[]{:S(2)}, u32[]{:S(2)}) %collective-permute-start) | collective-permute-done | bytes 131104 | tf_op jit(solution)/shard_map/ppermute | solution.py:539
  23.9 1.8 %nuclear.1.refs_2_ = f32[4,32,256]{2,1,0:T(8,128)S(1)} custom-call(f32[4,32,256]{2,1,0:T(8,128)S(1)} %get-tuple-element.15.refs_0_.own, f32[4,32,256]{2,1,0:T(8,128)S(1)} %collective-permute-done.refs_1_), custom_call_target="tpu_custom_call" | custom-call | tf_op jit(solution)/shard_map/nuclear/pallas_call | solution.py:548
  25.7 0.4 %first.1.refs_1_ = f32[4,128,128]{2,1,0:T(8,128)S(1)} custom-call(f32[4,32,256]{2,1,0:T(8,128)S(1)} %get-tuple-element.15.refs_0_.own, f32[4,32,256]{2,1,0:T(8,128)S(1)} %copy-done.1, f32[4,32,256]{2,1,0:T(8,128)S(1)} %nuclear.1.refs_2_, f32[112,1152]{1,0:T(8,128)S(1)} %get-tuple-element.17.refs_3_.refs_2_, ...), custom_call_target="tpu_custom_call" | custom-call | tf_op jit(solution)/shard_map/first/pallas_call | solution.py:548
  26.1 0.2 collective-permute-done.7.refs_5_
  26.4 1.2 %second.1 = f32[4,32,256]{2,1,0:T(8,128)} custom-call(f32[4,32,256]{2,1,0:T(8,128)S(1)} %get-tuple-element.15.refs_0_.own, f32[4,128,128]{2,1,0:T(8,128)S(1)} %first.1.refs_1_, f32[112,1152]{1,0:T(8,128)S(1)} %get-tuple-element.17.refs_3_.refs_2_, f32[32,1152]{1,0:T(8,128)S(1)} %get-tuple-element.20.refs_4_.refs_3_, f32[176,128]{1,0:T(8,128)S(1)} %add.5.refs_5_.refs_4_, ...), custom_call_target="tpu_custom_call" | custom-call | tf_op jit(solution)/shard_map/second/pallas_call | solution.py:548
  (6 shorter events, 0.0 us)
Async XLA Ops:
  0.0 1.8 %collective-permute-start.1 = (f32[4,32,256]{2,1,0:T(8,128)}, f32[4,32,256]{2,1,0:T(8,128)S(1)}, u32[]{:S(2)}, u32[]{:S(2)}) collective-permute-start(f32[4,32,256]{2,1,0:T(8,128)} %dirty.1), channel_id=1, source_target_pairs={{0,8},{8,0},{1,9},{9,1},{2,10},{10,2},{3,11},{11,3},{4,12},{12,4},... | collective-permute-start | bytes 393224 | tf_op jit(solution)/shard_map/ppermute | solution.py:539
  0.5 0.9 %copy-start = (f32[4,32,256]{2,1,0:T(8,128)S(1)}, f32[4,32,256]{2,1,0:T(8,128)}, u32[]{:S(2)}) copy-start(f32[4,32,256]{2,1,0:T(8,128)} %dirty.1) | copy-start | bytes 393220
  1.9 5.1 %collective-permute-start.2 = (f32[72,128]{1,0:T(8,128)S(1)}, f32[72,128]{1,0:T(8,128)S(1)}, u32[]{:S(2)}, u32[]{:S(2)}) collective-permute-start(f32[72,128]{1,0:T(8,128)S(1)} %rows.1), channel_id=1, source_target_pairs={{0,16},{16,0},{1,17},{17,1},{2,18},{18,2},{3,19},{19,3},{4,20},{20... | collective-permute-start | bytes 110600 | tf_op jit(solution)/shard_map/ppermute | solution.py:539
  5.5 4.2 %collective-permute-start.3 = (f32[112,128]{1,0:T(8,128)S(1)}, f32[112,128]{1,0:T(8,128)S(1)}, u32[]{:S(2)}, u32[]{:S(2)}) collective-permute-start(f32[112,128]{1,0:T(8,128)S(1)} %get-tuple-element.22), channel_id=1, source_target_pairs={{0,1},{1,0},{2,3},{3,2},{4,5},{5,4},{6,7},{7,6},{8,9},{9,8},{10,11... | collective-permute-start | bytes 172040 | tf_op jit(solution)/shard_map/ppermute | solution.py:539
  7.1 18.6 %copy-start.1 = (f32[4,32,256]{2,1,0:T(8,128)S(1)}, f32[4,32,256]{2,1,0:T(8,128)}, u32[]{:S(2)}) copy-start(f32[4,32,256]{2,1,0:T(8,128)} %refs_1_.1) | copy-start | bytes 393220
  7.6 4.0 %collective-permute-start.4 = (f32[64,128]{1,0:T(8,128)S(1)}, f32[64,128]{1,0:T(8,128)S(1)}, u32[]{:S(2)}, u32[]{:S(2)}) collective-permute-start(f32[64,128]{1,0:T(8,128)S(1)} %get-tuple-element.24), channel_id=1, source_target_pairs={{0,1},{1,0},{2,3},{3,2},{4,5},{5,4},{6,7},{7,6},{8,9},{9,8},{10,11... | collective-permute-start | bytes 98312 | tf_op jit(solution)/shard_map/ppermute | solution.py:539
  11.6 4.6 %collective-permute-start.5 = (f32[176,128]{1,0:T(8,128)S(1)}, f32[176,128]{1,0:T(8,128)S(1)}, u32[]{:S(2)}, u32[]{:S(2)}) collective-permute-start(f32[176,128]{1,0:T(8,128)S(1)} %add.3.one), channel_id=1, source_target_pairs={{0,2},{1,3},{2,0},{3,1},{4,6},{5,7},{6,4},{7,5},{8,10},{9,11},{10,... | collective-permute-start | bytes 270344 | tf_op jit(solution)/shard_map/ppermute | solution.py:539
  16.2 5.5 %collective-permute-start.6 = (f32[176,128]{1,0:T(8,128)S(1)}, f32[176,128]{1,0:T(8,128)S(1)}, u32[]{:S(2)}, u32[]{:S(2)}) collective-permute-start(f32[176,128]{1,0:T(8,128)S(1)} %add.4.one), channel_id=1, source_target_pairs={{0,4},{1,5},{2,6},{3,7},{4,0},{5,1},{6,2},{7,3},{8,12},{9,13},{10,... | collective-permute-start | bytes 270344 | tf_op jit(solution)/shard_map/ppermute | solution.py:539
  18.9 5.0 %collective-permute-start = (f32[4,32,256]{2,1,0:T(8,128)S(1)}, f32[4,32,256]{2,1,0:T(8,128)S(1)}, u32[]{:S(2)}, u32[]{:S(2)}) collective-permute-start(f32[4,32,256]{2,1,0:T(8,128)S(1)} %get-tuple-element.15.refs_0_.own), channel_id=1, source_target_pairs={{0,1},{1,0},{2,3},{3,2},{4,5},{5,4},{6,7},{7,6},{8,9},{9,8},{10,11... | collective-permute-start | bytes 393224 | tf_op jit(solution)/shard_map/ppermute | solution.py:539
  21.8 4.6 %collective-permute-start.7 = (f32[176,128]{1,0:T(8,128)S(1)}, f32[176,128]{1,0:T(8,128)S(1)}, u32[]{:S(2)}, u32[]{:S(2)}) collective-permute-start(f32[176,128]{1,0:T(8,128)S(1)} %add.5.refs_5_.refs_4_), channel_id=1, source_target_pairs={{0,1},{1,0},{2,3},{3,2},{4,5},{5,4},{6,7},{7,6},{8,9},{9,8},{10,11... | collective-permute-start | bytes 270344 | tf_op jit(solution)/shard_map/ppermute | solution.py:539

commit v8 on v7

--- a/solution.py
+++ b/solution.py
@@ -67,9 +67,9 @@
     return top, (values - top.astype(F32)).astype(BF16)
 
 
-def dot3(left, right, dims=((1,), (0,))):
+def dot3(left, right):
     def dot(one, two):
-        return lax.dot_general(one, two, (dims, ((), ())), preferred_element_type=F32)
+        return jnp.dot(one, two, preferred_element_type=F32)
 
     count = left[0].shape[0]
     both = dot(jnp.concatenate(left, 0), right[0])
@@ -407,7 +407,7 @@
     scale[...] = scales(limit, mine[...])
     half_duals(Places(rows, cols), y, scale, u_inner, u_border, spread)
     lanes = pl.ds(pl.multiple_of(y * NDB * LANES, NDB * LANES), NDB * LANES)
-    result = dot3(halves(spread[...]), [table[i, :cols, lanes] for i in range(2)], ((1,), (1,)))
+    result = dot3(halves(spread[...]), [table[i, lanes, :] for i in range(2)])
     for t in range(cols // LANES):
         step[cols // LANES + t] = result[:, t * LANES : (t + 1) * LANES]
     for c in range(channels):
@@ -438,8 +438,8 @@
     spread_rows(*duals, strip_row_taps((1, 2), 1.0), spread, slice(NDB * LANES, (NDB + 1) * LANES))
     lanes = pl.ds(pl.multiple_of((1 - y) * NDB * LANES, NDB * LANES), NDB * LANES)
     left = halves(spread[...])
-    right = [jnp.concatenate([table[i, :cols, lanes], table[i, :cols, main:]], 1) for i in range(2)]
-    result = dot3(left, right, ((1,), (1,)))
+    right = [jnp.concatenate([table[i, lanes, :], table[i, main:, :]], 0) for i in range(2)]
+    result = dot3(left, right)
     for t in range(cols // LANES):
         image[t] = result[:, t * LANES : (t + 1) * LANES] + step[cols // LANES + t]
     for c in range(channels):
@@ -532,6 +532,13 @@
     count = one.shape[0]
     out[:count, :] = one[...] + two[...]
     out[count:, :] = three[...] + four[...]
+
+
+def turn_kernel(table, out):
+    cols = out.shape[2]
+    for i in range(2):
+        for t in range(0, table.shape[2], LANES):
+            out[i, t : t + LANES, :] = table[i, :cols, t : t + LANES].astype(F32).T.astype(BF16)
 
 
 def exchange(values, axis, bit):
@@ -602,6 +609,7 @@
     received_more = exchange(send_more, "chan", 1)
     total = call(add_parts_kernel, "add", [(places.all, LANES)], [keep, received, keep_more, received_more])
     other = exchange(own, "chan", 1)
+    turned = call(turn_kernel, "turn", [jax.ShapeDtypeStruct((2, tiles * LANES, cols), BF16)], [near])
     nuclear = call(
         lambda *refs: nuclear_kernel(nuclear_limit, *refs),
         "nuclear",
@@ -619,7 +627,7 @@
         lambda *refs: first_kernel(sparse_limit, *refs),
         "first",
         [(2 * cols // LANES, channels * rows, LANES)],
-        [own, density, nuclear, u_inner, u_border, total, near],
+        [own, density, nuclear, u_inner, u_border, total, turned],
         [(4 * rows, NDB * LANES), (places.all, LANES)],
         24,
     )
@@ -627,7 +635,7 @@
         lambda *refs: second_kernel(sparse_limit, *refs),
         "second",
         [dirty_image.shape],
-        [own, step, u_inner, u_border, total, theirs, near],
+        [own, step, u_inner, u_border, total, theirs, turned],
         [(4 * rows, (NDB + 1) * LANES), (cols // LANES, 4 * rows, LANES), (2, places.all, LANES)],
         24,
     )

time: 27.7 us -> 27.7 us (level)
  Pallas kernels: 5.43 us -> 5.81 us
  waiting for transfers between devices: 7.38 us -> 7.02 us
    pallas_call x10 -> x11, Pallas kernels: 5.43 us -> 5.81 us  [call(): pl.pallas_call(kernel, name=name, out_shape=many, in_specs=vmem(len(opera...]
    ppermute x8, waiting for transfers between devices: 7.38 us -> 7.02 us  [exchange(): return lax.ppermute(values, axis, [(i, i ^ bit) for i in range(count)])]
  transfers between devices with their start and end apart: 8 -> 8, of which waited for: 6 -> 6; matrix products, arithmetic and copies ran while one was open for 0% -> 0% of each run, Pallas kernels for 15% -> 16%
where the time goes in v8:
time: 27.7 us; the launch traced here: 27.5 us
  starting transfers between devices  13.7 us (49%)
  waiting for transfers between devices  7.02 us (25%)
  Pallas kernels  5.81 us (21%)
  local copies, waits for them, and re-layouts  0.91 us (3%)
    ppermute x8, starting transfers between devices, exchange(): return lax.ppermute(values, axis, [(i, i ^ bit) for i in range(count)])  13.7 us
    ppermute x8, waiting for transfers between devices, exchange(): return lax.ppermute(values, axis, [(i, i ^ bit) for i in range(count)])  7.02 us
    pallas_call x11, Pallas kernels, call(): pl.pallas_call(kernel, name=name, out_shape=many, in_specs=vmem(len(opera...  5.81 us
    unnamed x4, local copies, waits for them, and re-layouts  0.91 us
  transfers between devices with their start and end apart: 8, of which 6 were waited for; matrix products, arithmetic and copies ran while one was open for 0% of the time, Pallas kernels for 16%

profile of v8, /device:TPU:0, one launch (start us, length us, event | category | flops | bytes accessed | tf_op | source)
XLA Modules:
  0.0 27.5 jit_solution(2432284662471689278)
XLA Ops:
  0.0 0.5 %collective-permute-start.1 = (f32[4,32,256]{2,1,0:T(8,128)}, f32[4,32,256]{2,1,0:T(8,128)S(1)}, u32[]{:S(2)}, u32[]{:S(2)}) collective-permute-start(f32[4,32,256]{2,1,0:T(8,128)} %dirty.1), channel_id=1, source_target_pairs={{0,8},{8,0},{1,9},{9,1},{2,10},{10,2},{3,11},{11,3},{4,12},{12,4},... | collective-permute-start | bytes 393224 | tf_op jit(solution)/shard_map/ppermute | solution.py:546
  0.5 0.9 %copy-done.1 = f32[4,32,256]{2,1,0:T(8,128)S(1)} copy-done((f32[4,32,256]{2,1,0:T(8,128)S(1)}, f32[4,32,256]{2,1,0:T(8,128)}, u32[]{:S(2)}) %copy-start.1) | copy-done | bytes 131096
  1.4 0.5 %hold.1 = (f32[4,32,256]{2,1,0:T(8,128)S(1)}, bf16[2,288,1152]{2,1,0:T(8,128)(2,1)S(1)}) custom-call(f32[4,32,256]{2,1,0:T(8,128)S(1)} %copy-done.1), custom_call_target="tpu_custom_call" | custom-call | tf_op jit(solution)/shard_map/hold/pallas_call | solution.py:555
  1.8 0.1 rows.1
  1.9 2.7 %collective-permute-start.2 = (f32[72,128]{1,0:T(8,128)S(1)}, f32[72,128]{1,0:T(8,128)S(1)}, u32[]{:S(2)}, u32[]{:S(2)}) collective-permute-start(f32[72,128]{1,0:T(8,128)S(1)} %rows.1), channel_id=1, source_target_pairs={{0,16},{16,0},{1,17},{17,1},{2,18},{18,2},{3,19},{19,3},{4,20},{20... | collective-permute-start | bytes 110600 | tf_op jit(solution)/shard_map/ppermute | solution.py:546
  4.6 0.9 %inner.1 = (f32[112,1152]{1,0:T(8,128)S(1)}, f32[112,128]{1,0:T(8,128)S(1)}, f32[112,128]{1,0:T(8,128)S(1)}, f32[40,128]{1,0:T(8,128)S(1)}, f32[40,128]{1,0:T(8,128)S(1)}) custom-call(f32[4,32,256]{2,1,0:T(8,128)S(1)} %get-tuple-element.15.refs_0_.own, f32[4,32,256]{2,1,0:T(8,128)S(1)} %collective-permute-done.1.refs_0_.refs_4_, ...), custom_call_target="tpu_custom_call" | custom-call | tf_op jit(solution)/shard_map/inner/pallas_call | solution.py:555
  5.5 1.6 %collective-permute-start.3 = (f32[112,128]{1,0:T(8,128)S(1)}, f32[112,128]{1,0:T(8,128)S(1)}, u32[]{:S(2)}, u32[]{:S(2)}) collective-permute-start(f32[112,128]{1,0:T(8,128)S(1)} %get-tuple-element.22), channel_id=1, source_target_pairs={{0,1},{1,0},{2,3},{3,2},{4,5},{5,4},{6,7},{7,6},{8,9},{9,8},{10,11... | collective-permute-start | bytes 172040 | tf_op jit(solution)/shard_map/ppermute | solution.py:546
  7.1 0.6 %border.1 = (f32[32,1152]{1,0:T(8,128)S(1)}, f32[64,128]{1,0:T(8,128)S(1)}, f32[64,128]{1,0:T(8,128)S(1)}) custom-call(f32[4,32,256]{2,1,0:T(8,128)S(1)} %get-tuple-element.15.refs_0_.own, f32[72,128]{1,0:T(8,128)S(1)} %collective-permute-done.2.refs_1_, f32[40,128]{1,0:T(8,128)S(1)} %get-tuple-element.18.refs_2_, f32[40,128]{1,0:T(8,128)S(1)} %get-tuple-element.19.refs_3_, ...), custom_call_target="tpu_custom_call" | custom-call | tf_op jit(solution)/shard_map/border/pallas_call | solution.py:555
  7.6 1.6 %collective-permute-start.4 = (f32[64,128]{1,0:T(8,128)S(1)}, f32[64,128]{1,0:T(8,128)S(1)}, u32[]{:S(2)}, u32[]{:S(2)}) collective-permute-start(f32[64,128]{1,0:T(8,128)S(1)} %get-tuple-element.24), channel_id=1, source_target_pairs={{0,1},{1,0},{2,3},{3,2},{4,5},{5,4},{6,7},{7,6},{8,9},{9,8},{10,11... | collective-permute-start | bytes 98312 | tf_op jit(solution)/shard_map/ppermute | solution.py:546
  9.2 0.5 %collective-permute-done.3.two = f32[112,128]{1,0:T(8,128)S(1)} collective-permute-done((f32[112,128]{1,0:T(8,128)S(1)}, f32[112,128]{1,0:T(8,128)S(1)}, u32[]{:S(2)}, u32[]{:S(2)}) %collective-permute-start.3) | collective-permute-done | bytes 57376 | tf_op jit(solution)/shard_map/ppermute | solution.py:546
  9.7 1.9 %collective-permute-done.4.four = f32[64,128]{1,0:T(8,128)S(1)} collective-permute-done((f32[64,128]{1,0:T(8,128)S(1)}, f32[64,128]{1,0:T(8,128)S(1)}, u32[]{:S(2)}, u32[]{:S(2)}) %collective-permute-start.4) | collective-permute-done | bytes 32800 | tf_op jit(solution)/shard_map/ppermute | solution.py:546
  11.6 1.6 %collective-permute-start.5 = (f32[176,128]{1,0:T(8,128)S(1)}, f32[176,128]{1,0:T(8,128)S(1)}, u32[]{:S(2)}, u32[]{:S(2)}) collective-permute-start(f32[176,128]{1,0:T(8,128)S(1)} %add.3.one), channel_id=1, source_target_pairs={{0,2},{1,3},{2,0},{3,1},{4,6},{5,7},{6,4},{7,5},{8,10},{9,11},{10,... | collective-permute-start | bytes 270344 | tf_op jit(solution)/shard_map/ppermute | solution.py:546
  13.3 3.0 %collective-permute-done.5.two = f32[176,128]{1,0:T(8,128)S(1)} collective-permute-done((f32[176,128]{1,0:T(8,128)S(1)}, f32[176,128]{1,0:T(8,128)S(1)}, u32[]{:S(2)}, u32[]{:S(2)}) %collective-permute-start.5) | collective-permute-done | bytes 90144 | tf_op jit(solution)/shard_map/ppermute | solution.py:546
  16.2 2.7 %collective-permute-start.6 = (f32[176,128]{1,0:T(8,128)S(1)}, f32[176,128]{1,0:T(8,128)S(1)}, u32[]{:S(2)}, u32[]{:S(2)}) collective-permute-start(f32[176,128]{1,0:T(8,128)S(1)} %add.4.one), channel_id=1, source_target_pairs={{0,4},{1,5},{2,6},{3,7},{4,0},{5,1},{6,2},{7,3},{8,12},{9,13},{10,... | collective-permute-start | bytes 270344 | tf_op jit(solution)/shard_map/ppermute | solution.py:546
  18.9 1.6 %collective-permute-start = (f32[4,32,256]{2,1,0:T(8,128)S(1)}, f32[4,32,256]{2,1,0:T(8,128)S(1)}, u32[]{:S(2)}, u32[]{:S(2)}) collective-permute-start(f32[4,32,256]{2,1,0:T(8,128)S(1)} %get-tuple-element.15.refs_0_.own), channel_id=1, source_target_pairs={{0,1},{1,0},{2,3},{3,2},{4,5},{5,4},{6,7},{7,6},{8,9},{9,8},{10,11... | collective-permute-start | bytes 393224 | tf_op jit(solution)/shard_map/ppermute | solution.py:546
  20.5 1.3 %collective-permute-done.6.two = f32[176,128]{1,0:T(8,128)S(1)} collective-permute-done((f32[176,128]{1,0:T(8,128)S(1)}, f32[176,128]{1,0:T(8,128)S(1)}, u32[]{:S(2)}, u32[]{:S(2)}) %collective-permute-start.6) | collective-permute-done | bytes 90144 | tf_op jit(solution)/shard_map/ppermute | solution.py:546
  21.8 0.0 copy-start
  21.8 1.6 %collective-permute-start.7 = (f32[176,128]{1,0:T(8,128)S(1)}, f32[176,128]{1,0:T(8,128)S(1)}, u32[]{:S(2)}, u32[]{:S(2)}) collective-permute-start(f32[176,128]{1,0:T(8,128)S(1)} %add.5.refs_5_.refs_4_), channel_id=1, source_target_pairs={{0,1},{1,0},{2,3},{3,2},{4,5},{5,4},{6,7},{7,6},{8,9},{9,8},{10,11... | collective-permute-start | bytes 270344 | tf_op jit(solution)/shard_map/ppermute | solution.py:546
  23.3 0.4 %turn.1.refs_6_ = bf16[2,1152,256]{2,1,0:T(8,128)(2,1)S(1)} custom-call(bf16[2,288,1152]{2,1,0:T(8,128)(2,1)S(1)} %get-tuple-element.16.refs_1_.refs_5_.table), custom_call_target="tpu_custom_call" | custom-call | tf_op jit(solution)/shard_map/turn/pallas_call | solution.py:555
  23.7 0.1 collective-permute-done.refs_1_
  23.9 1.8 %nuclear.1.refs_2_ = f32[4,32,256]{2,1,0:T(8,128)S(1)} custom-call(f32[4,32,256]{2,1,0:T(8,128)S(1)} %get-tuple-element.15.refs_0_.own, f32[4,32,256]{2,1,0:T(8,128)S(1)} %collective-permute-done.refs_1_), custom_call_target="tpu_custom_call" | custom-call | tf_op jit(solution)/shard_map/nuclear/pallas_call | solution.py:555
  25.7 0.4 %first.1.refs_1_ = f32[4,128,128]{2,1,0:T(8,128)S(1)} custom-call(f32[4,32,256]{2,1,0:T(8,128)S(1)} %get-tuple-element.15.refs_0_.own, f32[4,32,256]{2,1,0:T(8,128)S(1)} %copy-done, f32[4,32,256]{2,1,0:T(8,128)S(1)} %nuclear.1.refs_2_, f32[112,1152]{1,0:T(8,128)S(1)} %get-tuple-element.17.refs_3_.refs_2_, f32[32,1152]{1,0:T(8,128)S(1)} %get-tuple-element.20.refs_4_.refs_3_, ...), custom_call_target="tpu_custom_call" | custom-call | tf_op jit(solution)/shard_map/first/pallas_call | solution.py:555
  26.1 0.3 collective-permute-done.7.refs_5_
  26.4 1.2 %second.1 = f32[4,32,256]{2,1,0:T(8,128)} custom-call(f32[4,32,256]{2,1,0:T(8,128)S(1)} %get-tuple-element.15.refs_0_.own, f32[4,128,128]{2,1,0:T(8,128)S(1)} %first.1.refs_1_, f32[112,1152]{1,0:T(8,128)S(1)} %get-tuple-element.17.refs_3_.refs_2_, f32[32,1152]{1,0:T(8,128)S(1)} %get-tuple-element.20.refs_4_.refs_3_, f32[176,128]{1,0:T(8,128)S(1)} %add.5.refs_5_.refs_4_, ...), custom_call_target="tpu_custom_call" | custom-call | tf_op jit(solution)/shard_map/second/pallas_call | solution.py:555
  (7 shorter events, 0.0 us)
Async XLA Ops:
  0.0 1.8 %collective-permute-start.1 = (f32[4,32,256]{2,1,0:T(8,128)}, f32[4,32,256]{2,1,0:T(8,128)S(1)}, u32[]{:S(2)}, u32[]{:S(2)}) collective-permute-start(f32[4,32,256]{2,1,0:T(8,128)} %dirty.1), channel_id=1, source_target_pairs={{0,8},{8,0},{1,9},{9,1},{2,10},{10,2},{3,11},{11,3},{4,12},{12,4},... | collective-permute-start | bytes 393224 | tf_op jit(solution)/shard_map/ppermute | solution.py:546
  0.5 0.9 %copy-start.1 = (f32[4,32,256]{2,1,0:T(8,128)S(1)}, f32[4,32,256]{2,1,0:T(8,128)}, u32[]{:S(2)}) copy-start(f32[4,32,256]{2,1,0:T(8,128)} %dirty.1) | copy-start | bytes 393220
  1.9 5.1 %collective-permute-start.2 = (f32[72,128]{1,0:T(8,128)S(1)}, f32[72,128]{1,0:T(8,128)S(1)}, u32[]{:S(2)}, u32[]{:S(2)}) collective-permute-start(f32[72,128]{1,0:T(8,128)S(1)} %rows.1), channel_id=1, source_target_pairs={{0,16},{16,0},{1,17},{17,1},{2,18},{18,2},{3,19},{19,3},{4,20},{20... | collective-permute-start | bytes 110600 | tf_op jit(solution)/shard_map/ppermute | solution.py:546
  5.5 4.2 %collective-permute-start.3 = (f32[112,128]{1,0:T(8,128)S(1)}, f32[112,128]{1,0:T(8,128)S(1)}, u32[]{:S(2)}, u32[]{:S(2)}) collective-permute-start(f32[112,128]{1,0:T(8,128)S(1)} %get-tuple-element.22), channel_id=1, source_target_pairs={{0,1},{1,0},{2,3},{3,2},{4,5},{5,4},{6,7},{7,6},{8,9},{9,8},{10,11... | collective-permute-start | bytes 172040 | tf_op jit(solution)/shard_map/ppermute | solution.py:546
  7.6 4.0 %collective-permute-start.4 = (f32[64,128]{1,0:T(8,128)S(1)}, f32[64,128]{1,0:T(8,128)S(1)}, u32[]{:S(2)}, u32[]{:S(2)}) collective-permute-start(f32[64,128]{1,0:T(8,128)S(1)} %get-tuple-element.24), channel_id=1, source_target_pairs={{0,1},{1,0},{2,3},{3,2},{4,5},{5,4},{6,7},{7,6},{8,9},{9,8},{10,11... | collective-permute-start | bytes 98312 | tf_op jit(solution)/shard_map/ppermute | solution.py:546
  11.6 4.6 %collective-permute-start.5 = (f32[176,128]{1,0:T(8,128)S(1)}, f32[176,128]{1,0:T(8,128)S(1)}, u32[]{:S(2)}, u32[]{:S(2)}) collective-permute-start(f32[176,128]{1,0:T(8,128)S(1)} %add.3.one), channel_id=1, source_target_pairs={{0,2},{1,3},{2,0},{3,1},{4,6},{5,7},{6,4},{7,5},{8,10},{9,11},{10,... | collective-permute-start | bytes 270344 | tf_op jit(solution)/shard_map/ppermute | solution.py:546
  16.2 5.5 %collective-permute-start.6 = (f32[176,128]{1,0:T(8,128)S(1)}, f32[176,128]{1,0:T(8,128)S(1)}, u32[]{:S(2)}, u32[]{:S(2)}) collective-permute-start(f32[176,128]{1,0:T(8,128)S(1)} %add.4.one), channel_id=1, source_target_pairs={{0,4},{1,5},{2,6},{3,7},{4,0},{5,1},{6,2},{7,3},{8,12},{9,13},{10,... | collective-permute-start | bytes 270344 | tf_op jit(solution)/shard_map/ppermute | solution.py:546
  18.9 5.0 %collective-permute-start = (f32[4,32,256]{2,1,0:T(8,128)S(1)}, f32[4,32,256]{2,1,0:T(8,128)S(1)}, u32[]{:S(2)}, u32[]{:S(2)}) collective-permute-start(f32[4,32,256]{2,1,0:T(8,128)S(1)} %get-tuple-element.15.refs_0_.own), channel_id=1, source_target_pairs={{0,1},{1,0},{2,3},{3,2},{4,5},{5,4},{6,7},{7,6},{8,9},{9,8},{10,11... | collective-permute-start | bytes 393224 | tf_op jit(solution)/shard_map/ppermute | solution.py:546
  21.8 4.0 %copy-start = (f32[4,32,256]{2,1,0:T(8,128)S(1)}, f32[4,32,256]{2,1,0:T(8,128)}, u32[]{:S(2)}) copy-start(f32[4,32,256]{2,1,0:T(8,128)} %refs_1_.1) | copy-start | bytes 393220
  21.8 4.6 %collective-permute-start.7 = (f32[176,128]{1,0:T(8,128)S(1)}, f32[176,128]{1,0:T(8,128)S(1)}, u32[]{:S(2)}, u32[]{:S(2)}) collective-permute-start(f32[176,128]{1,0:T(8,128)S(1)} %add.5.refs_5_.refs_4_), channel_id=1, source_target_pairs={{0,1},{1,0},{2,3},{3,2},{4,5},{5,4},{6,7},{7,6},{8,9},{9,8},{10,11... | collective-permute-start | bytes 270344 | tf_op jit(solution)/shard_map/ppermute | solution.py:546

commit v9 on v7

--- a/solution.py
+++ b/solution.py
@@ -421,8 +421,7 @@
     channels, rows, cols = raw.shape
     y = lax.axis_index("chan") % 2
     places = Places(rows, cols)
-    both = slice(places.strip, places.border)
-    scale[y, both, :] = scales(limit, mine[both, :])
+    scale[y] = scales(limit, mine[...])
     scale[1 - y] = scales(limit, theirs[...])
     half_duals(places, 1 - y, scale.at[1 - y], u_inner, u_border, spread)
     main = 2 * NDB * LANES

time: 27.7 us -> 27.7 us (level)
  no operation moved by 1% of the time
where the time goes in v9:
time: 27.7 us; the launch traced here: 27.5 us
  starting transfers between devices  13.7 us (49%)
  waiting for transfers between devices  7.38 us (27%)
  Pallas kernels  5.45 us (20%)
  local copies, waits for them, and re-layouts  0.91 us (3%)
    ppermute x8, starting transfers between devices, exchange(): return lax.ppermute(values, axis, [(i, i ^ bit) for i in range(count)])  13.7 us
    ppermute x8, waiting for transfers between devices, exchange(): return lax.ppermute(values, axis, [(i, i ^ bit) for i in range(count)])  7.38 us
    pallas_call x10, Pallas kernels, call(): pl.pallas_call(kernel, name=name, out_shape=many, in_specs=vmem(len(opera...  5.45 us
    unnamed x4, local copies, waits for them, and re-layouts  0.91 us
  transfers between devices with their start and end apart: 8, of which 6 were waited for; matrix products, arithmetic and copies ran while one was open for 0% of the time, Pallas kernels for 15%

profile of v9, /device:TPU:0, one launch (start us, length us, event | category | flops | bytes accessed | tf_op | source)
XLA Modules:
  0.0 27.5 jit_solution(8813178178553020246)
XLA Ops:
  0.0 0.5 %collective-permute-start.1 = (f32[4,32,256]{2,1,0:T(8,128)}, f32[4,32,256]{2,1,0:T(8,128)S(1)}, u32[]{:S(2)}, u32[]{:S(2)}) collective-permute-start(f32[4,32,256]{2,1,0:T(8,128)} %dirty.1), channel_id=1, source_target_pairs={{0,8},{8,0},{1,9},{9,1},{2,10},{10,2},{3,11},{11,3},{4,12},{12,4},... | collective-permute-start | bytes 393224 | tf_op jit(solution)/shard_map/ppermute | solution.py:538
  0.5 0.9 %copy-done = f32[4,32,256]{2,1,0:T(8,128)S(1)} copy-done((f32[4,32,256]{2,1,0:T(8,128)S(1)}, f32[4,32,256]{2,1,0:T(8,128)}, u32[]{:S(2)}) %copy-start) | copy-done | bytes 131096
  1.4 0.5 %hold.1 = (f32[4,32,256]{2,1,0:T(8,128)S(1)}, bf16[2,288,1152]{2,1,0:T(8,128)(2,1)S(1)}) custom-call(f32[4,32,256]{2,1,0:T(8,128)S(1)} %copy-done), custom_call_target="tpu_custom_call" | custom-call | tf_op jit(solution)/shard_map/hold/pallas_call | solution.py:547
  1.8 0.0 collective-permute-done.1.refs_0_.refs_4_
  1.8 0.1 rows.1
  1.9 2.7 %collective-permute-start.2 = (f32[72,128]{1,0:T(8,128)S(1)}, f32[72,128]{1,0:T(8,128)S(1)}, u32[]{:S(2)}, u32[]{:S(2)}) collective-permute-start(f32[72,128]{1,0:T(8,128)S(1)} %rows.1), channel_id=1, source_target_pairs={{0,16},{16,0},{1,17},{17,1},{2,18},{18,2},{3,19},{19,3},{4,20},{20... | collective-permute-start | bytes 110600 | tf_op jit(solution)/shard_map/ppermute | solution.py:538
  4.6 0.9 %inner.1 = (f32[112,1152]{1,0:T(8,128)S(1)}, f32[112,128]{1,0:T(8,128)S(1)}, f32[112,128]{1,0:T(8,128)S(1)}, f32[40,128]{1,0:T(8,128)S(1)}, f32[40,128]{1,0:T(8,128)S(1)}) custom-call(f32[4,32,256]{2,1,0:T(8,128)S(1)} %get-tuple-element.15.refs_0_.own, f32[4,32,256]{2,1,0:T(8,128)S(1)} %collective-permute-done.1.refs_0_.refs_4_, ...), custom_call_target="tpu_custom_call" | custom-call | tf_op jit(solution)/shard_map/inner/pallas_call | solution.py:547
  5.5 1.6 %collective-permute-start.3 = (f32[112,128]{1,0:T(8,128)S(1)}, f32[112,128]{1,0:T(8,128)S(1)}, u32[]{:S(2)}, u32[]{:S(2)}) collective-permute-start(f32[112,128]{1,0:T(8,128)S(1)} %get-tuple-element.22), channel_id=1, source_target_pairs={{0,1},{1,0},{2,3},{3,2},{4,5},{5,4},{6,7},{7,6},{8,9},{9,8},{10,11... | collective-permute-start | bytes 172040 | tf_op jit(solution)/shard_map/ppermute | solution.py:538
  7.1 0.0 collective-permute-done.2.refs_1_
  7.1 0.6 %border.1 = (f32[32,1152]{1,0:T(8,128)S(1)}, f32[64,128]{1,0:T(8,128)S(1)}, f32[64,128]{1,0:T(8,128)S(1)}) custom-call(f32[4,32,256]{2,1,0:T(8,128)S(1)} %get-tuple-element.15.refs_0_.own, f32[72,128]{1,0:T(8,128)S(1)} %collective-permute-done.2.refs_1_, f32[40,128]{1,0:T(8,128)S(1)} %get-tuple-element.18.refs_2_, f32[40,128]{1,0:T(8,128)S(1)} %get-tuple-element.19.refs_3_, ...), custom_call_target="tpu_custom_call" | custom-call | tf_op jit(solution)/shard_map/border/pallas_call | solution.py:547
  7.6 1.6 %collective-permute-start.4 = (f32[64,128]{1,0:T(8,128)S(1)}, f32[64,128]{1,0:T(8,128)S(1)}, u32[]{:S(2)}, u32[]{:S(2)}) collective-permute-start(f32[64,128]{1,0:T(8,128)S(1)} %get-tuple-element.24), channel_id=1, source_target_pairs={{0,1},{1,0},{2,3},{3,2},{4,5},{5,4},{6,7},{7,6},{8,9},{9,8},{10,11... | collective-permute-start | bytes 98312 | tf_op jit(solution)/shard_map/ppermute | solution.py:538
  9.2 0.5 %collective-permute-done.3.two = f32[112,128]{1,0:T(8,128)S(1)} collective-permute-done((f32[112,128]{1,0:T(8,128)S(1)}, f32[112,128]{1,0:T(8,128)S(1)}, u32[]{:S(2)}, u32[]{:S(2)}) %collective-permute-start.3) | collective-permute-done | bytes 57376 | tf_op jit(solution)/shard_map/ppermute | solution.py:538
  9.7 1.9 %collective-permute-done.4.four = f32[64,128]{1,0:T(8,128)S(1)} collective-permute-done((f32[64,128]{1,0:T(8,128)S(1)}, f32[64,128]{1,0:T(8,128)S(1)}, u32[]{:S(2)}, u32[]{:S(2)}) %collective-permute-start.4) | collective-permute-done | bytes 32800 | tf_op jit(solution)/shard_map/ppermute | solution.py:538
  11.6 1.6 %collective-permute-start.5 = (f32[176,128]{1,0:T(8,128)S(1)}, f32[176,128]{1,0:T(8,128)S(1)}, u32[]{:S(2)}, u32[]{:S(2)}) collective-permute-start(f32[176,128]{1,0:T(8,128)S(1)} %add.3.one), channel_id=1, source_target_pairs={{0,2},{1,3},{2,0},{3,1},{4,6},{5,7},{6,4},{7,5},{8,10},{9,11},{10,... | collective-permute-start | bytes 270344 | tf_op jit(solution)/shard_map/ppermute | solution.py:538
  13.3 3.0 %collective-permute-done.5.two = f32[176,128]{1,0:T(8,128)S(1)} collective-permute-done((f32[176,128]{1,0:T(8,128)S(1)}, f32[176,128]{1,0:T(8,128)S(1)}, u32[]{:S(2)}, u32[]{:S(2)}) %collective-permute-start.5) | collective-permute-done | bytes 90144 | tf_op jit(solution)/shard_map/ppermute | solution.py:538
  16.2 2.7 %collective-permute-start.6 = (f32[176,128]{1,0:T(8,128)S(1)}, f32[176,128]{1,0:T(8,128)S(1)}, u32[]{:S(2)}, u32[]{:S(2)}) collective-permute-start(f32[176,128]{1,0:T(8,128)S(1)} %add.4.one), channel_id=1, source_target_pairs={{0,4},{1,5},{2,6},{3,7},{4,0},{5,1},{6,2},{7,3},{8,12},{9,13},{10,... | collective-permute-start | bytes 270344 | tf_op jit(solution)/shard_map/ppermute | solution.py:538
  18.9 1.6 %collective-permute-start = (f32[4,32,256]{2,1,0:T(8,128)S(1)}, f32[4,32,256]{2,1,0:T(8,128)S(1)}, u32[]{:S(2)}, u32[]{:S(2)}) collective-permute-start(f32[4,32,256]{2,1,0:T(8,128)S(1)} %get-tuple-element.15.refs_0_.own), channel_id=1, source_target_pairs={{0,1},{1,0},{2,3},{3,2},{4,5},{5,4},{6,7},{7,6},{8,9},{9,8},{10,11... | collective-permute-start | bytes 393224 | tf_op jit(solution)/shard_map/ppermute | solution.py:538
  20.5 1.3 %collective-permute-done.6.two = f32[176,128]{1,0:T(8,128)S(1)} collective-permute-done((f32[176,128]{1,0:T(8,128)S(1)}, f32[176,128]{1,0:T(8,128)S(1)}, u32[]{:S(2)}, u32[]{:S(2)}) %collective-permute-start.6) | collective-permute-done | bytes 90144 | tf_op jit(solution)/shard_map/ppermute | solution.py:538
  21.8 1.6 %collective-permute-start.7 = (f32[176,128]{1,0:T(8,128)S(1)}, f32[176,128]{1,0:T(8,128)S(1)}, u32[]{:S(2)}, u32[]{:S(2)}) collective-permute-start(f32[176,128]{1,0:T(8,128)S(1)} %add.5.refs_5_.refs_4_), channel_id=1, source_target_pairs={{0,1},{1,0},{2,3},{3,2},{4,5},{5,4},{6,7},{7,6},{8,9},{9,8},{10,11... | collective-permute-start | bytes 270344 | tf_op jit(solution)/shard_map/ppermute | solution.py:538
  23.3 0.5 %collective-permute-done.refs_1_ = f32[4,32,256]{2,1,0:T(8,128)S(1)} collective-permute-done((f32[4,32,256]{2,1,0:T(8,128)S(1)}, f32[4,32,256]{2,1,0:T(8,128)S(1)}, u32[]{:S(2)}, u32[]{:S(2)}) %collective-permute-start) | collective-permute-done | bytes 131104 | tf_op jit(solution)/shard_map/ppermute | solution.py:538
  23.9 1.8 %nuclear.1.refs_2_ = f32[4,32,256]{2,1,0:T(8,128)S(1)} custom-call(f32[4,32,256]{2,1,0:T(8,128)S(1)} %get-tuple-element.15.refs_0_.own, f32[4,32,256]{2,1,0:T(8,128)S(1)} %collective-permute-done.refs_1_), custom_call_target="tpu_custom_call" | custom-call | tf_op jit(solution)/shard_map/nuclear/pallas_call | solution.py:547
  25.7 0.4 %first.1.refs_1_ = f32[4,128,128]{2,1,0:T(8,128)S(1)} custom-call(f32[4,32,256]{2,1,0:T(8,128)S(1)} %get-tuple-element.15.refs_0_.own, f32[4,32,256]{2,1,0:T(8,128)S(1)} %copy-done.1, f32[4,32,256]{2,1,0:T(8,128)S(1)} %nuclear.1.refs_2_, f32[112,1152]{1,0:T(8,128)S(1)} %get-tuple-element.17.refs_3_.refs_2_, ...), custom_call_target="tpu_custom_call" | custom-call | tf_op jit(solution)/shard_map/first/pallas_call | solution.py:547
  26.1 0.2 collective-permute-done.7.refs_5_
  26.4 1.2 %second.1 = f32[4,32,256]{2,1,0:T(8,128)} custom-call(f32[4,32,256]{2,1,0:T(8,128)S(1)} %get-tuple-element.15.refs_0_.own, f32[4,128,128]{2,1,0:T(8,128)S(1)} %first.1.refs_1_, f32[112,1152]{1,0:T(8,128)S(1)} %get-tuple-element.17.refs_3_.refs_2_, f32[32,1152]{1,0:T(8,128)S(1)} %get-tuple-element.20.refs_4_.refs_3_, f32[176,128]{1,0:T(8,128)S(1)} %add.5.refs_5_.refs_4_, ...), custom_call_target="tpu_custom_call" | custom-call | tf_op jit(solution)/shard_map/second/pallas_call | solution.py:547
  (6 shorter events, 0.0 us)
Async XLA Ops:
  0.0 1.8 %collective-permute-start.1 = (f32[4,32,256]{2,1,0:T(8,128)}, f32[4,32,256]{2,1,0:T(8,128)S(1)}, u32[]{:S(2)}, u32[]{:S(2)}) collective-permute-start(f32[4,32,256]{2,1,0:T(8,128)} %dirty.1), channel_id=1, source_target_pairs={{0,8},{8,0},{1,9},{9,1},{2,10},{10,2},{3,11},{11,3},{4,12},{12,4},... | collective-permute-start | bytes 393224 | tf_op jit(solution)/shard_map/ppermute | solution.py:538
  0.5 0.9 %copy-start = (f32[4,32,256]{2,1,0:T(8,128)S(1)}, f32[4,32,256]{2,1,0:T(8,128)}, u32[]{:S(2)}) copy-start(f32[4,32,256]{2,1,0:T(8,128)} %dirty.1) | copy-start | bytes 393220
  1.9 5.1 %collective-permute-start.2 = (f32[72,128]{1,0:T(8,128)S(1)}, f32[72,128]{1,0:T(8,128)S(1)}, u32[]{:S(2)}, u32[]{:S(2)}) collective-permute-start(f32[72,128]{1,0:T(8,128)S(1)} %rows.1), channel_id=1, source_target_pairs={{0,16},{16,0},{1,17},{17,1},{2,18},{18,2},{3,19},{19,3},{4,20},{20... | collective-permute-start | bytes 110600 | tf_op jit(solution)/shard_map/ppermute | solution.py:538
  5.5 4.2 %collective-permute-start.3 = (f32[112,128]{1,0:T(8,128)S(1)}, f32[112,128]{1,0:T(8,128)S(1)}, u32[]{:S(2)}, u32[]{:S(2)}) collective-permute-start(f32[112,128]{1,0:T(8,128)S(1)} %get-tuple-element.22), channel_id=1, source_target_pairs={{0,1},{1,0},{2,3},{3,2},{4,5},{5,4},{6,7},{7,6},{8,9},{9,8},{10,11... | collective-permute-start | bytes 172040 | tf_op jit(solution)/shard_map/ppermute | solution.py:538
  7.1 18.6 %copy-start.1 = (f32[4,32,256]{2,1,0:T(8,128)S(1)}, f32[4,32,256]{2,1,0:T(8,128)}, u32[]{:S(2)}) copy-start(f32[4,32,256]{2,1,0:T(8,128)} %refs_1_.1) | copy-start | bytes 393220
  7.6 4.0 %collective-permute-start.4 = (f32[64,128]{1,0:T(8,128)S(1)}, f32[64,128]{1,0:T(8,128)S(1)}, u32[]{:S(2)}, u32[]{:S(2)}) collective-permute-start(f32[64,128]{1,0:T(8,128)S(1)} %get-tuple-element.24), channel_id=1, source_target_pairs={{0,1},{1,0},{2,3},{3,2},{4,5},{5,4},{6,7},{7,6},{8,9},{9,8},{10,11... | collective-permute-start | bytes 98312 | tf_op jit(solution)/shard_map/ppermute | solution.py:538
  11.6 4.6 %collective-permute-start.5 = (f32[176,128]{1,0:T(8,128)S(1)}, f32[176,128]{1,0:T(8,128)S(1)}, u32[]{:S(2)}, u32[]{:S(2)}) collective-permute-start(f32[176,128]{1,0:T(8,128)S(1)} %add.3.one), channel_id=1, source_target_pairs={{0,2},{1,3},{2,0},{3,1},{4,6},{5,7},{6,4},{7,5},{8,10},{9,11},{10,... | collective-permute-start | bytes 270344 | tf_op jit(solution)/shard_map/ppermute | solution.py:538
  16.2 5.5 %collective-permute-start.6 = (f32[176,128]{1,0:T(8,128)S(1)}, f32[176,128]{1,0:T(8,128)S(1)}, u32[]{:S(2)}, u32[]{:S(2)}) collective-permute-start(f32[176,128]{1,0:T(8,128)S(1)} %add.4.one), channel_id=1, source_target_pairs={{0,4},{1,5},{2,6},{3,7},{4,0},{5,1},{6,2},{7,3},{8,12},{9,13},{10,... | collective-permute-start | bytes 270344 | tf_op jit(solution)/shard_map/ppermute | solution.py:538
  18.9 5.0 %collective-permute-start = (f32[4,32,256]{2,1,0:T(8,128)S(1)}, f32[4,32,256]{2,1,0:T(8,128)S(1)}, u32[]{:S(2)}, u32[]{:S(2)}) collective-permute-start(f32[4,32,256]{2,1,0:T(8,128)S(1)} %get-tuple-element.15.refs_0_.own), channel_id=1, source_target_pairs={{0,1},{1,0},{2,3},{3,2},{4,5},{5,4},{6,7},{7,6},{8,9},{9,8},{10,11... | collective-permute-start | bytes 393224 | tf_op jit(solution)/shard_map/ppermute | solution.py:538
  21.8 4.6 %collective-permute-start.7 = (f32[176,128]{1,0:T(8,128)S(1)}, f32[176,128]{1,0:T(8,128)S(1)}, u32[]{:S(2)}, u32[]{:S(2)}) collective-permute-start(f32[176,128]{1,0:T(8,128)S(1)} %add.5.refs_5_.refs_4_), channel_id=1, source_target_pairs={{0,1},{1,0},{2,3},{3,2},{4,5},{5,4},{6,7},{7,6},{8,9},{9,8},{10,11... | collective-permute-start | bytes 270344 | tf_op jit(solution)/shard_map/ppermute | solution.py:538
